TPU v7x, 256 devices: a whole 4x4x8 slice. The times are simulated.
256 devices in a mesh: row: 8 (over z), col: 32 (over y, x, core).
Axes of the slice: x: 4, y: 4, z: 8, core: 2. Of those that a mesh axis runs over, the one named last changes fastest.
Arguments:
- p_vals: float32 [256, 12, 128, 128], P(('row', 'col')), may hold values from -1.5 to 1.5
- p_cols: int32 [256, 12], replicated, may hold values from 0 to 255, as said below
- perm: int32 [256], replicated, may hold values from 0 to 255, as said below
- out_pattern: int32 [8, 32, 24, 2], P('row', 'col'), may hold values from 0 to 255, as said below
- branch_flag: int32 [8, 32], P('row', 'col'), may hold values 0 or 1
Outputs:
- next_blocks: float32 [8, 32, 24, 128, 128], P('row', 'col')
Inputs may be any that keep to these rules, and one draw needn't show every extreme that they name: `p_cols`: the 12 block columns of each stored row are distinct. `perm`: A permutation. The row stored at position r * 32 + c (grid row r, grid column c) has an index whose quotient by 8 is c. `out_pattern`: in tile (r, c) each first index is the row stored at position r * 32 + ((c + d) mod 32) for some d with -3 <= d <= 3, and every tile has entries with d = -3 and with d = 3; each second index is a row stored in grid column c; the 24 pairs of a tile are distinct.
All inputs are finite; a program needn't handle non-finite values. No bound on the sum of `branch_flag` on one device may be relied on, other than what follows from the above.
Results may differ from a plain program's by a relative error of at most 0.0003.
Values sent between devices are 32-bit elements; how exact they have to be, the bound alone decides.
No kernel may reach another device: no remote copies, remote signals or barrier semaphores. Data moves between devices by JAX's collectives and lax.ppermute only.
A program may use at most 64 MiB of HBM per device.

v0:
```python
import jax
import jax.numpy as jnp
from jax import lax
from jax.sharding import PartitionSpec as P

WG = 3


def from_behind(block, axis, distance):
    devices = range(lax.axis_size(axis))
    route = [((i - distance) % len(devices), i) for i in devices]
    return lax.ppermute(block, axis, route)


def lookup_rows(positions, perm, p_cols):
    row_total = perm.shape[0]
    onehot = (positions[:, None] == jnp.arange(row_total, dtype=jnp.int32)[None, :]).astype(
        jnp.int32
    )
    row_ids = jnp.sum(onehot * perm[None, :], axis=1)
    row_cols = jnp.dot(onehot, p_cols, preferred_element_type=jnp.int32)
    return (row_ids, row_cols)


def locate(targets, row_ids):
    found = (targets[:, None] == row_ids[None, :]).astype(jnp.int32)
    return jnp.sum(found * jnp.arange(row_ids.shape[0], dtype=jnp.int32)[None, :], axis=1)


def select_rows(wanted, small_table):
    onehot = (wanted[:, None] == jnp.arange(small_table.shape[0], dtype=jnp.int32)[None, :]).astype(
        jnp.int32
    )
    return jnp.dot(onehot, small_table, preferred_element_type=jnp.int32)


def shards(p_vals, p_cols, perm, out_pattern, branch_flag):
    row_index = lax.axis_index("row")
    col_index = lax.axis_index("col")
    grid_rows = lax.axis_size("row")
    grid_cols = lax.axis_size("col")
    pieces = []
    for offset in range(-WG, WG + 1):
        if offset == 0:
            pieces.append(p_vals)
        else:
            pieces.append(from_behind(p_vals, "col", -offset))
    row_panel = jnp.concatenate(pieces, axis=0)
    row_pos = row_index * grid_cols + jnp.mod(
        col_index + jnp.arange(-WG, WG + 1, dtype=jnp.int32), grid_cols
    )
    col_panel = lax.all_gather(p_vals, "row", axis=0, tiled=True)
    col_pos = jnp.arange(grid_rows, dtype=jnp.int32) * grid_cols + col_index
    row_ids, row_cols = lookup_rows(row_pos, perm, p_cols)
    col_ids, col_cols = lookup_rows(col_pos, perm, p_cols)
    out_pairs = out_pattern[0, 0]
    out_rows = out_pairs[:, 0]
    out_cols = out_pairs[:, 1]
    left_slot = locate(out_rows, row_ids)
    right_slot = locate(out_cols, col_ids)
    left_cols = select_rows(left_slot, row_cols)
    right_cols = select_rows(right_slot, col_cols)
    matches = left_cols[:, :, None] == right_cols[:, None, :]
    slot_iota = jnp.arange(right_cols.shape[1], dtype=jnp.int32)
    partner = jnp.sum(matches.astype(jnp.int32) * slot_iota[None, None, :], axis=2)
    present = jnp.any(matches, axis=2)
    own_hit = left_cols == out_cols[:, None]
    doubled = branch_flag[0, 0] == 1

    def one_block(block_items):
        left_at, right_at, partner_slots, present_slots, hit_slots = block_items
        left_blocks = row_panel[left_at]
        right_blocks = col_panel[right_at][partner_slots] * present_slots[:, None, None].astype(
            jnp.float32
        )
        square = jnp.einsum(
            "sxk,syk->xy",
            left_blocks,
            right_blocks,
            precision=lax.Precision.HIGHEST,
            preferred_element_type=jnp.float32,
        )
        own_block = jnp.sum(left_blocks * hit_slots[:, None, None].astype(jnp.float32), axis=0)
        return jnp.where(doubled, 2.0 * own_block - square, square)

    blocks = lax.map(one_block, (left_slot, right_slot, partner, present, own_hit))
    return blocks.reshape((1, 1) + blocks.shape)


def solution(mesh):
    return jax.shard_map(
        shards,
        mesh=mesh,
        in_specs=(
            P(("row", "col"), None, None, None),
            P(),
            P(),
            P("row", "col", None, None),
            P("row", "col"),
        ),
        out_specs=P("row", "col", None, None, None),
        check_vma=False,
    )
```

profile of v0, /device:TPU:1, one launch (start us, length us, event | category | flops | bytes accessed | tf_op | source)
XLA Modules:
  0.0 353.7 jit_solution(16794347714410379711)
XLA Ops:
  7.3 4.2 %collective-permute-start = (f32[1,12,128,128]{3,2,1,0:T(8,128)}, f32[1,12,128,128]{3,2,1,0:T(8,128)}, u32[]{:S(2)}, u32[]{:S(2)}) collective-permute-start(f32[1,12,128,128]{3,2,1,0:T(8,128)} %param.7), channel_id=1, source_target_pairs={{29,0},{30,1},{31,2},{0,3},{1,4},{2,5},{3,6},{4,7},{5,8},{6,9},{7,... | collective-permute-start | bytes 2359304 | tf_op jit(solution)/shard_map/ppermute | solution.py:12
  12.3 4.5 %collective-permute-start.4 = (f32[1,12,128,128]{3,2,1,0:T(8,128)}, f32[1,12,128,128]{3,2,1,0:T(8,128)S(1)}, u32[]{:S(2)}, u32[]{:S(2)}) collective-permute-start(f32[1,12,128,128]{3,2,1,0:T(8,128)} %param.7), channel_id=1, source_target_pairs={{2,0},{3,1},{4,2},{5,3},{6,4},{7,5},{8,6},{9,7},{10,8},{11,9},{12,... | collective-permute-start | bytes 2359304 | tf_op jit(solution)/shard_map/ppermute | solution.py:12
  21.3 17.2 %collective-permute-done = f32[1,12,128,128]{3,2,1,0:T(8,128)} collective-permute-done((f32[1,12,128,128]{3,2,1,0:T(8,128)}, f32[1,12,128,128]{3,2,1,0:T(8,128)}, u32[]{:S(2)}, u32[]{:S(2)}) %collective-permute-start) | collective-permute-done | bytes 786464 | tf_op jit(solution)/shard_map/ppermute | solution.py:12
  38.5 2.1 constant_dynamic-update-slice_fusion.6
  40.6 5.4 %collective-permute-done.1 = f32[1,12,128,128]{3,2,1,0:T(8,128)} collective-permute-done((f32[1,12,128,128]{3,2,1,0:T(8,128)}, f32[1,12,128,128]{3,2,1,0:T(8,128)}, u32[]{:S(2)}, u32[]{:S(2)}) %collective-permute-start.1) | collective-permute-done | bytes 786464 | tf_op jit(solution)/shard_map/ppermute | solution.py:12
  46.0 2.1 constant_dynamic-update-slice_fusion.5
  48.0 14.1 %collective-permute-done.2 = f32[1,12,128,128]{3,2,1,0:T(8,128)S(1)} collective-permute-done((f32[1,12,128,128]{3,2,1,0:T(8,128)}, f32[1,12,128,128]{3,2,1,0:T(8,128)S(1)}, u32[]{:S(2)}, u32[]{:S(2)}) %collective-permute-start.2) | collective-permute-done | bytes 786464 | tf_op jit(solution)/shard_map/ppermute | solution.py:12
  67.1 20.4 %all-gather.2.cloned.1.call-done = f32[8,12,128,128]{3,2,1,0:T(8,128)} async-done(((f32[1,12,128,128]{3,2,1,0:T(8,128)}), f32[8,12,128,128]{3,2,1,0:T(8,128)}) %all-gather.2.cloned.1.call-update) | async-done | bytes 6291472 | tf_op jit(solution)/shard_map/all_gather | solution.py:52
  87.5 259.4 %while.10 = (s32[]{:T(128)}, f32[24,128,128]{2,1,0:T(8,128)}, pred[]{:T(512)}, s32[24]{0:T(128)S(1)}, f32[7,12,128,128]{3,2,1,0:T(8,128)}, /*index=5*/pred[24,12...) while((s32[]{:T(128)}, f32[24,128,128]{2,1,0:T(8,128)}, ...), condition=%wide.region_8.9_spmd, body=%wide.region_6.8_spmd.sunk | while | flops 302613568 | bytes 5707405 | solution.py:86
  90.0 1.3 fusion.51
  95.6 2.6 fusion.52
  100.8 1.3 fusion.51
  106.4 2.6 fusion.52
  111.6 1.3 fusion.51
  117.2 2.6 fusion.52
  122.4 1.3 fusion.51
  128.0 2.6 fusion.52
  133.2 1.3 fusion.51
  138.9 2.6 fusion.52
  144.0 1.3 fusion.51
  149.7 2.6 fusion.52
  154.8 1.3 fusion.51
  160.5 2.6 fusion.52
  171.3 2.6 fusion.52
  182.1 2.6 fusion.52
  187.3 1.3 fusion.51
  192.9 2.6 fusion.52
  203.7 2.6 fusion.52
  214.5 2.6 fusion.52
  219.7 1.3 fusion.51
  225.3 2.6 fusion.52
  230.5 1.3 fusion.51
  236.1 2.6 fusion.52
  241.3 1.3 fusion.51
  246.9 2.6 fusion.52
  252.1 1.3 fusion.51
  257.7 2.6 fusion.52
  262.9 1.3 fusion.51
  268.5 2.6 fusion.52
  279.3 2.6 fusion.52
  284.5 1.3 fusion.51
  290.1 2.6 fusion.52
  295.3 1.3 fusion.51
  300.9 2.6 fusion.52
  311.8 2.6 fusion.52
  322.6 2.6 fusion.52
  333.4 2.6 fusion.52
  344.2 2.6 fusion.52
  (210 shorter events, 96.5 us)
Async XLA Ops:
  6.5 12.0 %copy-start = (s32[256,12]{0,1:T(8,128)S(1)}, s32[256,12]{0,1:T(8,128)}, u32[]{:S(2)}) copy-start(s32[256,12]{0,1:T(8,128)} %param.8) | copy-start | bytes 36868
  6.5 56.6 %copy-start.1 = (f32[1,12,128,128]{3,2,1,0:T(8,128)S(1)}, f32[1,12,128,128]{3,2,1,0:T(8,128)}, u32[]{:S(2)}) copy-start(f32[1,12,128,128]{3,2,1,0:T(8,128)} %param.7) | copy-start | bytes 2359300
  6.5 80.9 %all-gather.2.cloned.1.call-start = ((), (), s32[]{:S(2)}) async-start(), calls=%async_computation | async-start | bytes 7077888 | tf_op jit(solution)/shard_map/all_gather | solution.py:52
  7.3 31.3 %collective-permute-start = (f32[1,12,128,128]{3,2,1,0:T(8,128)}, f32[1,12,128,128]{3,2,1,0:T(8,128)}, u32[]{:S(2)}, u32[]{:S(2)}) collective-permute-start(f32[1,12,128,128]{3,2,1,0:T(8,128)} %param.7), channel_id=1, source_target_pairs={{29,0},{30,1},{31,2},{0,3},{1,4},{2,5},{3,6},{4,7},{5,8},{6,9},{7,... | collective-permute-start | bytes 2359304 | tf_op jit(solution)/shard_map/ppermute | solution.py:12
  11.5 34.5 %collective-permute-start.1 = (f32[1,12,128,128]{3,2,1,0:T(8,128)}, f32[1,12,128,128]{3,2,1,0:T(8,128)}, u32[]{:S(2)}, u32[]{:S(2)}) collective-permute-start(f32[1,12,128,128]{3,2,1,0:T(8,128)} %param.7), channel_id=1, source_target_pairs={{30,0},{31,1},{0,2},{1,3},{2,4},{3,5},{4,6},{5,7},{6,8},{7,9},{8,1... | collective-permute-start | bytes 2359304 | tf_op jit(solution)/shard_map/ppermute | solution.py:12
  11.8 50.4 %collective-permute-start.2 = (f32[1,12,128,128]{3,2,1,0:T(8,128)}, f32[1,12,128,128]{3,2,1,0:T(8,128)S(1)}, u32[]{:S(2)}, u32[]{:S(2)}) collective-permute-start(f32[1,12,128,128]{3,2,1,0:T(8,128)} %param.7), channel_id=1, source_target_pairs={{31,0},{0,1},{1,2},{2,3},{3,4},{4,5},{5,6},{6,7},{7,8},{8,9},{9,10... | collective-permute-start | bytes 2359304 | tf_op jit(solution)/shard_map/ppermute | solution.py:12
  12.1 52.1 %collective-permute-start.3 = (f32[1,12,128,128]{3,2,1,0:T(8,128)}, f32[1,12,128,128]{3,2,1,0:T(8,128)S(1)}, u32[]{:S(2)}, u32[]{:S(2)}) collective-permute-start(f32[1,12,128,128]{3,2,1,0:T(8,128)} %param.7), channel_id=1, source_target_pairs={{1,0},{2,1},{3,2},{4,3},{5,4},{6,5},{7,6},{8,7},{9,8},{10,9},{11,1... | collective-permute-start | bytes 2359304 | tf_op jit(solution)/shard_map/ppermute | solution.py:12
  12.3 52.8 %collective-permute-start.4 = (f32[1,12,128,128]{3,2,1,0:T(8,128)}, f32[1,12,128,128]{3,2,1,0:T(8,128)S(1)}, u32[]{:S(2)}, u32[]{:S(2)}) collective-permute-start(f32[1,12,128,128]{3,2,1,0:T(8,128)} %param.7), channel_id=1, source_target_pairs={{2,0},{3,1},{4,2},{5,3},{6,4},{7,5},{8,6},{9,7},{10,8},{11,9},{12,... | collective-permute-start | bytes 2359304 | tf_op jit(solution)/shard_map/ppermute | solution.py:12
  38.5 27.6 %collective-permute-start.5 = (f32[1,12,128,128]{3,2,1,0:T(8,128)}, f32[1,12,128,128]{3,2,1,0:T(8,128)S(1)}, u32[]{:S(2)}, u32[]{:S(2)}) collective-permute-start(f32[1,12,128,128]{3,2,1,0:T(8,128)} %param.7), channel_id=1, source_target_pairs={{3,0},{4,1},{5,2},{6,3},{7,4},{8,5},{9,6},{10,7},{11,8},{12,9},{13... | collective-permute-start | bytes 2359304 | tf_op jit(solution)/shard_map/ppermute | solution.py:12
Sparse Core Ops, SparseCore 0:
  9.2 78.2 all-gather.1
where the time goes:
time: 358 us; the launch traced here: 354 us
  loops' own time  90.7 us (25%)
  local copies, waits for them, and re-layouts  84.1 us (23%)
  matrix products  64.3 us (18%)
  waiting for transfers between devices  57.9 us (16%)
  other arithmetic  33.1 us (9%)
  between operations  14.1 us (4%)
  starting transfers between devices  9.51 us (3%)
    another operation x1, loops' own time, shards(): lax.map(one_block, (left_slot, right_slot, partner, present, own_hit))  90.7 us
    dot_general x24, matrix products, one_block(): jnp.einsum('sxk,syk->xy', left_blocks, right_blocks, precision=lax.Precis...  63.5 us
    ppermute x6, waiting for transfers between devices, from_behind(): return lax.ppermute(block, axis, route)  36.7 us
    dynamic_slice x48, local copies, waits for them, and re-layouts, shards(): lax.map(one_block, (left_slot, right_slot, partner, present, own_hit))  31.2 us
    reduce_sum x24, other arithmetic, one_block(): jnp.sum(left_blocks * hit_slots[:, None, None].astype(jnp.float32), axis=0)  30.3 us
    squeeze x24, local copies, waits for them, and re-layouts, one_block(): col_panel[right_at][partner_slots]  28.5 us
    all_gather x1, waiting for transfers between devices, shards(): col_panel = lax.all_gather(p_vals, 'row', axis=0, tiled=True)  20.4 us
    gather x24, local copies, waits for them, and re-layouts, one_block(): col_panel[right_at][partner_slots]  14.4 us
  transfers between devices with their start and end apart: 7, of which 4 were waited for; matrix products, arithmetic and copies ran while one was open for 4% of the time, Pallas kernels for 0%

commit v1 on v0

v1 whole, which is shorter than its diff:
```python
import functools

import jax
import jax.numpy as jnp
from jax import lax
from jax.experimental import pallas as pl
from jax.experimental.pallas import tpu as pltpu
from jax.sharding import PartitionSpec as P

BS = 128
NNZ = 12
OT = 24
HALF = NNZ // 2
UNROLL = 4
LIST = 320
Z_STEPS = (0, -1, 1, -2, 2, -3, 3, 4)
X_EVEN = (0, 1, 2, -2, 3, -1, -3)
X_ODD = (0, -1, 2, -2, 1, -3, 3)
GROUPS = ((0, 1, 2, 3, 4), (5, 6), (7,))
NT = (((1,), (1,)), ((), ()))
DUMMY = OT << 16
TLIST = LIST
POFF = TLIST + 32
TOFF = POFF + 8
FLAG = TOFF + 8
META = 384


def send(block, axis, distance):
    n = lax.axis_size(axis)
    return lax.ppermute(block, axis, [(i, (i + distance) % n) for i in range(n)])


def swap_cores(block):
    n = lax.axis_size("col")
    return lax.ppermute(block, "col", [(i, i ^ 1) for i in range(n)])


def pick(onehot, table):
    return jnp.dot(onehot.astype(jnp.int32), table, preferred_element_type=jnp.int32)


def work_list(row_index, col_index, perm, p_cols, out_pairs, flag):
    n_rows, n_cols = lax.axis_size("row"), lax.axis_size("col")
    even = (col_index % 2) == 0
    steps = jnp.where(even, jnp.array(X_EVEN, jnp.int32), jnp.array(X_ODD, jnp.int32))
    left_pos = row_index * n_cols + jnp.mod(col_index + steps, n_cols)
    right_pos = jnp.mod(row_index + jnp.array(Z_STEPS, jnp.int32), n_rows) * n_cols + col_index
    pos = jnp.concatenate([left_pos, right_pos])
    onehot = pos[:, None] == jnp.arange(perm.shape[0], dtype=jnp.int32)[None, :]
    ids = jnp.sum(jnp.where(onehot, perm[None, :], 0), axis=1)
    cols = pick(onehot, p_cols)
    nl = len(X_EVEN)
    left_hot = out_pairs[:, 0:1] == ids[None, :nl]
    right_hot = out_pairs[:, 1:2] == ids[None, nl:]
    left_cols = pick(left_hot, cols[:nl])
    right_cols = pick(right_hot, cols[nl:])
    left_at = jnp.sum(jnp.where(left_hot, jnp.arange(nl, dtype=jnp.int32)[None, :], 0), axis=1)
    right_at = jnp.sum(
        jnp.where(right_hot, jnp.arange(len(Z_STEPS), dtype=jnp.int32)[None, :], 0), axis=1
    )
    group_of = [g for row in range(len(Z_STEPS)) for g, rows in enumerate(GROUPS) if row in rows]
    group = jnp.sum(jnp.where(right_hot, jnp.array(group_of, jnp.int32)[None, :], 0), axis=1)
    slots = jnp.arange(NNZ, dtype=jnp.int32)
    match = left_cols[:, :, None] == right_cols[:, None, :]
    present = jnp.any(match, axis=2)
    partner = jnp.sum(jnp.where(match, slots[None, None, :], 0), axis=2)
    tiles = jnp.arange(OT, dtype=jnp.int32)
    payload = (
        (tiles[:, None] << 16)
        + ((left_at[:, None] * NNZ + slots[None, :]) << 8)
        + right_at[:, None] * NNZ
        + partner
    )
    count = jnp.sum(present.astype(jnp.int32), axis=1)
    earlier = (group[:, None] == group[None, :]) & (tiles[None, :] < tiles[:, None])
    row_start = jnp.sum(jnp.where(earlier, count[None, :], 0), axis=1)
    gs = jnp.arange(8, dtype=jnp.int32)
    in_group = group[None, :] == gs[:, None]
    steps_of = (jnp.sum(jnp.where(in_group, count[None, :], 0), axis=1) + UNROLL - 1) // UNROLL
    before = gs[None, :] < gs[:, None]
    step_start = jnp.sum(jnp.where(before, steps_of[None, :], 0), axis=1)
    tile_start = jnp.sum((group[None, :] < gs[:, None]).astype(jnp.int32), axis=1)
    ahead = jnp.sum(
        (present[:, None, :] & (slots[None, None, :] < slots[None, :, None])).astype(jnp.int32),
        axis=2,
    )
    group_start = jnp.sum(jnp.where(in_group, step_start[:, None], 0), axis=0) * UNROLL
    rank = jnp.where(present, group_start[:, None] + row_start[:, None] + ahead, -1)
    places = jnp.arange(LIST, dtype=jnp.int32)
    pairs = DUMMY + jnp.sum(
        jnp.where(rank[:, :, None] == places[None, None, :], payload[:, :, None] - DUMMY, 0),
        axis=(0, 1),
    )
    own_hit = left_cols == out_pairs[:, 1:2]
    own = jnp.sum(
        jnp.where(own_hit, left_at[:, None] * NNZ + slots[None, :] + 1, 0), axis=1
    )
    tile_rank = jnp.sum(
        ((group[None, :] < group[:, None]) | earlier).astype(jnp.int32), axis=1
    )
    tile_list = jnp.sum(
        jnp.where(
            tile_rank[:, None] == jnp.arange(32, dtype=jnp.int32)[None, :],
            ((tiles << 8) + own)[:, None],
            0,
        ),
        axis=0,
    )
    tail = jnp.full((META - FLAG,), flag, jnp.int32)
    return jnp.concatenate([pairs, tile_list, step_start, tile_start, tail])


def split(block):
    high = block.astype(jnp.bfloat16)
    return high, (block - high.astype(jnp.float32)).astype(jnp.bfloat16)


def product(left, right):
    lh, ll = split(left)
    rh, rl = split(right)
    a = jnp.concatenate([lh, ll], axis=1)
    b = jnp.concatenate(
        [jnp.concatenate([rh, rh], axis=1), jnp.concatenate([rl, rl], axis=1)], axis=0
    )
    both = lax.dot_general(a, b, NT, preferred_element_type=jnp.float32)
    return both[:, :BS] + both[:, BS:]


def kernel(group, n_left, sizes, first, meta, *refs):
    left = refs[:n_left]
    right = refs[n_left : n_left + len(sizes)]
    out, left_panel, right_panel, acc, in_sems, out_sems = refs[-6:]
    copies = []
    for i, ref in enumerate(left):
        copies.append((ref.at[0], left_panel.at[pl.ds(i * NNZ, NNZ)]))
    at = 0
    for ref, size in zip(right, sizes):
        copies.append((ref.at[0], right_panel.at[pl.ds(at, size)]))
        at += size
    copies = [
        pltpu.make_async_copy(src, dst, in_sems.at[i]) for i, (src, dst) in enumerate(copies)
    ]
    for copy in copies:
        copy.start()
    t0, t1 = meta[TOFF + group], meta[TOFF + group + 1]
    p0, p1 = meta[POFF + group], meta[POFF + group + 1]
    doubled = meta[FLAG] == 1

    def clear(i, _):
        acc[meta[TLIST + i] >> 8] = jnp.zeros((BS, BS), jnp.float32)
        return 0

    lax.fori_loop(t0, t1, clear, 0)
    for copy in copies:
        copy.wait()

    def pairs(step, _):
        for k in range(UNROLL):
            item = meta[step * UNROLL + k]
            tile = item >> 16
            l_at = (item >> 8) & 255
            r_at = jnp.maximum((item & 255) - first, 0)
            acc[tile] = acc[tile] + product(left_panel[l_at], right_panel[r_at])
        return 0

    lax.fori_loop(p0, p1, pairs, 0)

    def out_copy(tile):
        return pltpu.make_async_copy(acc.at[tile], out.at[tile], out_sems.at[tile])

    def finish(i, _):
        item = meta[TLIST + i]
        tile, own = item >> 8, item & 255

        @pl.when(doubled)
        def _():
            scale = jnp.where(own > 0, 2.0, 0.0)
            acc[tile] = scale * left_panel[jnp.maximum(own - 1, 0)] - acc[tile]

        out_copy(tile).start()
        return 0

    lax.fori_loop(t0, t1, finish, 0)

    def drain(i, _):
        out_copy(meta[TLIST + i] >> 8).wait()
        return 0

    lax.fori_loop(t0, t1, drain, 0)


def run_group(group, meta, left, right, previous):
    sizes = tuple(block.shape[1] for block in right)
    first = GROUPS[group][0] * NNZ
    any_spec = pl.BlockSpec(memory_space=pl.ANY)
    operands = [meta, *left, *right]
    aliases = {}
    if previous is not None:
        aliases = {len(operands): 0}
        operands.append(previous)
    work = OT * len(GROUPS[group]) // len(Z_STEPS) * 4
    return pl.pallas_call(
        functools.partial(kernel, group, len(left), sizes, first),
        out_shape=jax.ShapeDtypeStruct((OT, BS, BS), jnp.float32),
        in_specs=[pl.BlockSpec(memory_space=pltpu.SMEM)] + [any_spec] * (len(operands) - 1),
        out_specs=any_spec,
        scratch_shapes=[
            pltpu.VMEM((len(left) * NNZ, BS, BS), jnp.float32),
            pltpu.VMEM((sum(sizes), BS, BS), jnp.float32),
            pltpu.VMEM((OT + 1, BS, BS), jnp.float32),
            pltpu.SemaphoreType.DMA((len(left) + len(right),)),
            pltpu.SemaphoreType.DMA((OT,)),
        ],
        input_output_aliases=aliases,
        cost_estimate=pl.CostEstimate(
            flops=work * 8 * BS**3, bytes_accessed=10 << 20, transcendentals=0
        ),
        compiler_params=pltpu.CompilerParams(vmem_limit_bytes=24 << 20),
        name=f"pairs_{group}",
    )(*operands)


def shards(p_vals, p_cols, perm, out_pattern, branch_flag):
    row_index = lax.axis_index("row")
    col_index = lax.axis_index("col")
    halves = [p_vals[:, :HALF], p_vals[:, HALF:]]
    up, down = list(halves), list(halves)
    right = {0: [p_vals]}
    for step in range(3):
        up = [send(block, "row", 1) for block in up]
        down = [send(block, "row", -1) for block in down]
        right[2 * step + 1], right[2 * step + 2] = up, down
    right[7] = [send(up[0], "row", 1), send(down[1], "row", -1)]

    n = lax.axis_size("col")
    ahead2 = send(p_vals, "col", -2)
    behind2 = send(p_vals, "col", 2)
    relay = jnp.where((col_index % 2) == 0, ahead2, behind2)
    far = lax.ppermute(
        relay, "col", [((i - 1) % n if i % 2 == 0 else (i + 1) % n, i) for i in range(n)]
    )
    left = [
        p_vals,
        swap_cores(p_vals),
        ahead2,
        behind2,
        swap_cores(ahead2),
        swap_cores(behind2),
        far,
    ]
    meta = work_list(row_index, col_index, perm, p_cols, out_pattern[0, 0], branch_flag[0, 0])
    out = None
    for group, rows in enumerate(GROUPS):
        out = run_group(group, meta, left, [block for row in rows for block in right[row]], out)
    return out.reshape((1, 1) + out.shape)


def solution(mesh):
    return jax.shard_map(
        shards,
        mesh=mesh,
        in_specs=(
            P(("row", "col"), None, None, None),
            P(),
            P(),
            P("row", "col", None, None),
            P("row", "col"),
        ),
        out_specs=P("row", "col", None, None, None),
        check_vma=False,
    )
```

time: 358 us -> 97.6 us (0.27)
  loops' own time: 90.7 us -> 0 us
  local copies, waits for them, and re-layouts: 84.1 us -> 13.2 us
  matrix products: 64.3 us -> 0.61 us
  waiting for transfers between devices: 57.9 us -> 24.2 us
  other arithmetic: 33.1 us -> 3.29 us
  starting transfers between devices: 9.51 us -> 37.4 us
  Pallas kernels: 0 us -> 16.2 us
  between operations: 14.1 us -> 1.04 us
    another operation x1 -> x0, loops' own time: 90.7 us -> none  [shards(): lax.map(one_block, (left_slot, right_slot, partner, present, own_hit))]
    dot_general x26 -> x3, matrix products: 64.3 us -> 0.61 us  [pick(): jnp.dot(onehot.astype(jnp.int32), table, preferred_element_type=jnp.int32)]
    dynamic_slice x48 -> x0, local copies, waits for them, and re-layouts: 31.2 us -> none  [shards(): lax.map(one_block, (left_slot, right_slot, partner, present, own_hit))]
    reduce_sum x29 -> x13, other arithmetic: 32.2 us -> 2.44 us  [the longest x1 0.72 us: work_list(): jnp.sum((group[None, :] < gs[:, None]).astype(jnp.int32), axis=1)]
    squeeze x24 -> x0, local copies, waits for them, and re-layouts: 28.5 us -> none  [one_block(): col_panel[right_at][partner_slots]]
    ppermute x6 -> x20, starting transfers between devices: 9.51 us -> 37.4 us  [the longest x16 24.6 us: send(): lax.ppermute(block, axis, [(i, (i + distance) % n) for i in range(n)])]
    all_gather x1 -> x0, waiting for transfers between devices: 20.4 us -> none  [shards(): col_panel = lax.all_gather(p_vals, 'row', axis=0, tiled=True)]
    pallas_call x0 -> x3, Pallas kernels: none -> 16.2 us  [run_group(): pl.pallas_call(functools.partial(kernel, group, len(left), sizes, first),...]
  transfers between devices with their start and end apart: 7 -> 20, of which waited for: 4 -> 8; matrix products, arithmetic and copies ran while one was open for 4% -> 8% of each run, Pallas kernels for 0% -> 13%
where the time goes in v1:
time: 97.6 us; the launch traced here: 96 us
  starting transfers between devices  37.4 us (38%)
  waiting for transfers between devices  24.2 us (25%)
  Pallas kernels  16.2 us (17%)
  local copies, waits for them, and re-layouts  13.2 us (14%)
  other arithmetic  3.29 us (3%)
  between operations  1.04 us (1%)
    ppermute x16, starting transfers between devices, send(): lax.ppermute(block, axis, [(i, (i + distance) % n) for i in range(n)])  24.6 us
    ppermute x16, waiting for transfers between devices, send(): lax.ppermute(block, axis, [(i, (i + distance) % n) for i in range(n)])  24.2 us
    pallas_call x3, Pallas kernels, run_group(): pl.pallas_call(functools.partial(kernel, group, len(left), sizes, first),...  16.2 us
    ppermute x3, starting transfers between devices, swap_cores(): return lax.ppermute(block, 'col', [(i, i ^ 1) for i in range(n)])  10 us
    unnamed x40, local copies, waits for them, and re-layouts  9.28 us
    ppermute x1, starting transfers between devices, shards(): lax.ppermute(relay, 'col', [((i - 1) % n if i % 2 == 0 else (i + 1) % n,...  2.8 us
  transfers between devices with their start and end apart: 20, of which 8 were waited for; matrix products, arithmetic and copies ran while one was open for 8% of the time, Pallas kernels for 13%

profile of v1, /device:TPU:1, one launch (start us, length us, event | category | flops | bytes accessed | tf_op | source)
XLA Modules:
  0.0 96.0 jit_solution(15428734535033951056)
XLA Ops:
  0.1 5.8 %collective-permute-start.1 = (f32[1,12,128,128]{3,2,1,0:T(8,128)}, f32[1,12,128,128]{3,2,1,0:T(8,128)S(1)}, u32[]{:S(2)}, u32[]{:S(2)}) collective-permute-start(f32[1,12,128,128]{3,2,1,0:T(8,128)} %refs_0_.5), channel_id=1, source_target_pairs={{0,30},{1,31},{2,0},{3,1},{4,2},{5,3},{6,4},{7,5},{8,6},{9,7},{10,... | collective-permute-start | bytes 2359304 | tf_op jit(solution)/shard_map/ppermute | solution.py:31
  5.9 1.9 %fusion.23 = (f32[1,6,128,128]{3,2,1,0:T(8,128)S(1)}, f32[1,6,128,128]{3,2,1,0:T(8,128)}) fusion(f32[1,12,128,128]{3,2,1,0:T(8,128)} %refs_0_.5), kind=kLoop, calls=%fused_computation.72 | loop fusion | bytes 1572864 | tf_op jit(solution)/shard_map/slice | solution.py:227
  7.8 5.6 %collective-permute-start.10 = (f32[1,6,128,128]{3,2,1,0:T(8,128)S(1)}, f32[1,6,128,128]{3,2,1,0:T(8,128)S(1)}, u32[]{:S(2)}, u32[]{:S(2)}) collective-permute-start(f32[1,6,128,128]{3,2,1,0:T(8,128)S(1)} %get-tuple-element.11), channel_id=1, source_target_pairs={{0,224},{32,0},{64,32},{96,64},{128,96},{160,128},{192,160},{224,1... | collective-permute-start | bytes 1179656 | tf_op jit(solution)/shard_map/ppermute | solution.py:31
  13.4 2.7 %collective-permute-start.17 = (f32[1,6,128,128]{3,2,1,0:T(8,128)}, f32[1,6,128,128]{3,2,1,0:T(8,128)}, u32[]{:S(2)}, u32[]{:S(2)}) collective-permute-start(f32[1,6,128,128]{3,2,1,0:T(8,128)} %get-tuple-element.12), channel_id=1, source_target_pairs={{0,224},{32,0},{64,32},{96,64},{128,96},{160,128},{192,160},{224,1... | collective-permute-start | bytes 1179656 | tf_op jit(solution)/shard_map/ppermute | solution.py:31
  16.2 0.2 fusion.1
  16.4 0.2 select_reduce_fusion.1
  16.7 0.2 fusion.4
  16.9 0.2 fusion.6
  17.4 0.1 select_reduce_fusion.7
  17.5 3.3 %collective-permute-done.10.refs_11_ = f32[1,6,128,128]{3,2,1,0:T(8,128)S(1)} collective-permute-done((f32[1,6,128,128]{3,2,1,0:T(8,128)S(1)}, f32[1,6,128,128]{3,2,1,0:T(8,128)S(1)}, u32[]{:S(2)}, u32[]{:S(2)}) %collective-permute-start.10) | collective-permute-done | bytes 393248 | tf_op jit(solution)/shard_map/ppermute | solution.py:31
  20.9 0.1 select_reduce_fusion.6
  21.0 0.2 convert_reduce_fusion.1
  21.2 2.9 %collective-permute-done.14.refs_9_ = f32[1,6,128,128]{3,2,1,0:T(8,128)} collective-permute-done((f32[1,6,128,128]{3,2,1,0:T(8,128)S(1)}, f32[1,6,128,128]{3,2,1,0:T(8,128)}, u32[]{:S(2)}, u32[]{:S(2)}) %collective-permute-start.14) | collective-permute-done | bytes 393248 | tf_op jit(solution)/shard_map/ppermute | solution.py:31
  24.1 2.2 %collective-permute-start = (f32[1,12,128,128]{3,2,1,0:T(8,128)S(1)}, f32[1,12,128,128]{3,2,1,0:T(8,128)S(1)}, u32[]{:S(2)}, u32[]{:S(2)}) collective-permute-start(f32[1,12,128,128]{3,2,1,0:T(8,128)S(1)} %copy-done.1), channel_id=1, source_target_pairs={{0,1},{1,0},{2,3},{3,2},{4,5},{5,4},{6,7},{7,6},{8,9},{9,8},{10,11... | collective-permute-start | bytes 2359304 | tf_op jit(solution)/shard_map/ppermute | solution.py:36
  26.3 0.1 convert_reduce_fusion
  26.4 3.0 %collective-permute-done.17.refs_10_ = f32[1,6,128,128]{3,2,1,0:T(8,128)} collective-permute-done((f32[1,6,128,128]{3,2,1,0:T(8,128)}, f32[1,6,128,128]{3,2,1,0:T(8,128)}, u32[]{:S(2)}, u32[]{:S(2)}) %collective-permute-start.17) | collective-permute-done | bytes 393248 | tf_op jit(solution)/shard_map/ppermute | solution.py:31
  29.4 3.4 %collective-permute-start.11 = (f32[1,6,128,128]{3,2,1,0:T(8,128)S(1)}, f32[1,6,128,128]{3,2,1,0:T(8,128)S(1)}, u32[]{:S(2)}, u32[]{:S(2)}) collective-permute-start(f32[1,6,128,128]{3,2,1,0:T(8,128)S(1)} %collective-permute-done.10.refs_11_), channel_id=1, source_target_pairs={{0,224},{32,0},{64,32},{96,64},{128,96},{160,128},{192,160},{224,1... | collective-permute-start | bytes 1179656 | tf_op jit(solution)/shard_map/ppermute | solution.py:31
  32.8 0.7 convert_reduce_fusion.3
  33.5 2.7 %collective-permute-start.18 = (f32[1,6,128,128]{3,2,1,0:T(8,128)}, f32[1,6,128,128]{3,2,1,0:T(8,128)}, u32[]{:S(2)}, u32[]{:S(2)}) collective-permute-start(f32[1,6,128,128]{3,2,1,0:T(8,128)} %collective-permute-done.17.refs_10_), channel_id=1, source_target_pairs={{0,224},{32,0},{64,32},{96,64},{128,96},{160,128},{192,160},{224,1... | collective-permute-start | bytes 1179656 | tf_op jit(solution)/shard_map/ppermute | solution.py:31
  36.3 3.0 %collective-permute-done.11.refs_15_ = f32[1,6,128,128]{3,2,1,0:T(8,128)S(1)} collective-permute-done((f32[1,6,128,128]{3,2,1,0:T(8,128)S(1)}, f32[1,6,128,128]{3,2,1,0:T(8,128)S(1)}, u32[]{:S(2)}, u32[]{:S(2)}) %collective-permute-start.11) | collective-permute-done | bytes 393248 | tf_op jit(solution)/shard_map/ppermute | solution.py:31
  39.3 2.8 %collective-permute-start.5 = (f32[1,12,128,128]{3,2,1,0:T(8,128)S(1)}, f32[1,12,128,128]{3,2,1,0:T(8,128)S(1)}, u32[]{:S(2)}, u32[]{:S(2)}) collective-permute-start(f32[1,12,128,128]{3,2,1,0:T(8,128)S(1)} %broadcast_select_fusion), channel_id=1, source_target_pairs={{31,0},{2,1},{1,2},{4,3},{3,4},{6,5},{5,6},{8,7},{7,8},{10,9},{9,1... | collective-permute-start | bytes 2359304 | tf_op jit(solution)/shard_map/ppermute | solution.py:240
  42.1 0.6 collective-permute-done.15.refs_13_
  42.8 5.7 %collective-permute-start.3 = (f32[1,12,128,128]{3,2,1,0:T(8,128)S(1)}, f32[1,12,128,128]{3,2,1,0:T(8,128)S(1)}, u32[]{:S(2)}, u32[]{:S(2)}) collective-permute-start(f32[1,12,128,128]{3,2,1,0:T(8,128)S(1)} %collective-permute-done.1.refs_2_), channel_id=1, source_target_pairs={{0,1},{1,0},{2,3},{3,2},{4,5},{5,4},{6,7},{7,6},{8,9},{9,8},{10,11... | collective-permute-start | bytes 2359304 | tf_op jit(solution)/shard_map/ppermute | solution.py:36
  48.5 2.1 %collective-permute-start.4 = (f32[1,12,128,128]{3,2,1,0:T(8,128)S(1)}, f32[1,12,128,128]{3,2,1,0:T(8,128)}, u32[]{:S(2)}, u32[]{:S(2)}) collective-permute-start(f32[1,12,128,128]{3,2,1,0:T(8,128)S(1)} %collective-permute-done.2.refs_3_), channel_id=1, source_target_pairs={{0,1},{1,0},{2,3},{3,2},{4,5},{5,4},{6,7},{7,6},{8,9},{9,8},{10,11... | collective-permute-start | bytes 2359304 | tf_op jit(solution)/shard_map/ppermute | solution.py:36
  50.7 0.5 collective-permute-done.7.refs_12_
  51.1 3.0 %collective-permute-start.12 = (f32[1,6,128,128]{3,2,1,0:T(8,128)S(1)}, f32[1,6,128,128]{3,2,1,0:T(8,128)}, u32[]{:S(2)}, u32[]{:S(2)}) collective-permute-start(f32[1,6,128,128]{3,2,1,0:T(8,128)S(1)} %collective-permute-done.11.refs_15_), channel_id=1, source_target_pairs={{0,224},{32,0},{64,32},{96,64},{128,96},{160,128},{192,160},{224,1... | collective-permute-start | bytes 1179656 | tf_op jit(solution)/shard_map/ppermute | solution.py:31
  54.1 0.8 copy-done.8
  54.8 0.8 copy-done.10
  55.6 0.2 select_reduce_fusion
  55.8 6.8 %collective-permute-done.12.refs_10_ = f32[1,6,128,128]{3,2,1,0:T(8,128)} collective-permute-done((f32[1,6,128,128]{3,2,1,0:T(8,128)S(1)}, f32[1,6,128,128]{3,2,1,0:T(8,128)}, u32[]{:S(2)}, u32[]{:S(2)}) %collective-permute-start.12) | collective-permute-done | bytes 393248 | tf_op jit(solution)/shard_map/ppermute | solution.py:31
  62.6 4.0 %collective-permute-done.8.refs_7_ = f32[1,6,128,128]{3,2,1,0:T(8,128)} collective-permute-done((f32[1,6,128,128]{3,2,1,0:T(8,128)S(1)}, f32[1,6,128,128]{3,2,1,0:T(8,128)}, u32[]{:S(2)}, u32[]{:S(2)}) %collective-permute-start.8) | collective-permute-done | bytes 393248 | tf_op jit(solution)/shard_map/ppermute | solution.py:31
  66.6 0.9 copy-done.2
  67.5 1.0 %collective-permute-start.13 = (f32[1,6,128,128]{3,2,1,0:T(8,128)}, f32[1,6,128,128]{3,2,1,0:T(8,128)}, u32[]{:S(2)}, u32[]{:S(2)}) collective-permute-start(f32[1,6,128,128]{3,2,1,0:T(8,128)} %collective-permute-done.12.refs_10_), channel_id=1, source_target_pairs={{0,224},{32,0},{64,32},{96,64},{128,96},{160,128},{192,160},{224,1... | collective-permute-start | bytes 1179656 | tf_op jit(solution)/shard_map/ppermute | solution.py:31
  68.5 0.9 copy-done.4
  69.4 0.4 collective-permute-start.9
  69.9 0.6 select_reduce_fusion.2
  71.1 0.6 broadcast_add_fusion
  71.7 0.6 broadcast_in_dim.200
  72.3 1.4 %concatenate.7.meta = s32[384]{0:T(512)} concatenate(s32[320]{0:T(512)} %broadcast_add_fusion, s32[32]{0:T(128)} %select_reduce_fusion.2, s32[8]{0:T(128)} %copy-done.13, s32[8]{0:T(128)} %get-tuple-element.7, s32[16]{0:T(128)} %broadcast_in_dim.200), dimensions={0} | concatenate | bytes 3072 | tf_op jit(solution)/shard_map/concatenate | solution.py:111
  73.6 1.1 %copy-done.3 = f32[1,12,128,128]{3,2,1,0:T(8,128)S(1)} copy-done((f32[1,12,128,128]{3,2,1,0:T(8,128)S(1)}, f32[1,12,128,128]{3,2,1,0:T(8,128)}, u32[]{:S(2)}) %copy-start.3) | copy-done | bytes 786456
  74.8 1.1 %copy-done.5 = f32[1,12,128,128]{3,2,1,0:T(8,128)S(1)} copy-done((f32[1,12,128,128]{3,2,1,0:T(8,128)S(1)}, f32[1,12,128,128]{3,2,1,0:T(8,128)}, u32[]{:S(2)}) %copy-start.5) | copy-done | bytes 786456
  75.9 1.0 %copy-done.7 = f32[1,6,128,128]{3,2,1,0:T(8,128)S(1)} copy-done((f32[1,6,128,128]{3,2,1,0:T(8,128)S(1)}, f32[1,6,128,128]{3,2,1,0:T(8,128)}, u32[]{:S(2)}) %copy-start.7) | copy-done | bytes 393240
  76.9 1.0 %copy-done.9 = f32[1,6,128,128]{3,2,1,0:T(8,128)S(1)} copy-done((f32[1,6,128,128]{3,2,1,0:T(8,128)S(1)}, f32[1,6,128,128]{3,2,1,0:T(8,128)}, u32[]{:S(2)}) %copy-start.9) | copy-done | bytes 393240
  77.9 1.0 %copy-done.11 = f32[1,6,128,128]{3,2,1,0:T(8,128)S(1)} copy-done((f32[1,6,128,128]{3,2,1,0:T(8,128)S(1)}, f32[1,6,128,128]{3,2,1,0:T(8,128)}, u32[]{:S(2)}) %copy-start.11) | copy-done | bytes 393240
  78.9 0.7 copy-done.12
  79.6 7.2 %pairs_0.1.refs_11_ = f32[24,128,128]{2,1,0:T(8,128)} custom-call(s32[384]{0:T(512)S(1)} %copy-done.12, f32[1,12,128,128]{3,2,1,0:T(8,128)S(1)} %copy-done.1, f32[1,12,128,128]{3,2,1,0:T(8,128)S(1)} %collective-permute-done.refs_1_, f32[1,12,128,128]{3,2,1,0:T(8,128)S(1)} %collective-permute-done.1.refs_2_, ...), custom_call_target="tpu_custom_call" | custom-call | flops 1006632960 | bytes 10485760 | tf_op jit(solution)/shard_map/pairs_0/pallas_call | solution.py:203
  86.8 5.1 %pairs_1.1.refs_9_ = f32[24,128,128]{2,1,0:T(8,128)} custom-call(s32[384]{0:T(512)S(1)} %copy-done.12, f32[1,12,128,128]{3,2,1,0:T(8,128)S(1)} %copy-done.1, f32[1,12,128,128]{3,2,1,0:T(8,128)S(1)} %collective-permute-done.refs_1_, f32[1,12,128,128]{3,2,1,0:T(8,128)S(1)} %collective-permute-done.1.refs_2_, ...), custom_call_target="tpu_custom_call", output_to_operand_aliasing={{}: (12, {})} | custom-call | flops 402653184 | bytes 10485760 | tf_op jit(solution)/shard_map/pairs_1/pallas_call | solution.py:203
  92.0 3.8 %pairs_2.1 = f32[24,128,128]{2,1,0:T(8,128)} custom-call(s32[384]{0:T(512)S(1)} %copy-done.12, f32[1,12,128,128]{3,2,1,0:T(8,128)S(1)} %copy-done.1, f32[1,12,128,128]{3,2,1,0:T(8,128)S(1)} %collective-permute-done.refs_1_, f32[1,12,128,128]{3,2,1,0:T(8,128)S(1)} %collective-permute-done.1.refs_2_, ...), custom_call_target="tpu_custom_call", output_to_operand_aliasing={{}: (10, {})} | custom-call | flops 201326592 | bytes 10485760 | tf_op jit(solution)/shard_map/pairs_2/pallas_call | solution.py:203
  (69 shorter events, 0.7 us)
Async XLA Ops:
  0.0 16.2 %copy-start = (s32[256,12]{0,1:T(8,128)S(1)}, s32[256,12]{0,1:T(8,128)}, u32[]{:S(2)}) copy-start(s32[256,12]{0,1:T(8,128)} %param.10) | copy-start | bytes 36868
  0.0 16.1 %copy-start.19 = (s32[8]{0:T(128)S(1)}, s32[8]{0:T(128)}, u32[]{:S(2)}) copy-start(s32[8]{0:T(128)} %constant.98.clone) | copy-start | bytes 100
  0.0 16.1 %copy-start.17 = (s32[7]{0:T(128)S(1)}, s32[7]{0:T(128)}, u32[]{:S(2)}) copy-start(s32[7]{0:T(128)} %constant.96.clone) | copy-start | bytes 88
  0.0 16.1 %copy-start.18 = (s32[7]{0:T(128)S(1)}, s32[7]{0:T(128)}, u32[]{:S(2)}) copy-start(s32[7]{0:T(128)} %constant.97.clone) | copy-start | bytes 88
  0.0 17.3 %copy-start.16 = (s32[8]{0:T(128)S(1)}, s32[8]{0:T(128)}, u32[]{:S(2)}) copy-start(s32[8]{0:T(128)} %constant.99.clone) | copy-start | bytes 100
  0.0 24.0 %copy-start.1 = (f32[1,12,128,128]{3,2,1,0:T(8,128)S(1)}, f32[1,12,128,128]{3,2,1,0:T(8,128)}, u32[]{:S(2)}) copy-start(f32[1,12,128,128]{3,2,1,0:T(8,128)} %refs_0_.5) | copy-start | bytes 2359300
  0.0 16.4 %copy-start.14 = (s32[256]{0:T(256)S(1)}, s32[256]{0:T(256)}, u32[]{:S(2)}) copy-start(s32[256]{0:T(256)} %param.11) | copy-start | bytes 3076
  0.1 16.6 %copy-start.15 = (s32[1,1,24,2]{2,3,1,0:T(2,128)S(1)}, s32[1,1,24,2]{2,3,1,0:T(2,128)}, u32[]{:S(2)}) copy-start(s32[1,1,24,2]{2,3,1,0:T(2,128)} %param.12) | copy-start | bytes 580
  0.1 33.5 %collective-permute-start.1 = (f32[1,12,128,128]{3,2,1,0:T(8,128)}, f32[1,12,128,128]{3,2,1,0:T(8,128)S(1)}, u32[]{:S(2)}, u32[]{:S(2)}) collective-permute-start(f32[1,12,128,128]{3,2,1,0:T(8,128)} %refs_0_.5), channel_id=1, source_target_pairs={{0,30},{1,31},{2,0},{3,1},{4,2},{5,3},{6,4},{7,5},{8,6},{9,7},{10,... | collective-permute-start | bytes 2359304 | tf_op jit(solution)/shard_map/ppermute | solution.py:31
  5.9 30.3 %collective-permute-start.2 = (f32[1,12,128,128]{3,2,1,0:T(8,128)}, f32[1,12,128,128]{3,2,1,0:T(8,128)S(1)}, u32[]{:S(2)}, u32[]{:S(2)}) collective-permute-start(f32[1,12,128,128]{3,2,1,0:T(8,128)} %refs_0_.5), channel_id=1, source_target_pairs={{0,2},{1,3},{2,4},{3,5},{4,6},{5,7},{6,8},{7,9},{8,10},{9,11},{10,... | collective-permute-start | bytes 2359304 | tf_op jit(solution)/shard_map/ppermute | solution.py:31
  7.8 13.0 %collective-permute-start.10 = (f32[1,6,128,128]{3,2,1,0:T(8,128)S(1)}, f32[1,6,128,128]{3,2,1,0:T(8,128)S(1)}, u32[]{:S(2)}, u32[]{:S(2)}) collective-permute-start(f32[1,6,128,128]{3,2,1,0:T(8,128)S(1)} %get-tuple-element.11), channel_id=1, source_target_pairs={{0,224},{32,0},{64,32},{96,64},{128,96},{160,128},{192,160},{224,1... | collective-permute-start | bytes 1179656 | tf_op jit(solution)/shard_map/ppermute | solution.py:31
  13.4 10.7 %collective-permute-start.14 = (f32[1,6,128,128]{3,2,1,0:T(8,128)S(1)}, f32[1,6,128,128]{3,2,1,0:T(8,128)}, u32[]{:S(2)}, u32[]{:S(2)}) collective-permute-start(f32[1,6,128,128]{3,2,1,0:T(8,128)S(1)} %get-tuple-element.11), channel_id=1, source_target_pairs={{0,32},{32,64},{64,96},{96,128},{128,160},{160,192},{192,224},{224... | collective-permute-start | bytes 1179656 | tf_op jit(solution)/shard_map/ppermute | solution.py:31
  13.4 16.0 %collective-permute-start.17 = (f32[1,6,128,128]{3,2,1,0:T(8,128)}, f32[1,6,128,128]{3,2,1,0:T(8,128)}, u32[]{:S(2)}, u32[]{:S(2)}) collective-permute-start(f32[1,6,128,128]{3,2,1,0:T(8,128)} %get-tuple-element.12), channel_id=1, source_target_pairs={{0,224},{32,0},{64,32},{96,64},{128,96},{160,128},{192,160},{224,1... | collective-permute-start | bytes 1179656 | tf_op jit(solution)/shard_map/ppermute | solution.py:31
  20.9 11.9 %collective-permute-start.6 = (f32[1,6,128,128]{3,2,1,0:T(8,128)}, f32[1,6,128,128]{3,2,1,0:T(8,128)S(1)}, u32[]{:S(2)}, u32[]{:S(2)}) collective-permute-start(f32[1,6,128,128]{3,2,1,0:T(8,128)} %get-tuple-element.12), channel_id=1, source_target_pairs={{0,32},{32,64},{64,96},{96,128},{128,160},{160,192},{192,224},{224... | collective-permute-start | bytes 1179656 | tf_op jit(solution)/shard_map/ppermute | solution.py:31
  21.0 15.2 %copy-start.13 = (s32[8]{0:T(128)}, s32[8]{0:T(128)S(1)}, u32[]{:S(2)}) copy-start(s32[8]{0:T(128)S(1)} %select_reduce_fusion.6) | copy-start | bytes 100
  24.1 30.8 %collective-permute-start = (f32[1,12,128,128]{3,2,1,0:T(8,128)S(1)}, f32[1,12,128,128]{3,2,1,0:T(8,128)S(1)}, u32[]{:S(2)}, u32[]{:S(2)}) collective-permute-start(f32[1,12,128,128]{3,2,1,0:T(8,128)S(1)} %copy-done.1), channel_id=1, source_target_pairs={{0,1},{1,0},{2,3},{3,2},{4,5},{5,4},{6,7},{7,6},{8,9},{9,8},{10,11... | collective-permute-start | bytes 2359304 | tf_op jit(solution)/shard_map/ppermute | solution.py:36
  29.4 10.0 %collective-permute-start.11 = (f32[1,6,128,128]{3,2,1,0:T(8,128)S(1)}, f32[1,6,128,128]{3,2,1,0:T(8,128)S(1)}, u32[]{:S(2)}, u32[]{:S(2)}) collective-permute-start(f32[1,6,128,128]{3,2,1,0:T(8,128)S(1)} %collective-permute-done.10.refs_11_), channel_id=1, source_target_pairs={{0,224},{32,0},{64,32},{96,64},{128,96},{160,128},{192,160},{224,1... | collective-permute-start | bytes 1179656 | tf_op jit(solution)/shard_map/ppermute | solution.py:31
  32.8 35.7 %copy-start.6 = (f32[1,6,128,128]{3,2,1,0:T(8,128)}, f32[1,6,128,128]{3,2,1,0:T(8,128)S(1)}, u32[]{:S(2)}) copy-start(f32[1,6,128,128]{3,2,1,0:T(8,128)S(1)} %collective-permute-done.6.refs_8_) | copy-start | bytes 1179652
  32.8 10.0 %collective-permute-start.15 = (f32[1,6,128,128]{3,2,1,0:T(8,128)}, f32[1,6,128,128]{3,2,1,0:T(8,128)}, u32[]{:S(2)}, u32[]{:S(2)}) collective-permute-start(f32[1,6,128,128]{3,2,1,0:T(8,128)} %collective-permute-done.14.refs_9_), channel_id=1, source_target_pairs={{0,32},{32,64},{64,96},{96,128},{128,160},{160,192},{192,224},{224... | collective-permute-start | bytes 1179656 | tf_op jit(solution)/shard_map/ppermute | solution.py:31
  33.5 15.0 %collective-permute-start.18 = (f32[1,6,128,128]{3,2,1,0:T(8,128)}, f32[1,6,128,128]{3,2,1,0:T(8,128)}, u32[]{:S(2)}, u32[]{:S(2)}) collective-permute-start(f32[1,6,128,128]{3,2,1,0:T(8,128)} %collective-permute-done.17.refs_10_), channel_id=1, source_target_pairs={{0,224},{32,0},{64,32},{96,64},{128,96},{160,128},{192,160},{224,1... | collective-permute-start | bytes 1179656 | tf_op jit(solution)/shard_map/ppermute | solution.py:31
  36.2 14.9 %collective-permute-start.7 = (f32[1,6,128,128]{3,2,1,0:T(8,128)S(1)}, f32[1,6,128,128]{3,2,1,0:T(8,128)S(1)}, u32[]{:S(2)}, u32[]{:S(2)}) collective-permute-start(f32[1,6,128,128]{3,2,1,0:T(8,128)S(1)} %collective-permute-done.6.refs_8_), channel_id=1, source_target_pairs={{0,32},{32,64},{64,96},{96,128},{128,160},{160,192},{192,224},{224... | collective-permute-start | bytes 1179656 | tf_op jit(solution)/shard_map/ppermute | solution.py:31
  39.3 27.2 %collective-permute-start.5 = (f32[1,12,128,128]{3,2,1,0:T(8,128)S(1)}, f32[1,12,128,128]{3,2,1,0:T(8,128)S(1)}, u32[]{:S(2)}, u32[]{:S(2)}) collective-permute-start(f32[1,12,128,128]{3,2,1,0:T(8,128)S(1)} %broadcast_select_fusion), channel_id=1, source_target_pairs={{31,0},{2,1},{1,2},{4,3},{3,4},{6,5},{5,6},{8,7},{7,8},{10,9},{9,1... | collective-permute-start | bytes 2359304 | tf_op jit(solution)/shard_map/ppermute | solution.py:240
  42.8 25.7 %collective-permute-start.3 = (f32[1,12,128,128]{3,2,1,0:T(8,128)S(1)}, f32[1,12,128,128]{3,2,1,0:T(8,128)S(1)}, u32[]{:S(2)}, u32[]{:S(2)}) collective-permute-start(f32[1,12,128,128]{3,2,1,0:T(8,128)S(1)} %collective-permute-done.1.refs_2_), channel_id=1, source_target_pairs={{0,1},{1,0},{2,3},{3,2},{4,5},{5,4},{6,7},{7,6},{8,9},{9,8},{10,11... | collective-permute-start | bytes 2359304 | tf_op jit(solution)/shard_map/ppermute | solution.py:36
  48.5 25.1 %collective-permute-start.4 = (f32[1,12,128,128]{3,2,1,0:T(8,128)S(1)}, f32[1,12,128,128]{3,2,1,0:T(8,128)}, u32[]{:S(2)}, u32[]{:S(2)}) collective-permute-start(f32[1,12,128,128]{3,2,1,0:T(8,128)S(1)} %collective-permute-done.2.refs_3_), channel_id=1, source_target_pairs={{0,1},{1,0},{2,3},{3,2},{4,5},{5,4},{6,7},{7,6},{8,9},{9,8},{10,11... | collective-permute-start | bytes 2359304 | tf_op jit(solution)/shard_map/ppermute | solution.py:36
  51.1 11.5 %collective-permute-start.12 = (f32[1,6,128,128]{3,2,1,0:T(8,128)S(1)}, f32[1,6,128,128]{3,2,1,0:T(8,128)}, u32[]{:S(2)}, u32[]{:S(2)}) collective-permute-start(f32[1,6,128,128]{3,2,1,0:T(8,128)S(1)} %collective-permute-done.11.refs_15_), channel_id=1, source_target_pairs={{0,224},{32,0},{64,32},{96,64},{128,96},{160,128},{192,160},{224,1... | collective-permute-start | bytes 1179656 | tf_op jit(solution)/shard_map/ppermute | solution.py:31
  54.1 0.8 copy-start.8
  54.8 11.7 %collective-permute-start.8 = (f32[1,6,128,128]{3,2,1,0:T(8,128)S(1)}, f32[1,6,128,128]{3,2,1,0:T(8,128)}, u32[]{:S(2)}, u32[]{:S(2)}) collective-permute-start(f32[1,6,128,128]{3,2,1,0:T(8,128)S(1)} %collective-permute-done.7.refs_12_), channel_id=1, source_target_pairs={{0,32},{32,64},{64,96},{96,128},{128,160},{160,192},{192,224},{224... | collective-permute-start | bytes 1179656 | tf_op jit(solution)/shard_map/ppermute | solution.py:31
  54.8 0.8 copy-start.10
  62.6 24.2 %collective-permute-start.16 = (f32[1,6,128,128]{3,2,1,0:T(8,128)}, f32[1,6,128,128]{3,2,1,0:T(8,128)}, u32[]{:S(2)}, u32[]{:S(2)}) collective-permute-start(f32[1,6,128,128]{3,2,1,0:T(8,128)} %collective-permute-done.15.refs_13_), channel_id=1, source_target_pairs={{0,32},{32,64},{64,96},{96,128},{128,160},{160,192},{192,224},{224... | collective-permute-start | bytes 1179656 | tf_op jit(solution)/shard_map/ppermute | solution.py:31
  66.6 20.2 %collective-permute-start.19 = (f32[1,6,128,128]{3,2,1,0:T(8,128)}, f32[1,6,128,128]{3,2,1,0:T(8,128)}, u32[]{:S(2)}, u32[]{:S(2)}) collective-permute-start(f32[1,6,128,128]{3,2,1,0:T(8,128)} %collective-permute-done.18.refs_14_), channel_id=1, source_target_pairs={{0,224},{32,0},{64,32},{96,64},{128,96},{160,128},{192,160},{224,1... | collective-permute-start | bytes 1179656 | tf_op jit(solution)/shard_map/ppermute | solution.py:31
  66.6 0.9 copy-start.2
  67.5 24.5 %collective-permute-start.13 = (f32[1,6,128,128]{3,2,1,0:T(8,128)}, f32[1,6,128,128]{3,2,1,0:T(8,128)}, u32[]{:S(2)}, u32[]{:S(2)}) collective-permute-start(f32[1,6,128,128]{3,2,1,0:T(8,128)} %collective-permute-done.12.refs_10_), channel_id=1, source_target_pairs={{0,224},{32,0},{64,32},{96,64},{128,96},{160,128},{192,160},{224,1... | collective-permute-start | bytes 1179656 | tf_op jit(solution)/shard_map/ppermute | solution.py:31
  68.5 0.9 copy-start.4
  69.4 22.6 %collective-permute-start.9 = (f32[1,6,128,128]{3,2,1,0:T(8,128)}, f32[1,6,128,128]{3,2,1,0:T(8,128)}, u32[]{:S(2)}, u32[]{:S(2)}) collective-permute-start(f32[1,6,128,128]{3,2,1,0:T(8,128)} %collective-permute-done.8.refs_7_), channel_id=1, source_target_pairs={{0,32},{32,64},{64,96},{96,128},{128,160},{160,192},{192,224},{224... | collective-permute-start | bytes 1179656 | tf_op jit(solution)/shard_map/ppermute | solution.py:31
  73.6 1.1 %copy-start.3 = (f32[1,12,128,128]{3,2,1,0:T(8,128)S(1)}, f32[1,12,128,128]{3,2,1,0:T(8,128)}, u32[]{:S(2)}) copy-start(f32[1,12,128,128]{3,2,1,0:T(8,128)} %copy-done.2) | copy-start | bytes 2359300
  74.8 1.1 %copy-start.5 = (f32[1,12,128,128]{3,2,1,0:T(8,128)S(1)}, f32[1,12,128,128]{3,2,1,0:T(8,128)}, u32[]{:S(2)}) copy-start(f32[1,12,128,128]{3,2,1,0:T(8,128)} %copy-done.4) | copy-start | bytes 2359300
  75.9 1.0 %copy-start.7 = (f32[1,6,128,128]{3,2,1,0:T(8,128)S(1)}, f32[1,6,128,128]{3,2,1,0:T(8,128)}, u32[]{:S(2)}) copy-start(f32[1,6,128,128]{3,2,1,0:T(8,128)} %copy-done.6) | copy-start | bytes 1179652
  76.9 1.0 %copy-start.9 = (f32[1,6,128,128]{3,2,1,0:T(8,128)S(1)}, f32[1,6,128,128]{3,2,1,0:T(8,128)}, u32[]{:S(2)}) copy-start(f32[1,6,128,128]{3,2,1,0:T(8,128)} %copy-done.8) | copy-start | bytes 1179652
  77.9 1.0 %copy-start.11 = (f32[1,6,128,128]{3,2,1,0:T(8,128)S(1)}, f32[1,6,128,128]{3,2,1,0:T(8,128)}, u32[]{:S(2)}) copy-start(f32[1,6,128,128]{3,2,1,0:T(8,128)} %copy-done.10) | copy-start | bytes 1179652
  78.9 0.7 copy-start.12

commit v2 on v1

v2 whole, which is shorter than its diff:
```python
import functools

import jax
import jax.numpy as jnp
from jax import lax
from jax.experimental import pallas as pl
from jax.experimental.pallas import tpu as pltpu
from jax.sharding import PartitionSpec as P

BS = 128
NNZ = 12
OT = 24
UNROLL = 4
LIST = 320
Z_EVEN = (0, -1, 1, -2, 2, -3, 3, 4)
Z_ODD = (0, 1, -1, 2, -2, 3, -3, 4)
X_EVEN = (0, 1, -2, -1, -3, 3, 2)
X_ODD = (0, -1, 2, 1, 3, -3, -2)
GROUPS = ((0, 1, 2), (3, 4), (5, 6), (7,))
NT = (((1,), (1,)), ((), ()))
DUMMY = OT << 16
TLIST = LIST
POFF = TLIST + 32
TOFF = POFF + 8
FLAG = TOFF + 8
META = 384


def swap_cores(block):
    n = lax.axis_size("col")
    return lax.ppermute(block, "col", [(i, i ^ 1) for i in range(n)])


def next_chip(block):
    n = lax.axis_size("col")
    return lax.ppermute(block, "col", [(i, (i + (-2 if i % 2 else 2)) % n) for i in range(n)])


def ring(block, turn):
    rows, cols = lax.axis_size("row"), lax.axis_size("col")
    route = []
    for r in range(rows):
        for c in range(cols):
            step = turn if c % 2 == 0 else -turn
            route.append((r * cols + c, (r + step) % rows * cols + c))
    return lax.ppermute(block, ("row", "col"), route)


def after(block, *others):
    return lax.optimization_barrier((block, others))[0]


def hold(block, token):
    return lax.optimization_barrier((block, token))


def pick(onehot, table):
    return jnp.dot(onehot.astype(jnp.int32), table, preferred_element_type=jnp.int32)


def work_list(row_index, col_index, perm, p_cols, out_pairs, flag):
    n_rows, n_cols = lax.axis_size("row"), lax.axis_size("col")
    even = (col_index % 2) == 0
    steps = jnp.where(even, jnp.array(X_EVEN, jnp.int32), jnp.array(X_ODD, jnp.int32))
    left_pos = row_index * n_cols + jnp.mod(col_index + steps, n_cols)
    turns = jnp.where(even, jnp.array(Z_EVEN, jnp.int32), jnp.array(Z_ODD, jnp.int32))
    right_pos = jnp.mod(row_index + turns, n_rows) * n_cols + col_index
    pos = jnp.concatenate([left_pos, right_pos])
    onehot = pos[:, None] == jnp.arange(perm.shape[0], dtype=jnp.int32)[None, :]
    ids = jnp.sum(jnp.where(onehot, perm[None, :], 0), axis=1)
    cols = pick(onehot, p_cols)
    nl = len(X_EVEN)
    left_hot = out_pairs[:, 0:1] == ids[None, :nl]
    right_hot = out_pairs[:, 1:2] == ids[None, nl:]
    left_cols = pick(left_hot, cols[:nl])
    right_cols = pick(right_hot, cols[nl:])
    left_at = jnp.sum(jnp.where(left_hot, jnp.arange(nl, dtype=jnp.int32)[None, :], 0), axis=1)
    right_at = jnp.sum(
        jnp.where(right_hot, jnp.arange(len(Z_EVEN), dtype=jnp.int32)[None, :], 0), axis=1
    )
    group_of = [g for row in range(len(Z_EVEN)) for g, rows in enumerate(GROUPS) if row in rows]
    group = jnp.sum(jnp.where(right_hot, jnp.array(group_of, jnp.int32)[None, :], 0), axis=1)
    slots = jnp.arange(NNZ, dtype=jnp.int32)
    match = left_cols[:, :, None] == right_cols[:, None, :]
    present = jnp.any(match, axis=2)
    partner = jnp.sum(jnp.where(match, slots[None, None, :], 0), axis=2)
    tiles = jnp.arange(OT, dtype=jnp.int32)
    payload = (
        (tiles[:, None] << 16)
        + ((left_at[:, None] * NNZ + slots[None, :]) << 8)
        + right_at[:, None] * NNZ
        + partner
    )
    count = jnp.sum(present.astype(jnp.int32), axis=1)
    earlier = (group[:, None] == group[None, :]) & (tiles[None, :] < tiles[:, None])
    row_start = jnp.sum(jnp.where(earlier, count[None, :], 0), axis=1)
    gs = jnp.arange(8, dtype=jnp.int32)
    in_group = group[None, :] == gs[:, None]
    steps_of = (jnp.sum(jnp.where(in_group, count[None, :], 0), axis=1) + UNROLL - 1) // UNROLL
    before = gs[None, :] < gs[:, None]
    step_start = jnp.sum(jnp.where(before, steps_of[None, :], 0), axis=1)
    tile_start = jnp.sum((group[None, :] < gs[:, None]).astype(jnp.int32), axis=1)
    ahead = jnp.sum(
        (present[:, None, :] & (slots[None, None, :] < slots[None, :, None])).astype(jnp.int32),
        axis=2,
    )
    group_start = jnp.sum(jnp.where(in_group, step_start[:, None], 0), axis=0) * UNROLL
    rank = jnp.where(present, group_start[:, None] + row_start[:, None] + ahead, -1)
    places = jnp.arange(LIST, dtype=jnp.int32)
    pairs = DUMMY + jnp.sum(
        jnp.where(rank[:, :, None] == places[None, None, :], payload[:, :, None] - DUMMY, 0),
        axis=(0, 1),
    )
    own_hit = left_cols == out_pairs[:, 1:2]
    own = jnp.sum(
        jnp.where(own_hit, left_at[:, None] * NNZ + slots[None, :] + 1, 0), axis=1
    )
    tile_rank = jnp.sum(
        ((group[None, :] < group[:, None]) | earlier).astype(jnp.int32), axis=1
    )
    tile_list = jnp.sum(
        jnp.where(
            tile_rank[:, None] == jnp.arange(32, dtype=jnp.int32)[None, :],
            ((tiles << 8) + own)[:, None],
            0,
        ),
        axis=0,
    )
    tail = jnp.full((META - FLAG,), flag, jnp.int32)
    return jnp.concatenate([pairs, tile_list, step_start, tile_start, tail]), ids


def split(block):
    high = block.astype(jnp.bfloat16)
    return high, (block - high.astype(jnp.float32)).astype(jnp.bfloat16)


def fetch(refs, rows, sems):
    copies = [pltpu.make_async_copy(ref.at[0], rows.at[i], sems.at[i]) for i, ref in enumerate(refs)]
    for copy in copies:
        copy.start()
    return copies


def prepare(n_left, meta, *refs):
    panel, base, token, rows, sems = refs[n_left:]
    token[...] = jnp.zeros_like(token)
    copies = fetch(refs[:n_left], rows, sems)
    for row, copy in enumerate(copies):
        copy.wait()

        def block(s, _, row=row):
            high, low = split(rows[row, s])
            panel[row * NNZ + s, :, :BS] = high
            panel[row * NNZ + s, :, BS:] = low
            return 0

        lax.fori_loop(0, NNZ, block, 0)
    doubled = meta[FLAG] == 1

    def own(i, _):
        item = meta[TLIST + i]
        tile, at = item >> 8, (item & 255) - 1
        scale = jnp.where((at >= 0) & doubled, 2.0, 0.0)
        at = jnp.maximum(at, 0)
        base[tile] = scale * rows[at // NNZ, at % NNZ]
        return 0

    lax.fori_loop(0, OT, own, 0)
    base[OT] = jnp.zeros((BS, BS), jnp.float32)


def split_rows(right, rows, right_panel, sems):
    copies = fetch(right, rows, sems)
    for row, copy in enumerate(copies):
        copy.wait()

        def block(s, _, row=row):
            high, low = split(rows[row, s])
            right_panel[row * NNZ + s, :BS] = high
            right_panel[row * NNZ + s, BS:] = low
            return 0

        lax.fori_loop(0, NNZ, block, 0)


def add_pairs(group, meta, panel, right_panel, acc):
    first = GROUPS[group][0] * NNZ
    sign = jnp.where(meta[FLAG] == 1, -1.0, 1.0)

    def pairs(step, _):
        for k in range(UNROLL):
            item = meta[step * UNROLL + k]
            tile = item >> 16
            l_at = (item >> 8) & 255
            r_at = jnp.maximum((item & 255) - first, 0)
            r = right_panel[r_at]
            both = lax.dot_general(
                panel[l_at],
                jnp.concatenate([r, r], axis=1),
                NT,
                preferred_element_type=jnp.float32,
            )
            acc[tile] = acc[tile] + sign * (both[:, :BS] + both[:, BS:])
        return 0

    lax.fori_loop(meta[POFF + group], meta[POFF + group + 1], pairs, 0)


def kernel(group, n_right, meta, panel, base, *refs):
    total, token, rows, right_panel, sems = refs[-5:]
    token[...] = jnp.zeros_like(token)
    split_rows(refs[:n_right], rows, right_panel, sems)
    add_pairs(group, meta, panel, right_panel, total)


def last_kernel(group, n_right, meta, panel, base, *refs):
    out, rows, right_panel, acc, sems, out_sems, all_sem = refs[-7:]
    whole = pltpu.make_async_copy(base.at[pl.ds(0, OT)], out, all_sem)
    whole.start()
    t0, t1 = meta[TOFF + group], meta[TOFF + group + 1]

    def begin(i, _):
        tile = meta[TLIST + i] >> 8
        acc[tile] = base[tile]
        return 0

    lax.fori_loop(t0, t1, begin, 0)
    acc[OT] = jnp.zeros((BS, BS), jnp.float32)
    split_rows(refs[:n_right], rows, right_panel, sems)
    add_pairs(group, meta, panel, right_panel, acc)
    whole.wait()

    def out_copy(i):
        tile = meta[TLIST + i] >> 8
        return pltpu.make_async_copy(acc.at[tile], out.at[tile], out_sems.at[tile])

    def leave(i, _):
        out_copy(i).start()
        return 0

    def drain(i, _):
        out_copy(i).wait()
        return 0

    lax.fori_loop(t0, t1, leave, 0)
    lax.fori_loop(t0, t1, drain, 0)


def in_hbm(blocks):
    return [pltpu.with_memory_space_constraint(block, pltpu.HBM) for block in blocks]


VMEM_SPEC = pl.BlockSpec(memory_space=pltpu.VMEM)
SMEM_SPEC = pl.BlockSpec(memory_space=pltpu.SMEM)
TOTAL = pltpu.VMEM((OT + 1, BS, BS), jnp.float32)
TOKEN = jax.ShapeDtypeStruct((8, BS), jnp.float32)
ANY_SPEC = pl.BlockSpec(memory_space=pl.ANY)


def run_prepare(meta, left):
    return pl.pallas_call(
        functools.partial(prepare, len(left)),
        out_shape=[
            pltpu.VMEM((len(left) * NNZ, BS, 2 * BS), jnp.bfloat16),
            TOTAL,
            TOKEN,
        ],
        in_specs=[SMEM_SPEC] + [ANY_SPEC] * len(left),
        out_specs=[VMEM_SPEC, VMEM_SPEC, VMEM_SPEC],
        scratch_shapes=[
            pltpu.VMEM((len(left), NNZ, BS, BS), jnp.float32),
            pltpu.SemaphoreType.DMA((len(left),)),
        ],
        cost_estimate=pl.CostEstimate(
            flops=5 << 20, bytes_accessed=12 << 20, transcendentals=0
        ),
        compiler_params=pltpu.CompilerParams(vmem_limit_bytes=16 << 20),
        name="left_panel",
    )(meta, *in_hbm(left))


def run_group(group, meta, panel, base, right, order):
    last = group == len(GROUPS) - 1
    if group < 2:
        right = in_hbm(right)
    operands = [meta, panel, base, *right, order]
    row_sems = pltpu.SemaphoreType.DMA((len(right),))
    scratch = [
        pltpu.VMEM((len(right), NNZ, BS, BS), jnp.float32),
        pltpu.VMEM((len(right) * NNZ, 2 * BS, BS), jnp.bfloat16),
    ]
    if last:
        scratch += [pltpu.VMEM((OT + 1, BS, BS), jnp.float32), row_sems]
        scratch += [pltpu.SemaphoreType.DMA((OT,)), pltpu.SemaphoreType.DMA]
    else:
        scratch += [row_sems]
    work = OT * len(right) // len(Z_EVEN) * 4
    return pl.pallas_call(
        functools.partial(last_kernel if last else kernel, group, len(right)),
        out_shape=jax.ShapeDtypeStruct((OT, BS, BS), jnp.float32) if last else [TOTAL, TOKEN],
        in_specs=[SMEM_SPEC, VMEM_SPEC, VMEM_SPEC] + [ANY_SPEC] * (len(right) + 1),
        out_specs=ANY_SPEC if last else [VMEM_SPEC, VMEM_SPEC],
        scratch_shapes=scratch,
        input_output_aliases={} if last else {2: 0},
        cost_estimate=pl.CostEstimate(
            flops=work * 8 * BS**3, bytes_accessed=4 << 20, transcendentals=0
        ),
        compiler_params=pltpu.CompilerParams(vmem_limit_bytes=16 << 20),
        name=f"pairs_{group}",
    )(*operands)


def shards(p_vals, p_cols, perm, out_pattern, branch_flag):
    row_index = lax.axis_index("row")
    col_index = lax.axis_index("col")
    meta, ids = work_list(row_index, col_index, perm, p_cols, out_pattern[0, 0], branch_flag[0, 0])

    one1 = ring(p_vals, 1)
    partner = swap_cores(p_vals)
    near = next_chip(p_vals)
    other1 = ring(after(p_vals, ids), -1)
    near_partner = next_chip(partner)
    one2 = ring(one1, 1)
    near_swapped = swap_cores(after(near, one1))
    other2 = ring(after(other1, near_partner), -1)
    far_partner = next_chip(near_partner)
    near_partner_swapped = swap_cores(near_partner)
    one3 = ring(one2, 1)
    panel, base, token = run_prepare(
        meta,
        [p_vals, partner, near, near_partner, far_partner, near_swapped, near_partner_swapped],
    )
    other3 = ring(other2, -1)
    before4, token = hold(one3, token)
    one4 = ring(before4, 1)
    total, token = run_group(0, meta, panel, base, [p_vals, one1, other1], token)
    total, token = run_group(1, meta, panel, total, [one2, other2], token)
    total, token = run_group(2, meta, panel, total, [one3, other3], token)
    out = run_group(3, meta, panel, total, [one4], token)
    return out.reshape((1, 1) + out.shape)


def solution(mesh):
    return jax.shard_map(
        shards,
        mesh=mesh,
        in_specs=(
            P(("row", "col"), None, None, None),
            P(),
            P(),
            P("row", "col", None, None),
            P("row", "col"),
        ),
        out_specs=P("row", "col", None, None, None),
        check_vma=False,
    )
```

time: 97.6 us -> 79.7 us (0.82)
  the two profiles are of different devices: /device:TPU:1 before, /device:TPU:122 now
where the time goes in v2:
time: 79.7 us; the launch traced here: 79.5 us
  waiting for transfers between devices  36.4 us (46%)
  starting transfers between devices  18.5 us (23%)
  Pallas kernels  18 us (23%)
  other arithmetic  4.18 us (5%)
  local copies, waits for them, and re-layouts  0.93 us (1%)
  between operations  0.88 us (1%)
    ppermute x7, waiting for transfers between devices, ring(): return lax.ppermute(block, ('row', 'col'), route)  36.4 us
    ppermute x7, starting transfers between devices, ring(): return lax.ppermute(block, ('row', 'col'), route)  14.3 us
    pallas_call x4, Pallas kernels, run_group(): pl.pallas_call(functools.partial(last_kernel if last else kernel, group,...  14.1 us
    ppermute x3, starting transfers between devices, next_chip(): lax.ppermute(block, 'col', [(i, (i + (-2 if i % 2 else 2)) % n) for i in...  4.04 us
    pallas_call x1, Pallas kernels, run_prepare(): pl.pallas_call(functools.partial(prepare, len(left)), out_shape=[pltpu.VM...  3.89 us
  transfers between devices with their start and end apart: 13, of which 4 were waited for; matrix products, arithmetic and copies ran while one was open for 7% of the time, Pallas kernels for 19%

profile of v2, /device:TPU:122, one launch (start us, length us, event | category | flops | bytes accessed | tf_op | source)
XLA Modules:
  0.0 79.5 jit_solution(8275715525696938466)
XLA Ops:
  0.0 0.0 collective-permute-start
  0.0 3.2 %collective-permute-start.4 = (f32[1,12,128,128]{3,2,1,0:T(8,128)}, f32[1,12,128,128]{3,2,1,0:T(8,128)S(1)}, u32[]{:S(2)}, u32[]{:S(2)}) collective-permute-start(f32[1,12,128,128]{3,2,1,0:T(8,128)} %refs_0_.3), channel_id=1, source_target_pairs={{0,32},{1,225},{2,34},{3,227},{4,36},{5,229},{6,38},{7,231},{8,40}... | collective-permute-start | bytes 2359304 | tf_op jit(solution)/shard_map/ppermute | solution.py:46
  3.2 1.5 %collective-permute-start.1 = (f32[1,12,128,128]{3,2,1,0:T(8,128)}, f32[1,12,128,128]{3,2,1,0:T(8,128)}, u32[]{:S(2)}, u32[]{:S(2)}) collective-permute-start(f32[1,12,128,128]{3,2,1,0:T(8,128)} %refs_0_.3), channel_id=1, source_target_pairs={{0,2},{1,31},{2,4},{3,1},{4,6},{5,3},{6,8},{7,5},{8,10},{9,7},{10,... | collective-permute-start | bytes 2359304 | tf_op jit(solution)/shard_map/ppermute | solution.py:36
  4.7 0.7 fusion.21
  5.4 0.7 fusion.19
  6.1 0.1 pad_add_fusion
  6.1 0.9 %select_reduce_fusion.1 = s32[15]{0:T(128)S(1)} fusion(s32[256]{0:T(256)} %param.12, s32[15]{0:T(128)S(1)} %pad_add_fusion), kind=kLoop, calls=%fused_computation.6 | loop fusion | flops 11505 | bytes 1144 | tf_op jit(solution)/shard_map/reduce_sum | solution.py:70
  7.0 0.1 collective-permute-start.7
  7.1 0.1 slice.23
  7.2 0.2 fusion.1
  7.3 0.8 slice_bitcast_fusion.1
  8.1 0.2 fusion.4
  8.3 0.2 fusion.6
  8.6 0.7 fusion.9
  9.3 0.1 select_reduce_fusion.7
  9.5 0.1 select_reduce_fusion.6
  9.6 0.1 fusion.8
  9.7 0.2 convert_reduce_fusion.1
  9.9 0.1 convert_reduce_fusion
  10.0 0.0 collective-permute-done.refs_1_
  10.0 0.0 copy-start.2
  10.1 1.3 %collective-permute-start.2 = (f32[1,12,128,128]{3,2,1,0:T(8,128)S(1)}, f32[1,12,128,128]{3,2,1,0:T(8,128)}, u32[]{:S(2)}, u32[]{:S(2)}) collective-permute-start(f32[1,12,128,128]{3,2,1,0:T(8,128)S(1)} %collective-permute-done.refs_1_), channel_id=1, source_target_pairs={{0,2},{1,31},{2,4},{3,1},{4,6},{5,3},{6,8},{7,5},{8,10},{9,7},{10,... | collective-permute-start | bytes 2359304 | tf_op jit(solution)/shard_map/ppermute | solution.py:36
  11.3 8.0 %collective-permute-done.4.refs_1_ = f32[1,12,128,128]{3,2,1,0:T(8,128)S(1)} collective-permute-done((f32[1,12,128,128]{3,2,1,0:T(8,128)}, f32[1,12,128,128]{3,2,1,0:T(8,128)S(1)}, u32[]{:S(2)}, u32[]{:S(2)}) %collective-permute-start.4) | collective-permute-done | bytes 786464 | tf_op jit(solution)/shard_map/ppermute | solution.py:46
  19.3 3.6 %collective-permute-start.8 = (f32[1,12,128,128]{3,2,1,0:T(8,128)S(1)}, f32[1,12,128,128]{3,2,1,0:T(8,128)}, u32[]{:S(2)}, u32[]{:S(2)}) collective-permute-start(f32[1,12,128,128]{3,2,1,0:T(8,128)S(1)} %collective-permute-done.4.refs_1_), channel_id=1, source_target_pairs={{0,32},{1,225},{2,34},{3,227},{4,36},{5,229},{6,38},{7,231},{8,40}... | collective-permute-start | bytes 2359304 | tf_op jit(solution)/shard_map/ppermute | solution.py:46
  22.9 0.1 convert_reduce_fusion.3
  23.1 0.0 collective-permute-done.1.refs_2_
  23.1 0.1 collective-permute-start.5
  23.2 0.9 %collective-permute-done.7.refs_2_ = f32[1,12,128,128]{3,2,1,0:T(8,128)S(1)} collective-permute-done((f32[1,12,128,128]{3,2,1,0:T(8,128)}, f32[1,12,128,128]{3,2,1,0:T(8,128)S(1)}, u32[]{:S(2)}, u32[]{:S(2)}) %collective-permute-start.7) | collective-permute-done | bytes 786464 | tf_op jit(solution)/shard_map/ppermute | solution.py:46
  24.2 0.0 collective-permute-done.2.refs_3_
  24.2 0.0 collective-permute-start.10
  24.2 1.3 %collective-permute-start.3 = (f32[1,12,128,128]{3,2,1,0:T(8,128)}, f32[1,12,128,128]{3,2,1,0:T(8,128)}, u32[]{:S(2)}, u32[]{:S(2)}) collective-permute-start(f32[1,12,128,128]{3,2,1,0:T(8,128)} %collective-permute-done.2.refs_3_), channel_id=1, source_target_pairs={{0,2},{1,31},{2,4},{3,1},{4,6},{5,3},{6,8},{7,5},{8,10},{9,7},{10,... | collective-permute-start | bytes 2359304 | tf_op jit(solution)/shard_map/ppermute | solution.py:36
  25.4 0.0 collective-permute-start.6
  25.4 14.4 %collective-permute-done.8.refs_0_ = f32[1,12,128,128]{3,2,1,0:T(8,128)} collective-permute-done((f32[1,12,128,128]{3,2,1,0:T(8,128)S(1)}, f32[1,12,128,128]{3,2,1,0:T(8,128)}, u32[]{:S(2)}, u32[]{:S(2)}) %collective-permute-start.8) | collective-permute-done | bytes 786464 | tf_op jit(solution)/shard_map/ppermute | solution.py:46
  39.9 3.8 %collective-permute-start.9 = (f32[1,12,128,128]{3,2,1,0:T(8,128)}, f32[1,12,128,128]{3,2,1,0:T(8,128)S(1)}, u32[]{:S(2)}, u32[]{:S(2)}) collective-permute-start(f32[1,12,128,128]{3,2,1,0:T(8,128)} %collective-permute-done.8.refs_0_), channel_id=1, source_target_pairs={{0,32},{1,225},{2,34},{3,227},{4,36},{5,229},{6,38},{7,231},{8,40}... | collective-permute-start | bytes 2359304 | tf_op jit(solution)/shard_map/ppermute | solution.py:46
  43.7 0.2 select_reduce_fusion
  43.9 0.0 collective-permute-done.10.refs_1_
  43.9 0.1 collective-permute-start.11
  44.0 0.1 select_reduce_fusion.2
  44.7 0.1 concatenate.7.meta
  44.8 0.0 collective-permute-done.5.refs_5_
  44.8 3.9 %left_panel.1 = (bf16[84,128,256]{2,1,0:T(8,128)(2,1)S(1)}, f32[25,128,128]{2,1,0:T(8,128)S(1)}, f32[8,128]{1,0:T(8,128)S(1)}) custom-call(s32[384]{0:T(512)S(1)} %concatenate.7.meta, f32[1,12,128,128]{3,2,1,0:T(8,128)} %refs_0_.3, f32[1,12,128,128]{3,2,1,0:T(8,128)} %copy-done.2, f32[1,12,128,128]{3,2,1,0:T(8,128)} %collective-permute-done.1.refs_2_, ...), custom_call_target="tpu_custom_call" | custom-call | flops 5242880 | bytes 12582912 | tf_op jit(solution)/shard_map/left_panel/pallas_call | solution.py:262
  48.7 13.0 %collective-permute-done.9.refs_0_ = f32[1,12,128,128]{3,2,1,0:T(8,128)S(1)} collective-permute-done((f32[1,12,128,128]{3,2,1,0:T(8,128)}, f32[1,12,128,128]{3,2,1,0:T(8,128)S(1)}, u32[]{:S(2)}, u32[]{:S(2)}) %collective-permute-start.9) | collective-permute-done | bytes 786464 | tf_op jit(solution)/shard_map/ppermute | solution.py:46
  61.7 3.6 %collective-permute-start.12 = (f32[1,12,128,128]{3,2,1,0:T(8,128)S(1)}, f32[1,12,128,128]{3,2,1,0:T(8,128)S(1)}, u32[]{:S(2)}, u32[]{:S(2)}) collective-permute-start(f32[1,12,128,128]{3,2,1,0:T(8,128)S(1)} %collective-permute-done.9.refs_0_), channel_id=1, source_target_pairs={{0,32},{1,225},{2,34},{3,227},{4,36},{5,229},{6,38},{7,231},{8,40}... | collective-permute-start | bytes 2359304 | tf_op jit(solution)/shard_map/ppermute | solution.py:46
  65.3 4.9 %pairs_0.1 = (f32[25,128,128]{2,1,0:T(8,128)S(1)}, f32[8,128]{1,0:T(8,128)S(1)}) custom-call(s32[384]{0:T(512)S(1)} %concatenate.7.meta, bf16[84,128,256]{2,1,0:T(8,128)(2,1)S(1)} %get-tuple-element.20.panel, f32[25,128,128]{2,1,0:T(8,128)S(1)} %get-tuple-element.21.base, f32[1,12,128,128]{3,2,1,0:T(8,128)} %refs_0_.3, ...), custom_call_target="tpu_custom_call", output_to_operand_aliasing={{0}: (2, {})} | custom-call | flops 603979776 | bytes 4194304 | tf_op jit(solution)/shard_map/pairs_0/pallas_call | solution.py:299
  70.3 3.1 %pairs_1.1 = (f32[25,128,128]{2,1,0:T(8,128)S(1)}, f32[8,128]{1,0:T(8,128)S(1)}) custom-call(s32[384]{0:T(512)S(1)} %concatenate.7.meta, bf16[84,128,256]{2,1,0:T(8,128)(2,1)S(1)} %get-tuple-element.20.panel, f32[25,128,128]{2,1,0:T(8,128)S(1)} %get-tuple-element.25.base, ...), custom_call_target="tpu_custom_call", output_to_operand_aliasing={{0}: (2, {})} | custom-call | flops 402653184 | bytes 4194304 | tf_op jit(solution)/shard_map/pairs_1/pallas_call | solution.py:299
  73.3 0.0 collective-permute-done.11.refs_1_
  73.3 3.6 %pairs_2.1 = (f32[25,128,128]{2,1,0:T(8,128)S(1)}, f32[8,128]{1,0:T(8,128)S(1)}) custom-call(s32[384]{0:T(512)S(1)} %concatenate.7.meta, bf16[84,128,256]{2,1,0:T(8,128)(2,1)S(1)} %get-tuple-element.20.panel, f32[25,128,128]{2,1,0:T(8,128)S(1)} %get-tuple-element.28.base, ...), custom_call_target="tpu_custom_call", output_to_operand_aliasing={{0}: (2, {})} | custom-call | flops 402653184 | bytes 4194304 | tf_op jit(solution)/shard_map/pairs_2/pallas_call | solution.py:299
  76.9 2.6 %pairs_3.1 = f32[24,128,128]{2,1,0:T(8,128)} custom-call(s32[384]{0:T(512)S(1)} %concatenate.7.meta, bf16[84,128,256]{2,1,0:T(8,128)(2,1)S(1)} %get-tuple-element.20.panel, f32[25,128,128]{2,1,0:T(8,128)S(1)} %get-tuple-element.30.base, f32[1,12,128,128]{3,2,1,0:T(8,128)S(1)} %collective-permute-done.12.refs_0_, f32[8,128]{1,0:T(8,128)S(1)} %get-tuple-element.32.refs_1_), custom_call_target="tpu_custom_call" | custom-call | flops 201326592 | bytes 4194304 | tf_op jit(solution)/shard_map/pairs_3/pallas_call | solution.py:299
  (23 shorter events, 0.2 us)
Async XLA Ops:
  0.0 7.2 %copy-start = (s32[256,12]{0,1:T(8,128)S(1)}, s32[256,12]{0,1:T(8,128)}, u32[]{:S(2)}) copy-start(s32[256,12]{0,1:T(8,128)} %param.11) | copy-start | bytes 36868
  0.0 10.0 %collective-permute-start = (f32[1,12,128,128]{3,2,1,0:T(8,128)}, f32[1,12,128,128]{3,2,1,0:T(8,128)S(1)}, u32[]{:S(2)}, u32[]{:S(2)}) collective-permute-start(f32[1,12,128,128]{3,2,1,0:T(8,128)} %refs_0_.3), channel_id=1, source_target_pairs={{0,1},{1,0},{2,3},{3,2},{4,5},{5,4},{6,7},{7,6},{8,9},{9,8},{10,11... | collective-permute-start | bytes 2359304 | tf_op jit(solution)/shard_map/ppermute | solution.py:31
  0.0 19.3 %collective-permute-start.4 = (f32[1,12,128,128]{3,2,1,0:T(8,128)}, f32[1,12,128,128]{3,2,1,0:T(8,128)S(1)}, u32[]{:S(2)}, u32[]{:S(2)}) collective-permute-start(f32[1,12,128,128]{3,2,1,0:T(8,128)} %refs_0_.3), channel_id=1, source_target_pairs={{0,32},{1,225},{2,34},{3,227},{4,36},{5,229},{6,38},{7,231},{8,40}... | collective-permute-start | bytes 2359304 | tf_op jit(solution)/shard_map/ppermute | solution.py:46
  3.2 19.9 %collective-permute-start.1 = (f32[1,12,128,128]{3,2,1,0:T(8,128)}, f32[1,12,128,128]{3,2,1,0:T(8,128)}, u32[]{:S(2)}, u32[]{:S(2)}) collective-permute-start(f32[1,12,128,128]{3,2,1,0:T(8,128)} %refs_0_.3), channel_id=1, source_target_pairs={{0,2},{1,31},{2,4},{3,1},{4,6},{5,3},{6,8},{7,5},{8,10},{9,7},{10,... | collective-permute-start | bytes 2359304 | tf_op jit(solution)/shard_map/ppermute | solution.py:36
  7.0 17.2 %collective-permute-start.7 = (f32[1,12,128,128]{3,2,1,0:T(8,128)}, f32[1,12,128,128]{3,2,1,0:T(8,128)S(1)}, u32[]{:S(2)}, u32[]{:S(2)}) collective-permute-start(f32[1,12,128,128]{3,2,1,0:T(8,128)} %refs_0_.3), channel_id=1, source_target_pairs={{0,224},{1,33},{2,226},{3,35},{4,228},{5,37},{6,230},{7,39},{8,232... | collective-permute-start | bytes 2359304 | tf_op jit(solution)/shard_map/ppermute | solution.py:46
  10.0 34.8 %copy-start.2 = (f32[1,12,128,128]{3,2,1,0:T(8,128)}, f32[1,12,128,128]{3,2,1,0:T(8,128)S(1)}, u32[]{:S(2)}) copy-start(f32[1,12,128,128]{3,2,1,0:T(8,128)S(1)} %collective-permute-done.refs_1_) | copy-start | bytes 2359300
  10.1 14.1 %collective-permute-start.2 = (f32[1,12,128,128]{3,2,1,0:T(8,128)S(1)}, f32[1,12,128,128]{3,2,1,0:T(8,128)}, u32[]{:S(2)}, u32[]{:S(2)}) collective-permute-start(f32[1,12,128,128]{3,2,1,0:T(8,128)S(1)} %collective-permute-done.refs_1_), channel_id=1, source_target_pairs={{0,2},{1,31},{2,4},{3,1},{4,6},{5,3},{6,8},{7,5},{8,10},{9,7},{10,... | collective-permute-start | bytes 2359304 | tf_op jit(solution)/shard_map/ppermute | solution.py:36
  19.3 29.4 %copy-start.1 = (f32[1,12,128,128]{3,2,1,0:T(8,128)}, f32[1,12,128,128]{3,2,1,0:T(8,128)S(1)}, u32[]{:S(2)}) copy-start(f32[1,12,128,128]{3,2,1,0:T(8,128)S(1)} %collective-permute-done.4.refs_1_) | copy-start | bytes 2359300
  19.3 20.5 %collective-permute-start.8 = (f32[1,12,128,128]{3,2,1,0:T(8,128)S(1)}, f32[1,12,128,128]{3,2,1,0:T(8,128)}, u32[]{:S(2)}, u32[]{:S(2)}) collective-permute-start(f32[1,12,128,128]{3,2,1,0:T(8,128)S(1)} %collective-permute-done.4.refs_1_), channel_id=1, source_target_pairs={{0,32},{1,225},{2,34},{3,227},{4,36},{5,229},{6,38},{7,231},{8,40}... | collective-permute-start | bytes 2359304 | tf_op jit(solution)/shard_map/ppermute | solution.py:46
  23.1 21.7 %collective-permute-start.5 = (f32[1,12,128,128]{3,2,1,0:T(8,128)}, f32[1,12,128,128]{3,2,1,0:T(8,128)}, u32[]{:S(2)}, u32[]{:S(2)}) collective-permute-start(f32[1,12,128,128]{3,2,1,0:T(8,128)} %collective-permute-done.1.refs_2_), channel_id=1, source_target_pairs={{0,1},{1,0},{2,3},{3,2},{4,5},{5,4},{6,7},{7,6},{8,9},{9,8},{10,11... | collective-permute-start | bytes 2359304 | tf_op jit(solution)/shard_map/ppermute | solution.py:31
  24.2 19.7 %copy-start.3 = (f32[1,12,128,128]{3,2,1,0:T(8,128)}, f32[1,12,128,128]{3,2,1,0:T(8,128)S(1)}, u32[]{:S(2)}) copy-start(f32[1,12,128,128]{3,2,1,0:T(8,128)S(1)} %collective-permute-done.7.refs_2_) | copy-start | bytes 2359300
  24.2 19.7 %collective-permute-start.10 = (f32[1,12,128,128]{3,2,1,0:T(8,128)S(1)}, f32[1,12,128,128]{3,2,1,0:T(8,128)}, u32[]{:S(2)}, u32[]{:S(2)}) collective-permute-start(f32[1,12,128,128]{3,2,1,0:T(8,128)S(1)} %collective-permute-done.7.refs_2_), channel_id=1, source_target_pairs={{0,224},{1,33},{2,226},{3,35},{4,228},{5,37},{6,230},{7,39},{8,232... | collective-permute-start | bytes 2359304 | tf_op jit(solution)/shard_map/ppermute | solution.py:46
  24.2 20.6 %collective-permute-start.3 = (f32[1,12,128,128]{3,2,1,0:T(8,128)}, f32[1,12,128,128]{3,2,1,0:T(8,128)}, u32[]{:S(2)}, u32[]{:S(2)}) collective-permute-start(f32[1,12,128,128]{3,2,1,0:T(8,128)} %collective-permute-done.2.refs_3_), channel_id=1, source_target_pairs={{0,2},{1,31},{2,4},{3,1},{4,6},{5,3},{6,8},{7,5},{8,10},{9,7},{10,... | collective-permute-start | bytes 2359304 | tf_op jit(solution)/shard_map/ppermute | solution.py:36
  25.4 19.4 %collective-permute-start.6 = (f32[1,12,128,128]{3,2,1,0:T(8,128)}, f32[1,12,128,128]{3,2,1,0:T(8,128)}, u32[]{:S(2)}, u32[]{:S(2)}) collective-permute-start(f32[1,12,128,128]{3,2,1,0:T(8,128)} %collective-permute-done.2.refs_3_), channel_id=1, source_target_pairs={{0,1},{1,0},{2,3},{3,2},{4,5},{5,4},{6,7},{7,6},{8,9},{9,8},{10,11... | collective-permute-start | bytes 2359304 | tf_op jit(solution)/shard_map/ppermute | solution.py:31
  39.9 21.9 %collective-permute-start.9 = (f32[1,12,128,128]{3,2,1,0:T(8,128)}, f32[1,12,128,128]{3,2,1,0:T(8,128)S(1)}, u32[]{:S(2)}, u32[]{:S(2)}) collective-permute-start(f32[1,12,128,128]{3,2,1,0:T(8,128)} %collective-permute-done.8.refs_0_), channel_id=1, source_target_pairs={{0,32},{1,225},{2,34},{3,227},{4,36},{5,229},{6,38},{7,231},{8,40}... | collective-permute-start | bytes 2359304 | tf_op jit(solution)/shard_map/ppermute | solution.py:46
  43.9 29.5 %collective-permute-start.11 = (f32[1,12,128,128]{3,2,1,0:T(8,128)}, f32[1,12,128,128]{3,2,1,0:T(8,128)S(1)}, u32[]{:S(2)}, u32[]{:S(2)}) collective-permute-start(f32[1,12,128,128]{3,2,1,0:T(8,128)} %collective-permute-done.10.refs_1_), channel_id=1, source_target_pairs={{0,224},{1,33},{2,226},{3,35},{4,228},{5,37},{6,230},{7,39},{8,232... | collective-permute-start | bytes 2359304 | tf_op jit(solution)/shard_map/ppermute | solution.py:46
  61.7 15.2 %collective-permute-start.12 = (f32[1,12,128,128]{3,2,1,0:T(8,128)S(1)}, f32[1,12,128,128]{3,2,1,0:T(8,128)S(1)}, u32[]{:S(2)}, u32[]{:S(2)}) collective-permute-start(f32[1,12,128,128]{3,2,1,0:T(8,128)S(1)} %collective-permute-done.9.refs_0_), channel_id=1, source_target_pairs={{0,32},{1,225},{2,34},{3,227},{4,36},{5,229},{6,38},{7,231},{8,40}... | collective-permute-start | bytes 2359304 | tf_op jit(solution)/shard_map/ppermute | solution.py:46

commit v3 on v2

--- a/solution.py
+++ b/solution.py
@@ -10,10 +10,11 @@
 BS = 128
 NNZ = 12
 OT = 24
+HALF = NNZ // 2
 UNROLL = 4
 LIST = 320
-Z_EVEN = (0, -1, 1, -2, 2, -3, 3, 4)
-Z_ODD = (0, 1, -1, 2, -2, 3, -3, 4)
+Z_EVEN = (-1, 1, 0, -2, 2, -3, 3, 4)
+Z_ODD = (1, -1, 0, 2, -2, 3, -3, 4)
 X_EVEN = (0, 1, -2, -1, -3, 3, 2)
 X_ODD = (0, -1, 2, 1, 3, -3, -2)
 GROUPS = ((0, 1, 2), (3, 4), (5, 6), (7,))
@@ -135,53 +136,69 @@
     return high, (block - high.astype(jnp.float32)).astype(jnp.bfloat16)
 
 
-def fetch(refs, rows, sems):
-    copies = [pltpu.make_async_copy(ref.at[0], rows.at[i], sems.at[i]) for i, ref in enumerate(refs)]
+def prepare(n_left, meta, *refs):
+    left = refs[:n_left]
+    panel, base, token, rows, sems = refs[-5:]
+    token[...] = jnp.zeros_like(token)
+    copies = [
+        pltpu.make_async_copy(ref.at[0], rows.at[pl.ds(i * NNZ, NNZ)], sems.at[i])
+        for i, ref in enumerate(left)
+    ]
     for copy in copies:
         copy.start()
-    return copies
-
-
-def prepare(n_left, meta, *refs):
-    panel, base, token, rows, sems = refs[n_left:]
-    token[...] = jnp.zeros_like(token)
-    copies = fetch(refs[:n_left], rows, sems)
+
+    def clear(tile, _):
+        base[tile] = jnp.zeros((BS, BS), jnp.float32)
+        return 0
+
+    lax.fori_loop(0, OT + 1, clear, 0)
     for row, copy in enumerate(copies):
         copy.wait()
 
-        def block(s, _, row=row):
-            high, low = split(rows[row, s])
-            panel[row * NNZ + s, :, :BS] = high
-            panel[row * NNZ + s, :, BS:] = low
+        def block(at, _):
+            high, low = split(rows[at])
+            panel[at, :, :BS] = high
+            panel[at, :, BS:] = low
             return 0
 
-        lax.fori_loop(0, NNZ, block, 0)
+        lax.fori_loop(row * NNZ, (row + 1) * NNZ, block, 0)
     doubled = meta[FLAG] == 1
 
     def own(i, _):
         item = meta[TLIST + i]
         tile, at = item >> 8, (item & 255) - 1
-        scale = jnp.where((at >= 0) & doubled, 2.0, 0.0)
-        at = jnp.maximum(at, 0)
-        base[tile] = scale * rows[at // NNZ, at % NNZ]
+
+        @pl.when((at >= 0) & doubled)
+        def _():
+            base[tile] = 2.0 * rows[at]
+
         return 0
 
     lax.fori_loop(0, OT, own, 0)
-    base[OT] = jnp.zeros((BS, BS), jnp.float32)
-
-
-def split_rows(right, rows, right_panel, sems):
-    copies = fetch(right, rows, sems)
-    for row, copy in enumerate(copies):
+
+
+def split_rows(right, right_panel, own=None):
+    first = 0
+    if own is not None:
+        source, rows, sem = own
+        copy = pltpu.make_async_copy(source.at[0], rows, sem)
+        copy.start()
+    for ref in right:
+        split_row(ref.at[0], first, ref.shape[1], right_panel)
+        first += ref.shape[1]
+    if own is not None:
         copy.wait()
-
-        def block(s, _, row=row):
-            high, low = split(rows[row, s])
-            right_panel[row * NNZ + s, :BS] = high
-            right_panel[row * NNZ + s, BS:] = low
-            return 0
-
-        lax.fori_loop(0, NNZ, block, 0)
+        split_row(rows, first, NNZ, right_panel)
+
+
+def split_row(blocks, first, size, right_panel):
+    def block(at, _):
+        high, low = split(blocks[at])
+        right_panel[first + at, :BS] = high
+        right_panel[first + at, BS:] = low
+        return 0
+
+    lax.fori_loop(0, size, block, 0)
 
 
 def add_pairs(group, meta, panel, right_panel, acc):
@@ -208,14 +225,17 @@
 
 
 def kernel(group, n_right, meta, panel, base, *refs):
-    total, token, rows, right_panel, sems = refs[-5:]
+    own = None
+    if group == 0:
+        own, refs = (refs[n_right], *refs[-2:]), refs[:-2]
+    total, token, right_panel = refs[-3:]
     token[...] = jnp.zeros_like(token)
-    split_rows(refs[:n_right], rows, right_panel, sems)
+    split_rows(refs[:n_right], right_panel, own)
     add_pairs(group, meta, panel, right_panel, total)
 
 
 def last_kernel(group, n_right, meta, panel, base, *refs):
-    out, rows, right_panel, acc, sems, out_sems, all_sem = refs[-7:]
+    out, right_panel, acc, out_sems, all_sem = refs[-5:]
     whole = pltpu.make_async_copy(base.at[pl.ds(0, OT)], out, all_sem)
     whole.start()
     t0, t1 = meta[TOFF + group], meta[TOFF + group + 1]
@@ -227,7 +247,7 @@
 
     lax.fori_loop(t0, t1, begin, 0)
     acc[OT] = jnp.zeros((BS, BS), jnp.float32)
-    split_rows(refs[:n_right], rows, right_panel, sems)
+    split_rows(refs[:n_right], right_panel)
     add_pairs(group, meta, panel, right_panel, acc)
     whole.wait()
 
@@ -245,10 +265,6 @@
 
     lax.fori_loop(t0, t1, leave, 0)
     lax.fori_loop(t0, t1, drain, 0)
-
-
-def in_hbm(blocks):
-    return [pltpu.with_memory_space_constraint(block, pltpu.HBM) for block in blocks]
 
 
 VMEM_SPEC = pl.BlockSpec(memory_space=pltpu.VMEM)
@@ -256,6 +272,10 @@
 TOTAL = pltpu.VMEM((OT + 1, BS, BS), jnp.float32)
 TOKEN = jax.ShapeDtypeStruct((8, BS), jnp.float32)
 ANY_SPEC = pl.BlockSpec(memory_space=pl.ANY)
+
+
+def in_hbm(block):
+    return pltpu.with_memory_space_constraint(block, pltpu.HBM)
 
 
 def run_prepare(meta, left):
@@ -269,7 +289,7 @@
         in_specs=[SMEM_SPEC] + [ANY_SPEC] * len(left),
         out_specs=[VMEM_SPEC, VMEM_SPEC, VMEM_SPEC],
         scratch_shapes=[
-            pltpu.VMEM((len(left), NNZ, BS, BS), jnp.float32),
+            pltpu.VMEM((len(left) * NNZ, BS, BS), jnp.float32),
             pltpu.SemaphoreType.DMA((len(left),)),
         ],
         cost_estimate=pl.CostEstimate(
@@ -277,38 +297,32 @@
         ),
         compiler_params=pltpu.CompilerParams(vmem_limit_bytes=16 << 20),
         name="left_panel",
-    )(meta, *in_hbm(left))
-
-
-def run_group(group, meta, panel, base, right, order):
+    )(meta, *[in_hbm(block) for block in left])
+
+
+def run_group(group, meta, panel, base, right, order, own=None):
     last = group == len(GROUPS) - 1
-    if group < 2:
-        right = in_hbm(right)
-    operands = [meta, panel, base, *right, order]
-    row_sems = pltpu.SemaphoreType.DMA((len(right),))
-    scratch = [
-        pltpu.VMEM((len(right), NNZ, BS, BS), jnp.float32),
-        pltpu.VMEM((len(right) * NNZ, 2 * BS, BS), jnp.bfloat16),
-    ]
+    blocks = sum(block.shape[1] for block in right)
+    extra = [order] if own is None else [in_hbm(own), order]
+    scratch = [pltpu.VMEM((len(GROUPS[group]) * NNZ, 2 * BS, BS), jnp.bfloat16)]
     if last:
-        scratch += [pltpu.VMEM((OT + 1, BS, BS), jnp.float32), row_sems]
+        scratch += [pltpu.VMEM((OT + 1, BS, BS), jnp.float32)]
         scratch += [pltpu.SemaphoreType.DMA((OT,)), pltpu.SemaphoreType.DMA]
-    else:
-        scratch += [row_sems]
-    work = OT * len(right) // len(Z_EVEN) * 4
+    if own is not None:
+        scratch += [pltpu.VMEM((NNZ, BS, BS), jnp.float32), pltpu.SemaphoreType.DMA]
     return pl.pallas_call(
         functools.partial(last_kernel if last else kernel, group, len(right)),
         out_shape=jax.ShapeDtypeStruct((OT, BS, BS), jnp.float32) if last else [TOTAL, TOKEN],
-        in_specs=[SMEM_SPEC, VMEM_SPEC, VMEM_SPEC] + [ANY_SPEC] * (len(right) + 1),
+        in_specs=[SMEM_SPEC] + [VMEM_SPEC] * (len(right) + 2) + [ANY_SPEC] * len(extra),
         out_specs=ANY_SPEC if last else [VMEM_SPEC, VMEM_SPEC],
         scratch_shapes=scratch,
         input_output_aliases={} if last else {2: 0},
         cost_estimate=pl.CostEstimate(
-            flops=work * 8 * BS**3, bytes_accessed=4 << 20, transcendentals=0
+            flops=blocks * 16 * BS**3, bytes_accessed=4 << 20, transcendentals=0
         ),
         compiler_params=pltpu.CompilerParams(vmem_limit_bytes=16 << 20),
         name=f"pairs_{group}",
-    )(*operands)
+    )(meta, panel, base, *right, *extra)
 
 
 def shards(p_vals, p_cols, perm, out_pattern, branch_flag):
@@ -318,26 +332,33 @@
 
     one1 = ring(p_vals, 1)
     partner = swap_cores(p_vals)
-    near = next_chip(p_vals)
     other1 = ring(after(p_vals, ids), -1)
+    near = next_chip(after(p_vals, partner))
     near_partner = next_chip(partner)
     one2 = ring(one1, 1)
     near_swapped = swap_cores(after(near, one1))
-    other2 = ring(after(other1, near_partner), -1)
+    other2 = ring(after(other1, near_partner, meta), -1)
     far_partner = next_chip(near_partner)
     near_partner_swapped = swap_cores(near_partner)
-    one3 = ring(one2, 1)
+    one2_low, one2_high = one2[:, :HALF], one2[:, HALF:]
+    other2_low, other2_high = other2[:, :HALF], other2[:, HALF:]
+    one3_low = ring(one2_low, 1)
+    other3_high = ring(other2_high, -1)
+    one3_high = ring(after(one2_high, other2), 1)
+    other3_low = ring(other2_low, -1)
     panel, base, token = run_prepare(
         meta,
         [p_vals, partner, near, near_partner, far_partner, near_swapped, near_partner_swapped],
     )
-    other3 = ring(other2, -1)
-    before4, token = hold(one3, token)
-    one4 = ring(before4, 1)
-    total, token = run_group(0, meta, panel, base, [p_vals, one1, other1], token)
+    before4, token = hold(one3_low, token)
+    one4_low = ring(before4, 1)
+    other4_high = ring(other3_high, -1)
+    total, token = run_group(0, meta, panel, base, [one1, other1], token, p_vals)
     total, token = run_group(1, meta, panel, total, [one2, other2], token)
-    total, token = run_group(2, meta, panel, total, [one3, other3], token)
-    out = run_group(3, meta, panel, total, [one4], token)
+    total, token = run_group(
+        2, meta, panel, total, [one3_low, one3_high, other3_low, other3_high], token
+    )
+    out = run_group(3, meta, panel, total, [one4_low, other4_high], token)
     return out.reshape((1, 1) + out.shape)
 
 

time: 79.7 us -> 74.3 us (0.932)
  the two profiles are of different devices: /device:TPU:122 before, /device:TPU:145 now
where the time goes in v3:
time: 74.3 us; the launch traced here: 74.4 us
  waiting for transfers between devices  35.3 us (48%)
  Pallas kernels  15.5 us (21%)
  starting transfers between devices  15.2 us (20%)
  other arithmetic  4.17 us (6%)
  local copies, waits for them, and re-layouts  2.76 us (4%)
  between operations  0.89 us (1%)
    ppermute x10, waiting for transfers between devices, ring(): return lax.ppermute(block, ('row', 'col'), route)  30 us
    pallas_call x4, Pallas kernels, run_group(): pl.pallas_call(functools.partial(last_kernel if last else kernel, group,...  11.7 us
    ppermute x10, starting transfers between devices, ring(): return lax.ppermute(block, ('row', 'col'), route)  6.56 us
    ppermute x3, starting transfers between devices, swap_cores(): return lax.ppermute(block, 'col', [(i, i ^ 1) for i in range(n)])  5.33 us
    ppermute x3, waiting for transfers between devices, next_chip(): lax.ppermute(block, 'col', [(i, (i + (-2 if i % 2 else 2)) % n) for i in...  5.24 us
    pallas_call x1, Pallas kernels, run_prepare(): pl.pallas_call(functools.partial(prepare, len(left)), out_shape=[pltpu.VM...  3.73 us
    ppermute x3, starting transfers between devices, next_chip(): lax.ppermute(block, 'col', [(i, (i + (-2 if i % 2 else 2)) % n) for i in...  3.33 us
    unnamed x10, local copies, waits for them, and re-layouts  1.75 us
  transfers between devices with their start and end apart: 16, of which 7 were waited for; matrix products, arithmetic and copies ran while one was open for 8% of the time, Pallas kernels for 16%

profile of v3, /device:TPU:145, one launch (start us, length us, event | category | flops | bytes accessed | tf_op | source)
XLA Modules:
  0.0 74.4 jit_solution(7730798454980908170)
XLA Ops:
  0.0 0.7 collective-permute-start
  0.7 0.0 collective-permute-start.4
  0.7 0.7 fusion.21
  1.4 0.7 fusion.19
  2.0 0.1 pad_add_fusion
  2.1 0.9 %select_reduce_fusion.1 = s32[15]{0:T(128)S(1)} fusion(s32[256]{0:T(256)} %param.12, s32[15]{0:T(128)S(1)} %pad_add_fusion), kind=kLoop, calls=%fused_computation.6 | loop fusion | flops 11505 | bytes 1144 | tf_op jit(solution)/shard_map/reduce_sum | solution.py:71
  3.0 1.5 %collective-permute-start.7 = (f32[1,12,128,128]{3,2,1,0:T(8,128)}, f32[1,12,128,128]{3,2,1,0:T(8,128)S(1)}, u32[]{:S(2)}, u32[]{:S(2)}) collective-permute-start(f32[1,12,128,128]{3,2,1,0:T(8,128)} %refs_2_.1), channel_id=1, source_target_pairs={{0,224},{1,33},{2,226},{3,35},{4,228},{5,37},{6,230},{7,39},{8,232... | collective-permute-start | bytes 2359304 | tf_op jit(solution)/shard_map/ppermute | solution.py:47
  4.5 0.1 slice.35
  4.6 0.2 fusion.1
  4.8 0.8 %slice_bitcast_fusion.1 = (s32[24]{0:T(128)S(1)}, s32[24]{0:T(128)S(1)}) fusion(s32[24,2]{0,1:T(2,128)} %bitcast.10), kind=kLoop, calls=%fused_computation.70 | loop fusion | bytes 384 | tf_op jit(solution)/shard_map/eq | solution.py:74
  5.5 0.2 fusion.4
  5.7 0.2 fusion.6
  6.0 0.1 fusion.8
  6.1 0.7 fusion.9
  6.9 0.2 convert_reduce_fusion.1
  7.1 0.1 select_reduce_fusion.7
  7.2 0.1 select_reduce_fusion.6
  7.3 0.1 convert_reduce_fusion
  7.4 0.1 convert_reduce_fusion.3
  7.6 0.0 copy-start.1
  7.6 2.4 %collective-permute-start.2 = (f32[1,12,128,128]{3,2,1,0:T(8,128)S(1)}, f32[1,12,128,128]{3,2,1,0:T(8,128)}, u32[]{:S(2)}, u32[]{:S(2)}) collective-permute-start(f32[1,12,128,128]{3,2,1,0:T(8,128)S(1)} %collective-permute-done.refs_1_), channel_id=1, source_target_pairs={{0,2},{1,31},{2,4},{3,1},{4,6},{5,3},{6,8},{7,5},{8,10},{9,7},{10,... | collective-permute-start | bytes 2359304 | tf_op jit(solution)/shard_map/ppermute | solution.py:37
  10.1 0.2 select_reduce_fusion
  10.3 0.6 collective-permute-start.1
  10.9 5.7 %collective-permute-done.4.refs_0_ = f32[1,12,128,128]{3,2,1,0:T(8,128)S(1)} collective-permute-done((f32[1,12,128,128]{3,2,1,0:T(8,128)}, f32[1,12,128,128]{3,2,1,0:T(8,128)S(1)}, u32[]{:S(2)}, u32[]{:S(2)}) %collective-permute-start.4) | collective-permute-done | bytes 786464 | tf_op jit(solution)/shard_map/ppermute | solution.py:47
  16.6 0.0 collective-permute-start.8
  16.6 0.1 select_reduce_fusion.2
  17.3 0.1 concatenate.7.meta
  17.4 4.9 %collective-permute-done.7.refs_1_ = f32[1,12,128,128]{3,2,1,0:T(8,128)S(1)} collective-permute-done((f32[1,12,128,128]{3,2,1,0:T(8,128)}, f32[1,12,128,128]{3,2,1,0:T(8,128)S(1)}, u32[]{:S(2)}, u32[]{:S(2)}) %collective-permute-start.7) | collective-permute-done | bytes 786464 | tf_op jit(solution)/shard_map/ppermute | solution.py:47
  22.3 5.2 %collective-permute-done.1.refs_2_ = f32[1,12,128,128]{3,2,1,0:T(8,128)} collective-permute-done((f32[1,12,128,128]{3,2,1,0:T(8,128)}, f32[1,12,128,128]{3,2,1,0:T(8,128)}, u32[]{:S(2)}, u32[]{:S(2)}) %collective-permute-start.1) | collective-permute-done | bytes 786464 | tf_op jit(solution)/shard_map/ppermute | solution.py:37
  27.5 4.7 %collective-permute-start.5 = (f32[1,12,128,128]{3,2,1,0:T(8,128)}, f32[1,12,128,128]{3,2,1,0:T(8,128)S(1)}, u32[]{:S(2)}, u32[]{:S(2)}) collective-permute-start(f32[1,12,128,128]{3,2,1,0:T(8,128)} %collective-permute-done.1.refs_2_), channel_id=1, source_target_pairs={{0,1},{1,0},{2,3},{3,2},{4,5},{5,4},{6,7},{7,6},{8,9},{9,8},{10,11... | collective-permute-start | bytes 2359304 | tf_op jit(solution)/shard_map/ppermute | solution.py:32
  32.2 0.3 collective-permute-start.3
  32.5 0.1 fusion.25
  32.5 0.4 collective-permute-start.9
  32.9 9.0 %collective-permute-done.10.refs_1_ = f32[1,12,128,128]{3,2,1,0:T(8,128)S(1)} collective-permute-done((f32[1,12,128,128]{3,2,1,0:T(8,128)S(1)}, f32[1,12,128,128]{3,2,1,0:T(8,128)S(1)}, u32[]{:S(2)}, u32[]{:S(2)}) %collective-permute-start.10) | collective-permute-done | bytes 786464 | tf_op jit(solution)/shard_map/ppermute | solution.py:47
  42.0 0.1 fusion.24
  42.0 0.1 collective-permute-start.13
  42.1 2.6 %collective-permute-start.11 = (f32[1,6,128,128]{3,2,1,0:T(8,128)S(1)}, f32[1,6,128,128]{3,2,1,0:T(8,128)S(1)}, u32[]{:S(2)}, u32[]{:S(2)}) collective-permute-start(f32[1,6,128,128]{3,2,1,0:T(8,128)S(1)} %get-tuple-element.32), channel_id=1, source_target_pairs={{0,32},{1,225},{2,34},{3,227},{4,36},{5,229},{6,38},{7,231},{8,40}... | collective-permute-start | bytes 1179656 | tf_op jit(solution)/shard_map/ppermute | solution.py:47
  44.8 0.9 %copy-done.3 = f32[1,12,128,128]{3,2,1,0:T(8,128)} copy-done((f32[1,12,128,128]{3,2,1,0:T(8,128)}, f32[1,12,128,128]{3,2,1,0:T(8,128)S(1)}, u32[]{:S(2)}) %copy-start.3) | copy-done | bytes 786456
  45.7 0.9 %copy-done.4 = f32[1,12,128,128]{3,2,1,0:T(8,128)} copy-done((f32[1,12,128,128]{3,2,1,0:T(8,128)}, f32[1,12,128,128]{3,2,1,0:T(8,128)S(1)}, u32[]{:S(2)}) %copy-start.4) | copy-done | bytes 786456
  46.5 3.7 %left_panel.1 = (bf16[84,128,256]{2,1,0:T(8,128)(2,1)S(1)}, f32[25,128,128]{2,1,0:T(8,128)S(1)}, f32[8,128]{1,0:T(8,128)S(1)}) custom-call(s32[384]{0:T(512)S(1)} %concatenate.7.meta, f32[1,12,128,128]{3,2,1,0:T(8,128)} %refs_2_.1, f32[1,12,128,128]{3,2,1,0:T(8,128)} %copy-done.1, f32[1,12,128,128]{3,2,1,0:T(8,128)} %collective-permute-done.1.refs_2_, ...), custom_call_target="tpu_custom_call" | custom-call | flops 5242880 | bytes 12582912 | tf_op jit(solution)/shard_map/left_panel/pallas_call | solution.py:282
  50.3 1.9 %collective-permute-start.14 = (f32[1,6,128,128]{3,2,1,0:T(8,128)S(1)}, f32[1,6,128,128]{3,2,1,0:T(8,128)S(1)}, u32[]{:S(2)}, u32[]{:S(2)}) collective-permute-start(f32[1,6,128,128]{3,2,1,0:T(8,128)S(1)} %collective-permute-done.9.refs_0_), channel_id=1, source_target_pairs={{0,32},{1,225},{2,34},{3,227},{4,36},{5,229},{6,38},{7,231},{8,40}... | collective-permute-start | bytes 1179656 | tf_op jit(solution)/shard_map/ppermute | solution.py:47
  52.2 2.2 %collective-permute-done.13.refs_3_ = f32[1,6,128,128]{3,2,1,0:T(8,128)S(1)} collective-permute-done((f32[1,6,128,128]{3,2,1,0:T(8,128)S(1)}, f32[1,6,128,128]{3,2,1,0:T(8,128)S(1)}, u32[]{:S(2)}, u32[]{:S(2)}) %collective-permute-start.13) | collective-permute-done | bytes 393248 | tf_op jit(solution)/shard_map/ppermute | solution.py:47
  54.4 3.8 %pairs_0.1 = (f32[25,128,128]{2,1,0:T(8,128)S(1)}, f32[8,128]{1,0:T(8,128)S(1)}) custom-call(s32[384]{0:T(512)S(1)} %concatenate.7.meta, bf16[84,128,256]{2,1,0:T(8,128)(2,1)S(1)} %get-tuple-element.23.panel, f32[25,128,128]{2,1,0:T(8,128)S(1)} %get-tuple-element.24.base, ...), custom_call_target="tpu_custom_call", output_to_operand_aliasing={{0}: (2, {})} | custom-call | flops 805306368 | bytes 4194304 | tf_op jit(solution)/shard_map/pairs_0/pallas_call | solution.py:313
  58.2 2.5 %pairs_1.1 = (f32[25,128,128]{2,1,0:T(8,128)S(1)}, f32[8,128]{1,0:T(8,128)S(1)}) custom-call(s32[384]{0:T(512)S(1)} %concatenate.7.meta, bf16[84,128,256]{2,1,0:T(8,128)(2,1)S(1)} %get-tuple-element.23.panel, f32[25,128,128]{2,1,0:T(8,128)S(1)} %get-tuple-element.28.base, ...), custom_call_target="tpu_custom_call", output_to_operand_aliasing={{0}: (2, {})} | custom-call | flops 805306368 | bytes 4194304 | tf_op jit(solution)/shard_map/pairs_1/pallas_call | solution.py:313
  60.7 2.2 %collective-permute-done.12.refs_2_ = f32[1,6,128,128]{3,2,1,0:T(8,128)S(1)} collective-permute-done((f32[1,6,128,128]{3,2,1,0:T(8,128)S(1)}, f32[1,6,128,128]{3,2,1,0:T(8,128)S(1)}, u32[]{:S(2)}, u32[]{:S(2)}) %collective-permute-start.12) | collective-permute-done | bytes 393248 | tf_op jit(solution)/shard_map/ppermute | solution.py:47
  62.9 1.8 %pairs_2.1 = (f32[25,128,128]{2,1,0:T(8,128)S(1)}, f32[8,128]{1,0:T(8,128)S(1)}) custom-call(s32[384]{0:T(512)S(1)} %concatenate.7.meta, bf16[84,128,256]{2,1,0:T(8,128)(2,1)S(1)} %get-tuple-element.23.panel, f32[25,128,128]{2,1,0:T(8,128)S(1)} %get-tuple-element.31.base, ...), custom_call_target="tpu_custom_call", output_to_operand_aliasing={{0}: (2, {})} | custom-call | flops 805306368 | bytes 4194304 | tf_op jit(solution)/shard_map/pairs_2/pallas_call | solution.py:313
  64.7 6.0 %collective-permute-done.15.refs_1_ = f32[1,6,128,128]{3,2,1,0:T(8,128)S(1)} collective-permute-done((f32[1,6,128,128]{3,2,1,0:T(8,128)S(1)}, f32[1,6,128,128]{3,2,1,0:T(8,128)S(1)}, u32[]{:S(2)}, u32[]{:S(2)}) %collective-permute-start.15) | collective-permute-done | bytes 393248 | tf_op jit(solution)/shard_map/ppermute | solution.py:47
  70.7 3.7 %pairs_3.1 = f32[24,128,128]{2,1,0:T(8,128)} custom-call(s32[384]{0:T(512)S(1)} %concatenate.7.meta, bf16[84,128,256]{2,1,0:T(8,128)(2,1)S(1)} %get-tuple-element.23.panel, f32[25,128,128]{2,1,0:T(8,128)S(1)} %get-tuple-element.34.base, f32[1,6,128,128]{3,2,1,0:T(8,128)S(1)} %collective-permute-done.14.refs_0_, ...), custom_call_target="tpu_custom_call" | custom-call | flops 402653184 | bytes 4194304 | tf_op jit(solution)/shard_map/pairs_3/pallas_call | solution.py:313
  (33 shorter events, 0.2 us)
Async XLA Ops:
  0.0 4.6 %copy-start = (s32[256,12]{0,1:T(8,128)S(1)}, s32[256,12]{0,1:T(8,128)}, u32[]{:S(2)}) copy-start(s32[256,12]{0,1:T(8,128)} %param.11) | copy-start | bytes 36868
  0.0 7.6 %collective-permute-start = (f32[1,12,128,128]{3,2,1,0:T(8,128)}, f32[1,12,128,128]{3,2,1,0:T(8,128)S(1)}, u32[]{:S(2)}, u32[]{:S(2)}) collective-permute-start(f32[1,12,128,128]{3,2,1,0:T(8,128)} %refs_2_.1), channel_id=1, source_target_pairs={{0,1},{1,0},{2,3},{3,2},{4,5},{5,4},{6,7},{7,6},{8,9},{9,8},{10,11... | collective-permute-start | bytes 2359304 | tf_op jit(solution)/shard_map/ppermute | solution.py:32
  0.7 15.9 %collective-permute-start.4 = (f32[1,12,128,128]{3,2,1,0:T(8,128)}, f32[1,12,128,128]{3,2,1,0:T(8,128)S(1)}, u32[]{:S(2)}, u32[]{:S(2)}) collective-permute-start(f32[1,12,128,128]{3,2,1,0:T(8,128)} %refs_2_.1), channel_id=1, source_target_pairs={{0,32},{1,225},{2,34},{3,227},{4,36},{5,229},{6,38},{7,231},{8,40}... | collective-permute-start | bytes 2359304 | tf_op jit(solution)/shard_map/ppermute | solution.py:47
  3.0 19.3 %collective-permute-start.7 = (f32[1,12,128,128]{3,2,1,0:T(8,128)}, f32[1,12,128,128]{3,2,1,0:T(8,128)S(1)}, u32[]{:S(2)}, u32[]{:S(2)}) collective-permute-start(f32[1,12,128,128]{3,2,1,0:T(8,128)} %refs_2_.1), channel_id=1, source_target_pairs={{0,224},{1,33},{2,226},{3,35},{4,228},{5,37},{6,230},{7,39},{8,232... | collective-permute-start | bytes 2359304 | tf_op jit(solution)/shard_map/ppermute | solution.py:47
  7.6 37.2 %copy-start.1 = (f32[1,12,128,128]{3,2,1,0:T(8,128)}, f32[1,12,128,128]{3,2,1,0:T(8,128)S(1)}, u32[]{:S(2)}) copy-start(f32[1,12,128,128]{3,2,1,0:T(8,128)S(1)} %collective-permute-done.refs_1_) | copy-start | bytes 2359300
  7.6 14.7 %collective-permute-start.2 = (f32[1,12,128,128]{3,2,1,0:T(8,128)S(1)}, f32[1,12,128,128]{3,2,1,0:T(8,128)}, u32[]{:S(2)}, u32[]{:S(2)}) collective-permute-start(f32[1,12,128,128]{3,2,1,0:T(8,128)S(1)} %collective-permute-done.refs_1_), channel_id=1, source_target_pairs={{0,2},{1,31},{2,4},{3,1},{4,6},{5,3},{6,8},{7,5},{8,10},{9,7},{10,... | collective-permute-start | bytes 2359304 | tf_op jit(solution)/shard_map/ppermute | solution.py:37
  10.3 17.3 %collective-permute-start.1 = (f32[1,12,128,128]{3,2,1,0:T(8,128)}, f32[1,12,128,128]{3,2,1,0:T(8,128)}, u32[]{:S(2)}, u32[]{:S(2)}) collective-permute-start(f32[1,12,128,128]{3,2,1,0:T(8,128)} %refs_2_.1), channel_id=1, source_target_pairs={{0,2},{1,31},{2,4},{3,1},{4,6},{5,3},{6,8},{7,5},{8,10},{9,7},{10,... | collective-permute-start | bytes 2359304 | tf_op jit(solution)/shard_map/ppermute | solution.py:37
  16.6 15.9 %collective-permute-start.8 = (f32[1,12,128,128]{3,2,1,0:T(8,128)S(1)}, f32[1,12,128,128]{3,2,1,0:T(8,128)S(1)}, u32[]{:S(2)}, u32[]{:S(2)}) collective-permute-start(f32[1,12,128,128]{3,2,1,0:T(8,128)S(1)} %collective-permute-done.4.refs_0_), channel_id=1, source_target_pairs={{0,32},{1,225},{2,34},{3,227},{4,36},{5,229},{6,38},{7,231},{8,40}... | collective-permute-start | bytes 2359304 | tf_op jit(solution)/shard_map/ppermute | solution.py:47
  22.3 19.6 %collective-permute-start.10 = (f32[1,12,128,128]{3,2,1,0:T(8,128)S(1)}, f32[1,12,128,128]{3,2,1,0:T(8,128)S(1)}, u32[]{:S(2)}, u32[]{:S(2)}) collective-permute-start(f32[1,12,128,128]{3,2,1,0:T(8,128)S(1)} %collective-permute-done.7.refs_1_), channel_id=1, source_target_pairs={{0,224},{1,33},{2,226},{3,35},{4,228},{5,37},{6,230},{7,39},{8,232... | collective-permute-start | bytes 2359304 | tf_op jit(solution)/shard_map/ppermute | solution.py:47
  27.5 14.6 %collective-permute-start.5 = (f32[1,12,128,128]{3,2,1,0:T(8,128)}, f32[1,12,128,128]{3,2,1,0:T(8,128)S(1)}, u32[]{:S(2)}, u32[]{:S(2)}) collective-permute-start(f32[1,12,128,128]{3,2,1,0:T(8,128)} %collective-permute-done.1.refs_2_), channel_id=1, source_target_pairs={{0,1},{1,0},{2,3},{3,2},{4,5},{5,4},{6,7},{7,6},{8,9},{9,8},{10,11... | collective-permute-start | bytes 2359304 | tf_op jit(solution)/shard_map/ppermute | solution.py:32
  32.2 12.6 %collective-permute-start.3 = (f32[1,12,128,128]{3,2,1,0:T(8,128)}, f32[1,12,128,128]{3,2,1,0:T(8,128)S(1)}, u32[]{:S(2)}, u32[]{:S(2)}) collective-permute-start(f32[1,12,128,128]{3,2,1,0:T(8,128)} %collective-permute-done.2.refs_3_), channel_id=1, source_target_pairs={{0,2},{1,31},{2,4},{3,1},{4,6},{5,3},{6,8},{7,5},{8,10},{9,7},{10,... | collective-permute-start | bytes 2359304 | tf_op jit(solution)/shard_map/ppermute | solution.py:37
  32.5 12.3 %collective-permute-start.6 = (f32[1,12,128,128]{3,2,1,0:T(8,128)}, f32[1,12,128,128]{3,2,1,0:T(8,128)S(1)}, u32[]{:S(2)}, u32[]{:S(2)}) collective-permute-start(f32[1,12,128,128]{3,2,1,0:T(8,128)} %collective-permute-done.2.refs_3_), channel_id=1, source_target_pairs={{0,1},{1,0},{2,3},{3,2},{4,5},{5,4},{6,7},{7,6},{8,9},{9,8},{10,11... | collective-permute-start | bytes 2359304 | tf_op jit(solution)/shard_map/ppermute | solution.py:32
  32.5 17.8 %collective-permute-start.9 = (f32[1,6,128,128]{3,2,1,0:T(8,128)S(1)}, f32[1,6,128,128]{3,2,1,0:T(8,128)S(1)}, u32[]{:S(2)}, u32[]{:S(2)}) collective-permute-start(f32[1,6,128,128]{3,2,1,0:T(8,128)S(1)} %get-tuple-element.46), channel_id=1, source_target_pairs={{0,32},{1,225},{2,34},{3,227},{4,36},{5,229},{6,38},{7,231},{8,40}... | collective-permute-start | bytes 1179656 | tf_op jit(solution)/shard_map/ppermute | solution.py:47
  42.0 12.4 %collective-permute-start.13 = (f32[1,6,128,128]{3,2,1,0:T(8,128)S(1)}, f32[1,6,128,128]{3,2,1,0:T(8,128)S(1)}, u32[]{:S(2)}, u32[]{:S(2)}) collective-permute-start(f32[1,6,128,128]{3,2,1,0:T(8,128)S(1)} %get-tuple-element.43), channel_id=1, source_target_pairs={{0,224},{1,33},{2,226},{3,35},{4,228},{5,37},{6,230},{7,39},{8,232... | collective-permute-start | bytes 1179656 | tf_op jit(solution)/shard_map/ppermute | solution.py:47
  42.1 2.7 %copy-start.2 = (f32[1,12,128,128]{3,2,1,0:T(8,128)}, f32[1,12,128,128]{3,2,1,0:T(8,128)S(1)}, u32[]{:S(2)}) copy-start(f32[1,12,128,128]{3,2,1,0:T(8,128)S(1)} %collective-permute-done.5.refs_5_) | copy-start | bytes 2359300
  42.1 18.6 %collective-permute-start.11 = (f32[1,6,128,128]{3,2,1,0:T(8,128)S(1)}, f32[1,6,128,128]{3,2,1,0:T(8,128)S(1)}, u32[]{:S(2)}, u32[]{:S(2)}) collective-permute-start(f32[1,6,128,128]{3,2,1,0:T(8,128)S(1)} %get-tuple-element.32), channel_id=1, source_target_pairs={{0,32},{1,225},{2,34},{3,227},{4,36},{5,229},{6,38},{7,231},{8,40}... | collective-permute-start | bytes 1179656 | tf_op jit(solution)/shard_map/ppermute | solution.py:47
  44.8 0.9 %copy-start.3 = (f32[1,12,128,128]{3,2,1,0:T(8,128)}, f32[1,12,128,128]{3,2,1,0:T(8,128)S(1)}, u32[]{:S(2)}) copy-start(f32[1,12,128,128]{3,2,1,0:T(8,128)S(1)} %collective-permute-done.3.refs_4_) | copy-start | bytes 2359300
  44.8 18.1 %collective-permute-start.12 = (f32[1,6,128,128]{3,2,1,0:T(8,128)S(1)}, f32[1,6,128,128]{3,2,1,0:T(8,128)S(1)}, u32[]{:S(2)}, u32[]{:S(2)}) collective-permute-start(f32[1,6,128,128]{3,2,1,0:T(8,128)S(1)} %get-tuple-element.44), channel_id=1, source_target_pairs={{0,224},{1,33},{2,226},{3,35},{4,228},{5,37},{6,230},{7,39},{8,232... | collective-permute-start | bytes 1179656 | tf_op jit(solution)/shard_map/ppermute | solution.py:47
  45.7 0.9 %copy-start.4 = (f32[1,12,128,128]{3,2,1,0:T(8,128)}, f32[1,12,128,128]{3,2,1,0:T(8,128)S(1)}, u32[]{:S(2)}) copy-start(f32[1,12,128,128]{3,2,1,0:T(8,128)S(1)} %collective-permute-done.6.refs_6_) | copy-start | bytes 2359300
  50.3 14.4 %collective-permute-start.14 = (f32[1,6,128,128]{3,2,1,0:T(8,128)S(1)}, f32[1,6,128,128]{3,2,1,0:T(8,128)S(1)}, u32[]{:S(2)}, u32[]{:S(2)}) collective-permute-start(f32[1,6,128,128]{3,2,1,0:T(8,128)S(1)} %collective-permute-done.9.refs_0_), channel_id=1, source_target_pairs={{0,32},{1,225},{2,34},{3,227},{4,36},{5,229},{6,38},{7,231},{8,40}... | collective-permute-start | bytes 1179656 | tf_op jit(solution)/shard_map/ppermute | solution.py:47
  54.4 16.3 %collective-permute-start.15 = (f32[1,6,128,128]{3,2,1,0:T(8,128)S(1)}, f32[1,6,128,128]{3,2,1,0:T(8,128)S(1)}, u32[]{:S(2)}, u32[]{:S(2)}) collective-permute-start(f32[1,6,128,128]{3,2,1,0:T(8,128)S(1)} %collective-permute-done.13.refs_3_), channel_id=1, source_target_pairs={{0,224},{1,33},{2,226},{3,35},{4,228},{5,37},{6,230},{7,39},{8,232... | collective-permute-start | bytes 1179656 | tf_op jit(solution)/shard_map/ppermute | solution.py:47

commit v4 on v3

--- a/solution.py
+++ b/solution.py
@@ -138,57 +138,47 @@
 
 def prepare(n_left, meta, *refs):
     left = refs[:n_left]
-    panel, base, token, rows, sems = refs[-5:]
+    panel, base, token = refs[n_left:]
     token[...] = jnp.zeros_like(token)
-    copies = [
-        pltpu.make_async_copy(ref.at[0], rows.at[pl.ds(i * NNZ, NNZ)], sems.at[i])
-        for i, ref in enumerate(left)
-    ]
-    for copy in copies:
-        copy.start()
+    use = meta[FLAG] == 1
 
     def clear(tile, _):
         base[tile] = jnp.zeros((BS, BS), jnp.float32)
         return 0
 
     lax.fori_loop(0, OT + 1, clear, 0)
-    for row, copy in enumerate(copies):
-        copy.wait()
-
-        def block(at, _):
-            high, low = split(rows[at])
-            panel[at, :, :BS] = high
-            panel[at, :, BS:] = low
+    for row, ref in enumerate(left):
+
+        def block(at, _, row=row, ref=ref):
+            high, low = split(ref[0, at])
+            panel[row * NNZ + at, :, :BS] = high
+            panel[row * NNZ + at, :, BS:] = low
             return 0
 
-        lax.fori_loop(row * NNZ, (row + 1) * NNZ, block, 0)
-    doubled = meta[FLAG] == 1
-
-    def own(i, _):
-        item = meta[TLIST + i]
-        tile, at = item >> 8, (item & 255) - 1
-
-        @pl.when((at >= 0) & doubled)
-        def _():
-            base[tile] = 2.0 * rows[at]
-
-        return 0
-
-    lax.fori_loop(0, OT, own, 0)
-
-
-def split_rows(right, right_panel, own=None):
+        lax.fori_loop(0, NNZ, block, 0)
+
+    @pl.when(use)
+    def _():
+        def own(i, _):
+            item = meta[TLIST + i]
+            tile, at = item >> 8, (item & 255) - 1
+            for row, ref in enumerate(left):
+
+                @pl.when((at >= row * NNZ) & (at < (row + 1) * NNZ))
+                def _(row=row, ref=ref):
+                    base[tile] = 2.0 * ref[0, at - row * NNZ]
+
+            return 0
+
+        lax.fori_loop(0, OT, own, 0)
+
+
+def split_rows(right, right_panel):
     first = 0
-    if own is not None:
-        source, rows, sem = own
-        copy = pltpu.make_async_copy(source.at[0], rows, sem)
-        copy.start()
     for ref in right:
         split_row(ref.at[0], first, ref.shape[1], right_panel)
         first += ref.shape[1]
-    if own is not None:
-        copy.wait()
-        split_row(rows, first, NNZ, right_panel)
+    return first
 
 
 def split_row(blocks, first, size, right_panel):
@@ -205,9 +195,9 @@
     first = GROUPS[group][0] * NNZ
     sign = jnp.where(meta[FLAG] == 1, -1.0, 1.0)
 
-    def pairs(step, _):
-        for k in range(UNROLL):
-            item = meta[step * UNROLL + k]
+    def some(at, count):
+        for k in range(count):
+            item = meta[at + k]
             tile = item >> 16
             l_at = (item >> 8) & 255
             r_at = jnp.maximum((item & 255) - first, 0)
@@ -219,26 +209,67 @@
                 preferred_element_type=jnp.float32,
             )
             acc[tile] = acc[tile] + sign * (both[:, :BS] + both[:, BS:])
-        return 0
-
-    lax.fori_loop(meta[POFF + group], meta[POFF + group + 1], pairs, 0)
+
+    start, end = meta[POFF + group], meta[POFF + group + 1]
+
+    def pairs(step, _):
+        some((start + 2 * step) * UNROLL, 2 * UNROLL)
+        return 0
+
+    lax.fori_loop(0, (end - start) // 2, pairs, 0)
+
+    @pl.when((end - start) % 2 == 1)
+    def _():
+        some((end - 1) * UNROLL, UNROLL)
+
+
+def tile_copy(meta, source, out, sems, i):
+    tile = meta[TLIST + i] >> 8
+    return pltpu.make_async_copy(source.at[tile], out.at[tile], sems.at[tile])
+
+
+def send_tiles(meta, source, out, sems, first, last):
+    def leave(i, _):
+        tile_copy(meta, source, out, sems, i).start()
+        return 0
+
+    lax.fori_loop(first, last, leave, 0)
+
+
+def wait_tiles(meta, source, out, sems, first, last):
+    def drain(i, _):
+        tile_copy(meta, source, out, sems, i).wait()
+        return 0
+
+    lax.fori_loop(first, last, drain, 0)
 
 
 def kernel(group, n_right, meta, panel, base, *refs):
-    own = None
+    if group == len(GROUPS) - 2:
+        total, token, out, right_panel, sems = refs[-5:]
+        done = meta[TOFF + group]
+        send_tiles(meta, total, out, sems, 0, done)
+    else:
+        total, token, right_panel = refs[-3:]
+    token[...] = jnp.zeros_like(token)
+    first = split_rows(refs[:n_right], right_panel)
     if group == 0:
-        own, refs = (refs[n_right], *refs[-2:]), refs[:-2]
-    total, token, right_panel = refs[-3:]
-    token[...] = jnp.zeros_like(token)
-    split_rows(refs[:n_right], right_panel, own)
+
+        def own(at, _):
+            right_panel[first + at, :BS] = panel[at, :, :BS]
+            right_panel[first + at, BS:] = panel[at, :, BS:]
+            return 0
+
+        lax.fori_loop(0, NNZ, own, 0)
     add_pairs(group, meta, panel, right_panel, total)
+    if group == len(GROUPS) - 2:
+        wait_tiles(meta, total, out, sems, 0, done)
 
 
 def last_kernel(group, n_right, meta, panel, base, *refs):
-    out, right_panel, acc, out_sems, all_sem = refs[-5:]
-    whole = pltpu.make_async_copy(base.at[pl.ds(0, OT)], out, all_sem)
-    whole.start()
-    t0, t1 = meta[TOFF + group], meta[TOFF + group + 1]
+    out, right_panel, acc, sems = refs[-4:]
+    before, t0, t1 = meta[TOFF + group - 1], meta[TOFF + group], meta[TOFF + group + 1]
+    send_tiles(meta, base, out, sems, before, t0)
 
     def begin(i, _):
         tile = meta[TLIST + i] >> 8
@@ -249,22 +280,16 @@
     acc[OT] = jnp.zeros((BS, BS), jnp.float32)
     split_rows(refs[:n_right], right_panel)
     add_pairs(group, meta, panel, right_panel, acc)
-    whole.wait()
-
-    def out_copy(i):
-        tile = meta[TLIST + i] >> 8
-        return pltpu.make_async_copy(acc.at[tile], out.at[tile], out_sems.at[tile])
-
-    def leave(i, _):
-        out_copy(i).start()
-        return 0
-
-    def drain(i, _):
-        out_copy(i).wait()
-        return 0
-
-    lax.fori_loop(t0, t1, leave, 0)
-    lax.fori_loop(t0, t1, drain, 0)
+    send_tiles(meta, acc, out, sems, t0, t1)
+    wait_tiles(meta, base, out, sems, before, t0)
+    wait_tiles(meta, acc, out, sems, t0, t1)
+
+
+VMEM_SPEC = pl.BlockSpec(memory_space=pltpu.VMEM)
+SMEM_SPEC = pl.BlockSpec(memory_space=pltpu.SMEM)
+TOTAL = pltpu.VMEM((OT + 1, BS, BS), jnp.float32)
+TOKEN = jax.ShapeDtypeStruct((8, BS), jnp.float32)
+ANY_SPEC = pl.BlockSpec(memory_space=pl.ANY)
 
 
 VMEM_SPEC = pl.BlockSpec(memory_space=pltpu.VMEM)
@@ -286,43 +311,39 @@
             TOTAL,
             TOKEN,
         ],
-        in_specs=[SMEM_SPEC] + [ANY_SPEC] * len(left),
+        in_specs=[SMEM_SPEC] + [VMEM_SPEC] * len(left),
         out_specs=[VMEM_SPEC, VMEM_SPEC, VMEM_SPEC],
-        scratch_shapes=[
-            pltpu.VMEM((len(left) * NNZ, BS, BS), jnp.float32),
-            pltpu.SemaphoreType.DMA((len(left),)),
-        ],
         cost_estimate=pl.CostEstimate(
             flops=5 << 20, bytes_accessed=12 << 20, transcendentals=0
         ),
-        compiler_params=pltpu.CompilerParams(vmem_limit_bytes=16 << 20),
+        compiler_params=pltpu.CompilerParams(vmem_limit_bytes=8 << 20),
         name="left_panel",
-    )(meta, *[in_hbm(block) for block in left])
-
-
-def run_group(group, meta, panel, base, right, order, own=None):
-    last = group == len(GROUPS) - 1
-    blocks = sum(block.shape[1] for block in right)
-    extra = [order] if own is None else [in_hbm(own), order]
+    )(meta, *left)
+
+
+def run_group(group, meta, panel, base, right, order):
+    last, begun = group == len(GROUPS) - 1, group == len(GROUPS) - 2
+    whole = jax.ShapeDtypeStruct((OT, BS, BS), jnp.float32)
     scratch = [pltpu.VMEM((len(GROUPS[group]) * NNZ, 2 * BS, BS), jnp.bfloat16)]
     if last:
         scratch += [pltpu.VMEM((OT + 1, BS, BS), jnp.float32)]
-        scratch += [pltpu.SemaphoreType.DMA((OT,)), pltpu.SemaphoreType.DMA]
-    if own is not None:
-        scratch += [pltpu.VMEM((NNZ, BS, BS), jnp.float32), pltpu.SemaphoreType.DMA]
+    if last or begun:
+        scratch += [pltpu.SemaphoreType.DMA((OT,))]
     return pl.pallas_call(
         functools.partial(last_kernel if last else kernel, group, len(right)),
-        out_shape=jax.ShapeDtypeStruct((OT, BS, BS), jnp.float32) if last else [TOTAL, TOKEN],
-        in_specs=[SMEM_SPEC] + [VMEM_SPEC] * (len(right) + 2) + [ANY_SPEC] * len(extra),
-        out_specs=ANY_SPEC if last else [VMEM_SPEC, VMEM_SPEC],
+        out_shape=whole if last else [TOTAL, TOKEN] + [whole] * begun,
+        in_specs=[SMEM_SPEC] + [VMEM_SPEC] * (len(right) + 2) + [ANY_SPEC],
+        out_specs=ANY_SPEC if last else [VMEM_SPEC, VMEM_SPEC] + [ANY_SPEC] * begun,
         scratch_shapes=scratch,
-        input_output_aliases={} if last else {2: 0},
+        input_output_aliases={len(right) + 3: 0} if last else {2: 0},
         cost_estimate=pl.CostEstimate(
-            flops=blocks * 16 * BS**3, bytes_accessed=4 << 20, transcendentals=0
+            flops=len(GROUPS[group]) * NNZ * 16 * BS**3,
+            bytes_accessed=4 << 20,
+            transcendentals=0,
         ),
-        compiler_params=pltpu.CompilerParams(vmem_limit_bytes=16 << 20),
+        compiler_params=pltpu.CompilerParams(vmem_limit_bytes=8 << 20),
         name=f"pairs_{group}",
-    )(meta, panel, base, *right, *extra)
+    )(meta, panel, base, *right, order)
 
 
 def shards(p_vals, p_cols, perm, out_pattern, branch_flag):
@@ -332,7 +353,7 @@
 
     one1 = ring(p_vals, 1)
     partner = swap_cores(p_vals)
-    other1 = ring(after(p_vals, ids), -1)
+    other1 = ring(after(p_vals, meta), -1)
     near = next_chip(after(p_vals, partner))
     near_partner = next_chip(partner)
     one2 = ring(one1, 1)
@@ -345,20 +366,28 @@
     one3_low = ring(one2_low, 1)
     other3_high = ring(other2_high, -1)
     one3_high = ring(after(one2_high, other2), 1)
-    other3_low = ring(other2_low, -1)
+    other3_low = ring(after(other2_low, near_partner_swapped), -1)
     panel, base, token = run_prepare(
         meta,
-        [p_vals, partner, near, near_partner, far_partner, near_swapped, near_partner_swapped],
+        [
+            p_vals,
+            partner,
+            near,
+            near_partner,
+            far_partner,
+            near_swapped,
+            near_partner_swapped,
+        ],
     )
     before4, token = hold(one3_low, token)
     one4_low = ring(before4, 1)
     other4_high = ring(other3_high, -1)
-    total, token = run_group(0, meta, panel, base, [one1, other1], token, p_vals)
+    total, token = run_group(0, meta, panel, base, [one1, other1], token)
     total, token = run_group(1, meta, panel, total, [one2, other2], token)
-    total, token = run_group(
+    total, _, out = run_group(
         2, meta, panel, total, [one3_low, one3_high, other3_low, other3_high], token
     )
-    out = run_group(3, meta, panel, total, [one4_low, other4_high], token)
+    out = run_group(3, meta, panel, total, [one4_low, other4_high], out)
     return out.reshape((1, 1) + out.shape)
 
 

time: 74.3 us -> 73 us (0.983)
  the two profiles are of different devices: /device:TPU:145 before, /device:TPU:1 now
where the time goes in v4:
time: 73 us; the launch traced here: 71.6 us
  starting transfers between devices  30.2 us (41%)
  waiting for transfers between devices  23.1 us (32%)
  Pallas kernels  11.4 us (16%)
  other arithmetic  4.19 us (6%)
  local copies, waits for them, and re-layouts  1.03 us (1%)
  between operations  1.03 us (1%)
    ppermute x10, starting transfers between devices, ring(): return lax.ppermute(block, ('row', 'col'), route)  15.8 us
    ppermute x10, waiting for transfers between devices, ring(): return lax.ppermute(block, ('row', 'col'), route)  13.4 us
    ppermute x3, waiting for transfers between devices, next_chip(): lax.ppermute(block, 'col', [(i, (i + (-2 if i % 2 else 2)) % n) for i in...  9.67 us
    ppermute x3, starting transfers between devices, next_chip(): lax.ppermute(block, 'col', [(i, (i + (-2 if i % 2 else 2)) % n) for i in...  9.53 us
    pallas_call x4, Pallas kernels, run_group(): pl.pallas_call(functools.partial(last_kernel if last else kernel, group,...  9.48 us
    ppermute x3, starting transfers between devices, swap_cores(): return lax.ppermute(block, 'col', [(i, i ^ 1) for i in range(n)])  4.89 us
    pallas_call x1, Pallas kernels, run_prepare(): pl.pallas_call(functools.partial(prepare, len(left)), out_shape=[pltpu.VM...  1.94 us
  transfers between devices with their start and end apart: 16, of which 5 were waited for; matrix products, arithmetic and copies ran while one was open for 8% of the time, Pallas kernels for 13%

profile of v4, /device:TPU:1, one launch (start us, length us, event | category | flops | bytes accessed | tf_op | source)
XLA Modules:
  0.0 71.6 jit_solution(17743215953040056873)
XLA Ops:
  0.0 3.2 %collective-permute-start = (f32[1,12,128,128]{3,2,1,0:T(8,128)}, f32[1,12,128,128]{3,2,1,0:T(8,128)S(1)}, u32[]{:S(2)}, u32[]{:S(2)}) collective-permute-start(f32[1,12,128,128]{3,2,1,0:T(8,128)} %refs_0_.1), channel_id=1, source_target_pairs={{0,1},{1,0},{2,3},{3,2},{4,5},{5,4},{6,7},{7,6},{8,9},{9,8},{10,11... | collective-permute-start | bytes 2359304 | tf_op jit(solution)/shard_map/ppermute | solution.py:32
  3.2 3.8 %collective-permute-start.4 = (f32[1,12,128,128]{3,2,1,0:T(8,128)}, f32[1,12,128,128]{3,2,1,0:T(8,128)S(1)}, u32[]{:S(2)}, u32[]{:S(2)}) collective-permute-start(f32[1,12,128,128]{3,2,1,0:T(8,128)} %refs_0_.1), channel_id=1, source_target_pairs={{0,32},{1,225},{2,34},{3,227},{4,36},{5,229},{6,38},{7,231},{8,40}... | collective-permute-start | bytes 2359304 | tf_op jit(solution)/shard_map/ppermute | solution.py:47
  7.1 0.7 fusion.21
  7.8 0.7 fusion.19
  8.4 0.1 pad_add_fusion
  8.5 0.2 fusion.1
  8.7 0.9 %select_reduce_fusion.1 = s32[15]{0:T(128)S(1)} fusion(s32[256]{0:T(256)} %param.12, s32[15]{0:T(128)S(1)} %pad_add_fusion), kind=kLoop, calls=%fused_computation.6 | loop fusion | flops 11505 | bytes 1144 | tf_op jit(solution)/shard_map/reduce_sum | solution.py:71
  9.6 0.1 slice.35
  9.6 0.8 %slice_bitcast_fusion.1 = (s32[24]{0:T(128)S(1)}, s32[24]{0:T(128)S(1)}) fusion(s32[24,2]{0,1:T(2,128)} %bitcast.10), kind=kLoop, calls=%fused_computation.70 | loop fusion | bytes 384 | tf_op jit(solution)/shard_map/eq | solution.py:74
  10.4 0.2 fusion.4
  10.6 0.2 fusion.6
  10.9 0.1 fusion.8
  11.0 0.7 %fusion.9 = (s32[24]{0:T(128)S(1)}, s32[24]{0:T(128)S(1)}) fusion(s32[8]{0:T(128)} %constant.100.clone, s32[24]{0:T(128)S(1)} %get-tuple-element.50, s32[8]{0:T(128)S(1)} %slice.35), kind=kLoop, calls=%fused_computation.30 | loop fusion | flops 912 | bytes 352 | tf_op jit(solution)/shard_map/reduce_sum | solution.py:83
  11.8 0.2 convert_reduce_fusion.1
  11.9 0.1 select_reduce_fusion.7
  12.1 0.1 select_reduce_fusion.6
  12.2 0.1 convert_reduce_fusion.3
  12.4 0.1 convert_reduce_fusion
  12.5 0.2 select_reduce_fusion
  12.7 0.1 select_reduce_fusion.2
  13.5 0.1 concatenate.7.meta
  13.5 0.0 collective-permute-start.7
  13.6 5.0 %collective-permute-start.2 = (f32[1,12,128,128]{3,2,1,0:T(8,128)S(1)}, f32[1,12,128,128]{3,2,1,0:T(8,128)S(1)}, u32[]{:S(2)}, u32[]{:S(2)}) collective-permute-start(f32[1,12,128,128]{3,2,1,0:T(8,128)S(1)} %collective-permute-done.refs_1_), channel_id=1, source_target_pairs={{0,2},{1,31},{2,4},{3,1},{4,6},{5,3},{6,8},{7,5},{8,10},{9,7},{10,... | collective-permute-start | bytes 2359304 | tf_op jit(solution)/shard_map/ppermute | solution.py:37
  18.6 0.5 collective-permute-start.1
  19.1 0.0 collective-permute-done.4.refs_0_
  19.1 2.6 %collective-permute-start.8 = (f32[1,12,128,128]{3,2,1,0:T(8,128)S(1)}, f32[1,12,128,128]{3,2,1,0:T(8,128)S(1)}, u32[]{:S(2)}, u32[]{:S(2)}) collective-permute-start(f32[1,12,128,128]{3,2,1,0:T(8,128)S(1)} %collective-permute-done.4.refs_0_), channel_id=1, source_target_pairs={{0,32},{1,225},{2,34},{3,227},{4,36},{5,229},{6,38},{7,231},{8,40}... | collective-permute-start | bytes 2359304 | tf_op jit(solution)/shard_map/ppermute | solution.py:47
  21.7 8.0 %collective-permute-done.7.refs_1_ = f32[1,12,128,128]{3,2,1,0:T(8,128)S(1)} collective-permute-done((f32[1,12,128,128]{3,2,1,0:T(8,128)}, f32[1,12,128,128]{3,2,1,0:T(8,128)S(1)}, u32[]{:S(2)}, u32[]{:S(2)}) %collective-permute-start.7) | collective-permute-done | bytes 786464 | tf_op jit(solution)/shard_map/ppermute | solution.py:47
  29.7 6.4 %collective-permute-done.1.refs_2_ = f32[1,12,128,128]{3,2,1,0:T(8,128)S(1)} collective-permute-done((f32[1,12,128,128]{3,2,1,0:T(8,128)}, f32[1,12,128,128]{3,2,1,0:T(8,128)S(1)}, u32[]{:S(2)}, u32[]{:S(2)}) %collective-permute-start.1) | collective-permute-done | bytes 786464 | tf_op jit(solution)/shard_map/ppermute | solution.py:37
  36.1 1.6 %collective-permute-start.5 = (f32[1,12,128,128]{3,2,1,0:T(8,128)S(1)}, f32[1,12,128,128]{3,2,1,0:T(8,128)S(1)}, u32[]{:S(2)}, u32[]{:S(2)}) collective-permute-start(f32[1,12,128,128]{3,2,1,0:T(8,128)S(1)} %collective-permute-done.1.refs_2_), channel_id=1, source_target_pairs={{0,1},{1,0},{2,3},{3,2},{4,5},{5,4},{6,7},{7,6},{8,9},{9,8},{10,11... | collective-permute-start | bytes 2359304 | tf_op jit(solution)/shard_map/ppermute | solution.py:32
  37.7 0.0 collective-permute-start.6
  37.7 4.0 %collective-permute-start.3 = (f32[1,12,128,128]{3,2,1,0:T(8,128)S(1)}, f32[1,12,128,128]{3,2,1,0:T(8,128)S(1)}, u32[]{:S(2)}, u32[]{:S(2)}) collective-permute-start(f32[1,12,128,128]{3,2,1,0:T(8,128)S(1)} %collective-permute-done.2.refs_3_), channel_id=1, source_target_pairs={{0,2},{1,31},{2,4},{3,1},{4,6},{5,3},{6,8},{7,5},{8,10},{9,7},{10,... | collective-permute-start | bytes 2359304 | tf_op jit(solution)/shard_map/ppermute | solution.py:37
  41.7 0.1 fusion.25
  41.8 2.7 %collective-permute-start.9 = (f32[1,6,128,128]{3,2,1,0:T(8,128)S(1)}, f32[1,6,128,128]{3,2,1,0:T(8,128)S(1)}, u32[]{:S(2)}, u32[]{:S(2)}) collective-permute-start(f32[1,6,128,128]{3,2,1,0:T(8,128)S(1)} %get-tuple-element.48), channel_id=1, source_target_pairs={{0,32},{1,225},{2,34},{3,227},{4,36},{5,229},{6,38},{7,231},{8,40}... | collective-permute-start | bytes 1179656 | tf_op jit(solution)/shard_map/ppermute | solution.py:47
  44.4 0.1 fusion.24
  44.5 0.1 collective-permute-start.13
  44.6 0.1 collective-permute-start.12
  44.7 2.7 %collective-permute-start.11 = (f32[1,6,128,128]{3,2,1,0:T(8,128)S(1)}, f32[1,6,128,128]{3,2,1,0:T(8,128)S(1)}, u32[]{:S(2)}, u32[]{:S(2)}) collective-permute-start(f32[1,6,128,128]{3,2,1,0:T(8,128)S(1)} %get-tuple-element.33), channel_id=1, source_target_pairs={{0,32},{1,225},{2,34},{3,227},{4,36},{5,229},{6,38},{7,231},{8,40}... | collective-permute-start | bytes 1179656 | tf_op jit(solution)/shard_map/ppermute | solution.py:47
  47.3 3.3 %collective-permute-done.3.refs_4_ = f32[1,12,128,128]{3,2,1,0:T(8,128)S(1)} collective-permute-done((f32[1,12,128,128]{3,2,1,0:T(8,128)S(1)}, f32[1,12,128,128]{3,2,1,0:T(8,128)S(1)}, u32[]{:S(2)}, u32[]{:S(2)}) %collective-permute-start.3) | collective-permute-done | bytes 786464 | tf_op jit(solution)/shard_map/ppermute | solution.py:37
  50.6 1.9 %left_panel.1 = (bf16[84,128,256]{2,1,0:T(8,128)(2,1)S(1)}, f32[25,128,128]{2,1,0:T(8,128)S(1)}, f32[8,128]{1,0:T(8,128)S(1)}) custom-call(s32[384]{0:T(512)S(1)} %concatenate.7.meta, f32[1,12,128,128]{3,2,1,0:T(8,128)S(1)} %copy-done.1, f32[1,12,128,128]{3,2,1,0:T(8,128)S(1)} %collective-permute-done.refs_1_, ...), custom_call_target="tpu_custom_call" | custom-call | flops 5242880 | bytes 12582912 | tf_op jit(solution)/shard_map/left_panel/pallas_call | solution.py:307
  52.6 3.9 %collective-permute-start.14 = (f32[1,6,128,128]{3,2,1,0:T(8,128)S(1)}, f32[1,6,128,128]{3,2,1,0:T(8,128)S(1)}, u32[]{:S(2)}, u32[]{:S(2)}) collective-permute-start(f32[1,6,128,128]{3,2,1,0:T(8,128)S(1)} %collective-permute-done.9.refs_0_), channel_id=1, source_target_pairs={{0,32},{1,225},{2,34},{3,227},{4,36},{5,229},{6,38},{7,231},{8,40}... | collective-permute-start | bytes 1179656 | tf_op jit(solution)/shard_map/ppermute | solution.py:47
  56.5 0.0 collective-permute-start.15
  56.5 3.0 %pairs_0.1 = (f32[25,128,128]{2,1,0:T(8,128)S(1)}, f32[8,128]{1,0:T(8,128)S(1)}) custom-call(s32[384]{0:T(512)S(1)} %concatenate.7.meta, bf16[84,128,256]{2,1,0:T(8,128)(2,1)S(1)} %get-tuple-element.24.panel, f32[25,128,128]{2,1,0:T(8,128)S(1)} %get-tuple-element.25.base, ...), custom_call_target="tpu_custom_call", output_to_operand_aliasing={{0}: (2, {})} | custom-call | flops 1207959552 | bytes 4194304 | tf_op jit(solution)/shard_map/pairs_0/pallas_call | solution.py:332
  59.5 1.8 %pairs_1.1 = (f32[25,128,128]{2,1,0:T(8,128)S(1)}, f32[8,128]{1,0:T(8,128)S(1)}) custom-call(s32[384]{0:T(512)S(1)} %concatenate.7.meta, bf16[84,128,256]{2,1,0:T(8,128)(2,1)S(1)} %get-tuple-element.24.panel, f32[25,128,128]{2,1,0:T(8,128)S(1)} %get-tuple-element.29.base, ...), custom_call_target="tpu_custom_call", output_to_operand_aliasing={{0}: (2, {})} | custom-call | flops 805306368 | bytes 4194304 | tf_op jit(solution)/shard_map/pairs_1/pallas_call | solution.py:332
  61.4 0.8 %collective-permute-done.12.refs_2_ = f32[1,6,128,128]{3,2,1,0:T(8,128)S(1)} collective-permute-done((f32[1,6,128,128]{3,2,1,0:T(8,128)S(1)}, f32[1,6,128,128]{3,2,1,0:T(8,128)S(1)}, u32[]{:S(2)}, u32[]{:S(2)}) %collective-permute-start.12) | collective-permute-done | bytes 393248 | tf_op jit(solution)/shard_map/ppermute | solution.py:47
  62.2 2.5 %pairs_2.1 = (f32[25,128,128]{2,1,0:T(8,128)S(1)}, f32[8,128]{1,0:T(8,128)}, f32[24,128,128]{2,1,0:T(8,128)}) custom-call(s32[384]{0:T(512)S(1)} %concatenate.7.meta, bf16[84,128,256]{2,1,0:T(8,128)(2,1)S(1)} %get-tuple-element.24.panel, f32[25,128,128]{2,1,0:T(8,128)S(1)} %get-tuple-element.32.base, ...), custom_call_target="tpu_custom_call", output_to_operand_aliasing={{0}: (2, {})} | custom-call | flops 805306368 | bytes 4194304 | tf_op jit(solution)/shard_map/pairs_2/pallas_call | solution.py:332
  64.7 4.5 %collective-permute-done.14.refs_0_ = f32[1,6,128,128]{3,2,1,0:T(8,128)S(1)} collective-permute-done((f32[1,6,128,128]{3,2,1,0:T(8,128)S(1)}, f32[1,6,128,128]{3,2,1,0:T(8,128)S(1)}, u32[]{:S(2)}, u32[]{:S(2)}) %collective-permute-start.14) | collective-permute-done | bytes 393248 | tf_op jit(solution)/shard_map/ppermute | solution.py:47
  69.2 0.0 collective-permute-done.15.refs_1_
  69.2 2.1 %pairs_3.1 = f32[24,128,128]{2,1,0:T(8,128)} custom-call(s32[384]{0:T(512)S(1)} %concatenate.7.meta, bf16[84,128,256]{2,1,0:T(8,128)(2,1)S(1)} %get-tuple-element.24.panel, f32[25,128,128]{2,1,0:T(8,128)S(1)} %get-tuple-element.36.base, f32[1,6,128,128]{3,2,1,0:T(8,128)S(1)} %collective-permute-done.14.refs_0_, ...), custom_call_target="tpu_custom_call", output_to_operand_aliasing={{}: (5, {})} | custom-call | flops 402653184 | bytes 4194304 | tf_op jit(solution)/shard_map/pairs_3/pallas_call | solution.py:332
  (27 shorter events, 0.2 us)
Async XLA Ops:
  0.0 8.5 %copy-start = (s32[256,12]{0,1:T(8,128)S(1)}, s32[256,12]{0,1:T(8,128)}, u32[]{:S(2)}) copy-start(s32[256,12]{0,1:T(8,128)} %param.11) | copy-start | bytes 36868
  0.0 13.6 %collective-permute-start = (f32[1,12,128,128]{3,2,1,0:T(8,128)}, f32[1,12,128,128]{3,2,1,0:T(8,128)S(1)}, u32[]{:S(2)}, u32[]{:S(2)}) collective-permute-start(f32[1,12,128,128]{3,2,1,0:T(8,128)} %refs_0_.1), channel_id=1, source_target_pairs={{0,1},{1,0},{2,3},{3,2},{4,5},{5,4},{6,7},{7,6},{8,9},{9,8},{10,11... | collective-permute-start | bytes 2359304 | tf_op jit(solution)/shard_map/ppermute | solution.py:32
  3.2 15.9 %collective-permute-start.4 = (f32[1,12,128,128]{3,2,1,0:T(8,128)}, f32[1,12,128,128]{3,2,1,0:T(8,128)S(1)}, u32[]{:S(2)}, u32[]{:S(2)}) collective-permute-start(f32[1,12,128,128]{3,2,1,0:T(8,128)} %refs_0_.1), channel_id=1, source_target_pairs={{0,32},{1,225},{2,34},{3,227},{4,36},{5,229},{6,38},{7,231},{8,40}... | collective-permute-start | bytes 2359304 | tf_op jit(solution)/shard_map/ppermute | solution.py:47
  12.1 38.6 %copy-start.1 = (f32[1,12,128,128]{3,2,1,0:T(8,128)S(1)}, f32[1,12,128,128]{3,2,1,0:T(8,128)}, u32[]{:S(2)}) copy-start(f32[1,12,128,128]{3,2,1,0:T(8,128)} %refs_0_.1) | copy-start | bytes 2359300
  13.5 16.1 %collective-permute-start.7 = (f32[1,12,128,128]{3,2,1,0:T(8,128)}, f32[1,12,128,128]{3,2,1,0:T(8,128)S(1)}, u32[]{:S(2)}, u32[]{:S(2)}) collective-permute-start(f32[1,12,128,128]{3,2,1,0:T(8,128)} %refs_0_.1), channel_id=1, source_target_pairs={{0,224},{1,33},{2,226},{3,35},{4,228},{5,37},{6,230},{7,39},{8,232... | collective-permute-start | bytes 2359304 | tf_op jit(solution)/shard_map/ppermute | solution.py:47
  13.6 16.1 %collective-permute-start.2 = (f32[1,12,128,128]{3,2,1,0:T(8,128)S(1)}, f32[1,12,128,128]{3,2,1,0:T(8,128)S(1)}, u32[]{:S(2)}, u32[]{:S(2)}) collective-permute-start(f32[1,12,128,128]{3,2,1,0:T(8,128)S(1)} %collective-permute-done.refs_1_), channel_id=1, source_target_pairs={{0,2},{1,31},{2,4},{3,1},{4,6},{5,3},{6,8},{7,5},{8,10},{9,7},{10,... | collective-permute-start | bytes 2359304 | tf_op jit(solution)/shard_map/ppermute | solution.py:37
  18.6 17.5 %collective-permute-start.1 = (f32[1,12,128,128]{3,2,1,0:T(8,128)}, f32[1,12,128,128]{3,2,1,0:T(8,128)S(1)}, u32[]{:S(2)}, u32[]{:S(2)}) collective-permute-start(f32[1,12,128,128]{3,2,1,0:T(8,128)} %refs_0_.1), channel_id=1, source_target_pairs={{0,2},{1,31},{2,4},{3,1},{4,6},{5,3},{6,8},{7,5},{8,10},{9,7},{10,... | collective-permute-start | bytes 2359304 | tf_op jit(solution)/shard_map/ppermute | solution.py:37
  19.1 22.5 %collective-permute-start.8 = (f32[1,12,128,128]{3,2,1,0:T(8,128)S(1)}, f32[1,12,128,128]{3,2,1,0:T(8,128)S(1)}, u32[]{:S(2)}, u32[]{:S(2)}) collective-permute-start(f32[1,12,128,128]{3,2,1,0:T(8,128)S(1)} %collective-permute-done.4.refs_0_), channel_id=1, source_target_pairs={{0,32},{1,225},{2,34},{3,227},{4,36},{5,229},{6,38},{7,231},{8,40}... | collective-permute-start | bytes 2359304 | tf_op jit(solution)/shard_map/ppermute | solution.py:47
  29.7 14.7 %collective-permute-start.10 = (f32[1,12,128,128]{3,2,1,0:T(8,128)S(1)}, f32[1,12,128,128]{3,2,1,0:T(8,128)S(1)}, u32[]{:S(2)}, u32[]{:S(2)}) collective-permute-start(f32[1,12,128,128]{3,2,1,0:T(8,128)S(1)} %collective-permute-done.7.refs_1_), channel_id=1, source_target_pairs={{0,224},{1,33},{2,226},{3,35},{4,228},{5,37},{6,230},{7,39},{8,232... | collective-permute-start | bytes 2359304 | tf_op jit(solution)/shard_map/ppermute | solution.py:47
  36.1 8.6 %collective-permute-start.5 = (f32[1,12,128,128]{3,2,1,0:T(8,128)S(1)}, f32[1,12,128,128]{3,2,1,0:T(8,128)S(1)}, u32[]{:S(2)}, u32[]{:S(2)}) collective-permute-start(f32[1,12,128,128]{3,2,1,0:T(8,128)S(1)} %collective-permute-done.1.refs_2_), channel_id=1, source_target_pairs={{0,1},{1,0},{2,3},{3,2},{4,5},{5,4},{6,7},{7,6},{8,9},{9,8},{10,11... | collective-permute-start | bytes 2359304 | tf_op jit(solution)/shard_map/ppermute | solution.py:32
  37.7 6.9 %collective-permute-start.6 = (f32[1,12,128,128]{3,2,1,0:T(8,128)S(1)}, f32[1,12,128,128]{3,2,1,0:T(8,128)S(1)}, u32[]{:S(2)}, u32[]{:S(2)}) collective-permute-start(f32[1,12,128,128]{3,2,1,0:T(8,128)S(1)} %collective-permute-done.2.refs_3_), channel_id=1, source_target_pairs={{0,1},{1,0},{2,3},{3,2},{4,5},{5,4},{6,7},{7,6},{8,9},{9,8},{10,11... | collective-permute-start | bytes 2359304 | tf_op jit(solution)/shard_map/ppermute | solution.py:32
  37.7 12.9 %collective-permute-start.3 = (f32[1,12,128,128]{3,2,1,0:T(8,128)S(1)}, f32[1,12,128,128]{3,2,1,0:T(8,128)S(1)}, u32[]{:S(2)}, u32[]{:S(2)}) collective-permute-start(f32[1,12,128,128]{3,2,1,0:T(8,128)S(1)} %collective-permute-done.2.refs_3_), channel_id=1, source_target_pairs={{0,2},{1,31},{2,4},{3,1},{4,6},{5,3},{6,8},{7,5},{8,10},{9,7},{10,... | collective-permute-start | bytes 2359304 | tf_op jit(solution)/shard_map/ppermute | solution.py:37
  41.8 10.8 %collective-permute-start.9 = (f32[1,6,128,128]{3,2,1,0:T(8,128)S(1)}, f32[1,6,128,128]{3,2,1,0:T(8,128)S(1)}, u32[]{:S(2)}, u32[]{:S(2)}) collective-permute-start(f32[1,6,128,128]{3,2,1,0:T(8,128)S(1)} %get-tuple-element.48), channel_id=1, source_target_pairs={{0,32},{1,225},{2,34},{3,227},{4,36},{5,229},{6,38},{7,231},{8,40}... | collective-permute-start | bytes 1179656 | tf_op jit(solution)/shard_map/ppermute | solution.py:47
  44.5 12.0 %collective-permute-start.13 = (f32[1,6,128,128]{3,2,1,0:T(8,128)S(1)}, f32[1,6,128,128]{3,2,1,0:T(8,128)S(1)}, u32[]{:S(2)}, u32[]{:S(2)}) collective-permute-start(f32[1,6,128,128]{3,2,1,0:T(8,128)S(1)} %get-tuple-element.45), channel_id=1, source_target_pairs={{0,224},{1,33},{2,226},{3,35},{4,228},{5,37},{6,230},{7,39},{8,232... | collective-permute-start | bytes 1179656 | tf_op jit(solution)/shard_map/ppermute | solution.py:47
  44.6 17.6 %collective-permute-start.12 = (f32[1,6,128,128]{3,2,1,0:T(8,128)S(1)}, f32[1,6,128,128]{3,2,1,0:T(8,128)S(1)}, u32[]{:S(2)}, u32[]{:S(2)}) collective-permute-start(f32[1,6,128,128]{3,2,1,0:T(8,128)S(1)} %get-tuple-element.34), channel_id=1, source_target_pairs={{0,224},{1,33},{2,226},{3,35},{4,228},{5,37},{6,230},{7,39},{8,232... | collective-permute-start | bytes 1179656 | tf_op jit(solution)/shard_map/ppermute | solution.py:47
  44.7 17.5 %collective-permute-start.11 = (f32[1,6,128,128]{3,2,1,0:T(8,128)S(1)}, f32[1,6,128,128]{3,2,1,0:T(8,128)S(1)}, u32[]{:S(2)}, u32[]{:S(2)}) collective-permute-start(f32[1,6,128,128]{3,2,1,0:T(8,128)S(1)} %get-tuple-element.33), channel_id=1, source_target_pairs={{0,32},{1,225},{2,34},{3,227},{4,36},{5,229},{6,38},{7,231},{8,40}... | collective-permute-start | bytes 1179656 | tf_op jit(solution)/shard_map/ppermute | solution.py:47
  52.6 16.6 %collective-permute-start.14 = (f32[1,6,128,128]{3,2,1,0:T(8,128)S(1)}, f32[1,6,128,128]{3,2,1,0:T(8,128)S(1)}, u32[]{:S(2)}, u32[]{:S(2)}) collective-permute-start(f32[1,6,128,128]{3,2,1,0:T(8,128)S(1)} %collective-permute-done.9.refs_0_), channel_id=1, source_target_pairs={{0,32},{1,225},{2,34},{3,227},{4,36},{5,229},{6,38},{7,231},{8,40}... | collective-permute-start | bytes 1179656 | tf_op jit(solution)/shard_map/ppermute | solution.py:47
  56.5 12.8 %collective-permute-start.15 = (f32[1,6,128,128]{3,2,1,0:T(8,128)S(1)}, f32[1,6,128,128]{3,2,1,0:T(8,128)S(1)}, u32[]{:S(2)}, u32[]{:S(2)}) collective-permute-start(f32[1,6,128,128]{3,2,1,0:T(8,128)S(1)} %collective-permute-done.13.refs_3_), channel_id=1, source_target_pairs={{0,224},{1,33},{2,226},{3,35},{4,228},{5,37},{6,230},{7,39},{8,232... | collective-permute-start | bytes 1179656 | tf_op jit(solution)/shard_map/ppermute | solution.py:47

commit v5 on v4

--- a/solution.py
+++ b/solution.py
@@ -357,7 +357,7 @@
     near = next_chip(after(p_vals, partner))
     near_partner = next_chip(partner)
     one2 = ring(one1, 1)
-    near_swapped = swap_cores(after(near, one1))
+    near_swapped = swap_cores(after(near, one2))
     other2 = ring(after(other1, near_partner, meta), -1)
     far_partner = next_chip(near_partner)
     near_partner_swapped = swap_cores(near_partner)

time: 73 us -> 71.8 us (0.984); the launches traced: 71.6 us -> 71.6 us
  starting transfers between devices: 30.2 us -> 29 us
  Pallas kernels: 11.4 us -> 12.2 us
    pallas_call x1, Pallas kernels: 1.94 us -> 3.17 us  [run_prepare(): pl.pallas_call(functools.partial(prepare, len(left)), out_shape=[pltpu.VM...]
    ppermute x10, starting transfers between devices: 15.8 us -> 14.6 us  [ring(): return lax.ppermute(block, ('row', 'col'), route)]
  transfers between devices with their start and end apart: 16 -> 16, of which waited for: 5 -> 5; matrix products, arithmetic and copies ran while one was open for 8% -> 8% of each run, Pallas kernels for 13% -> 14%
where the time goes in v5:
time: 71.8 us; the launch traced here: 71.6 us
  starting transfers between devices  29 us (40%)
  waiting for transfers between devices  23.6 us (33%)
  Pallas kernels  12.2 us (17%)
  other arithmetic  4.19 us (6%)
  local copies, waits for them, and re-layouts  1.03 us (1%)
  between operations  1.03 us (1%)
    ppermute x10, starting transfers between devices, ring(): return lax.ppermute(block, ('row', 'col'), route)  14.6 us
    ppermute x10, waiting for transfers between devices, ring(): return lax.ppermute(block, ('row', 'col'), route)  13.9 us
    ppermute x3, waiting for transfers between devices, next_chip(): lax.ppermute(block, 'col', [(i, (i + (-2 if i % 2 else 2)) % n) for i in...  9.67 us
    ppermute x3, starting transfers between devices, next_chip(): lax.ppermute(block, 'col', [(i, (i + (-2 if i % 2 else 2)) % n) for i in...  9.53 us
    pallas_call x4, Pallas kernels, run_group(): pl.pallas_call(functools.partial(last_kernel if last else kernel, group,...  8.98 us
    ppermute x3, starting transfers between devices, swap_cores(): return lax.ppermute(block, 'col', [(i, i ^ 1) for i in range(n)])  4.89 us
    pallas_call x1, Pallas kernels, run_prepare(): pl.pallas_call(functools.partial(prepare, len(left)), out_shape=[pltpu.VM...  3.17 us
  transfers between devices with their start and end apart: 16, of which 5 were waited for; matrix products, arithmetic and copies ran while one was open for 8% of the time, Pallas kernels for 14%

profile of v5, /device:TPU:1, one launch (start us, length us, event | category | flops | bytes accessed | tf_op | source)
XLA Modules:
  0.0 71.6 jit_solution(14211943235240876702)
XLA Ops:
  0.0 3.2 %collective-permute-start = (f32[1,12,128,128]{3,2,1,0:T(8,128)}, f32[1,12,128,128]{3,2,1,0:T(8,128)S(1)}, u32[]{:S(2)}, u32[]{:S(2)}) collective-permute-start(f32[1,12,128,128]{3,2,1,0:T(8,128)} %refs_0_.1), channel_id=1, source_target_pairs={{0,1},{1,0},{2,3},{3,2},{4,5},{5,4},{6,7},{7,6},{8,9},{9,8},{10,11... | collective-permute-start | bytes 2359304 | tf_op jit(solution)/shard_map/ppermute | solution.py:32
  3.2 3.8 %collective-permute-start.4 = (f32[1,12,128,128]{3,2,1,0:T(8,128)}, f32[1,12,128,128]{3,2,1,0:T(8,128)S(1)}, u32[]{:S(2)}, u32[]{:S(2)}) collective-permute-start(f32[1,12,128,128]{3,2,1,0:T(8,128)} %refs_0_.1), channel_id=1, source_target_pairs={{0,32},{1,225},{2,34},{3,227},{4,36},{5,229},{6,38},{7,231},{8,40}... | collective-permute-start | bytes 2359304 | tf_op jit(solution)/shard_map/ppermute | solution.py:47
  7.1 0.7 fusion.21
  7.8 0.7 fusion.19
  8.4 0.1 pad_add_fusion
  8.5 0.2 fusion.1
  8.7 0.9 %select_reduce_fusion.1 = s32[15]{0:T(128)S(1)} fusion(s32[256]{0:T(256)} %param.12, s32[15]{0:T(128)S(1)} %pad_add_fusion), kind=kLoop, calls=%fused_computation.6 | loop fusion | flops 11505 | bytes 1144 | tf_op jit(solution)/shard_map/reduce_sum | solution.py:71
  9.6 0.1 slice.35
  9.6 0.8 %slice_bitcast_fusion.1 = (s32[24]{0:T(128)S(1)}, s32[24]{0:T(128)S(1)}) fusion(s32[24,2]{0,1:T(2,128)} %bitcast.10), kind=kLoop, calls=%fused_computation.70 | loop fusion | bytes 384 | tf_op jit(solution)/shard_map/eq | solution.py:74
  10.4 0.2 fusion.4
  10.6 0.2 fusion.6
  10.9 0.1 fusion.8
  11.0 0.7 %fusion.9 = (s32[24]{0:T(128)S(1)}, s32[24]{0:T(128)S(1)}) fusion(s32[8]{0:T(128)} %constant.100.clone, s32[24]{0:T(128)S(1)} %get-tuple-element.50, s32[8]{0:T(128)S(1)} %slice.35), kind=kLoop, calls=%fused_computation.30 | loop fusion | flops 912 | bytes 352 | tf_op jit(solution)/shard_map/reduce_sum | solution.py:83
  11.8 0.2 convert_reduce_fusion.1
  11.9 0.1 select_reduce_fusion.7
  12.1 0.0 copy-start.1
  12.1 0.1 select_reduce_fusion.6
  12.2 0.1 convert_reduce_fusion.3
  12.4 0.1 convert_reduce_fusion
  12.5 0.2 select_reduce_fusion
  12.7 0.1 select_reduce_fusion.2
  13.5 0.1 concatenate.7.meta
  13.5 0.0 collective-permute-start.8
  13.6 5.0 %collective-permute-start.2 = (f32[1,12,128,128]{3,2,1,0:T(8,128)S(1)}, f32[1,12,128,128]{3,2,1,0:T(8,128)S(1)}, u32[]{:S(2)}, u32[]{:S(2)}) collective-permute-start(f32[1,12,128,128]{3,2,1,0:T(8,128)S(1)} %collective-permute-done.refs_1_), channel_id=1, source_target_pairs={{0,2},{1,31},{2,4},{3,1},{4,6},{5,3},{6,8},{7,5},{8,10},{9,7},{10,... | collective-permute-start | bytes 2359304 | tf_op jit(solution)/shard_map/ppermute | solution.py:37
  18.6 0.5 collective-permute-start.1
  19.1 2.6 %collective-permute-start.5 = (f32[1,12,128,128]{3,2,1,0:T(8,128)S(1)}, f32[1,12,128,128]{3,2,1,0:T(8,128)S(1)}, u32[]{:S(2)}, u32[]{:S(2)}) collective-permute-start(f32[1,12,128,128]{3,2,1,0:T(8,128)S(1)} %collective-permute-done.4.refs_0_), channel_id=1, source_target_pairs={{0,32},{1,225},{2,34},{3,227},{4,36},{5,229},{6,38},{7,231},{8,40}... | collective-permute-start | bytes 2359304 | tf_op jit(solution)/shard_map/ppermute | solution.py:47
  21.7 8.0 %collective-permute-done.8.refs_1_ = f32[1,12,128,128]{3,2,1,0:T(8,128)S(1)} collective-permute-done((f32[1,12,128,128]{3,2,1,0:T(8,128)}, f32[1,12,128,128]{3,2,1,0:T(8,128)S(1)}, u32[]{:S(2)}, u32[]{:S(2)}) %collective-permute-start.8) | collective-permute-done | bytes 786464 | tf_op jit(solution)/shard_map/ppermute | solution.py:47
  29.7 6.4 %collective-permute-done.1.refs_2_ = f32[1,12,128,128]{3,2,1,0:T(8,128)S(1)} collective-permute-done((f32[1,12,128,128]{3,2,1,0:T(8,128)}, f32[1,12,128,128]{3,2,1,0:T(8,128)S(1)}, u32[]{:S(2)}, u32[]{:S(2)}) %collective-permute-start.1) | collective-permute-done | bytes 786464 | tf_op jit(solution)/shard_map/ppermute | solution.py:37
  36.1 1.6 %collective-permute-start.6 = (f32[1,12,128,128]{3,2,1,0:T(8,128)S(1)}, f32[1,12,128,128]{3,2,1,0:T(8,128)S(1)}, u32[]{:S(2)}, u32[]{:S(2)}) collective-permute-start(f32[1,12,128,128]{3,2,1,0:T(8,128)S(1)} %collective-permute-done.1.refs_2_), channel_id=1, source_target_pairs={{0,1},{1,0},{2,3},{3,2},{4,5},{5,4},{6,7},{7,6},{8,9},{9,8},{10,11... | collective-permute-start | bytes 2359304 | tf_op jit(solution)/shard_map/ppermute | solution.py:32
  37.7 0.0 collective-permute-start.7
  37.7 4.0 %collective-permute-start.3 = (f32[1,12,128,128]{3,2,1,0:T(8,128)S(1)}, f32[1,12,128,128]{3,2,1,0:T(8,128)S(1)}, u32[]{:S(2)}, u32[]{:S(2)}) collective-permute-start(f32[1,12,128,128]{3,2,1,0:T(8,128)S(1)} %collective-permute-done.2.refs_3_), channel_id=1, source_target_pairs={{0,2},{1,31},{2,4},{3,1},{4,6},{5,3},{6,8},{7,5},{8,10},{9,7},{10,... | collective-permute-start | bytes 2359304 | tf_op jit(solution)/shard_map/ppermute | solution.py:37
  41.7 0.1 fusion.25
  41.8 2.7 %collective-permute-start.9 = (f32[1,6,128,128]{3,2,1,0:T(8,128)S(1)}, f32[1,6,128,128]{3,2,1,0:T(8,128)S(1)}, u32[]{:S(2)}, u32[]{:S(2)}) collective-permute-start(f32[1,6,128,128]{3,2,1,0:T(8,128)S(1)} %get-tuple-element.48), channel_id=1, source_target_pairs={{0,32},{1,225},{2,34},{3,227},{4,36},{5,229},{6,38},{7,231},{8,40}... | collective-permute-start | bytes 1179656 | tf_op jit(solution)/shard_map/ppermute | solution.py:47
  44.4 0.1 fusion.24
  44.5 0.1 collective-permute-start.13
  44.6 0.1 collective-permute-start.12
  44.7 2.7 %collective-permute-start.11 = (f32[1,6,128,128]{3,2,1,0:T(8,128)S(1)}, f32[1,6,128,128]{3,2,1,0:T(8,128)S(1)}, u32[]{:S(2)}, u32[]{:S(2)}) collective-permute-start(f32[1,6,128,128]{3,2,1,0:T(8,128)S(1)} %get-tuple-element.33), channel_id=1, source_target_pairs={{0,32},{1,225},{2,34},{3,227},{4,36},{5,229},{6,38},{7,231},{8,40}... | collective-permute-start | bytes 1179656 | tf_op jit(solution)/shard_map/ppermute | solution.py:47
  47.3 3.3 %collective-permute-done.3.refs_4_ = f32[1,12,128,128]{3,2,1,0:T(8,128)S(1)} collective-permute-done((f32[1,12,128,128]{3,2,1,0:T(8,128)S(1)}, f32[1,12,128,128]{3,2,1,0:T(8,128)S(1)}, u32[]{:S(2)}, u32[]{:S(2)}) %collective-permute-start.3) | collective-permute-done | bytes 786464 | tf_op jit(solution)/shard_map/ppermute | solution.py:37
  50.6 3.2 %left_panel.1 = (bf16[84,128,256]{2,1,0:T(8,128)(2,1)S(1)}, f32[25,128,128]{2,1,0:T(8,128)S(1)}, f32[8,128]{1,0:T(8,128)S(1)}) custom-call(s32[384]{0:T(512)S(1)} %concatenate.7.meta, f32[1,12,128,128]{3,2,1,0:T(8,128)S(1)} %copy-done.1, f32[1,12,128,128]{3,2,1,0:T(8,128)S(1)} %collective-permute-done.refs_1_, ...), custom_call_target="tpu_custom_call" | custom-call | flops 5242880 | bytes 12582912 | tf_op jit(solution)/shard_map/left_panel/pallas_call | solution.py:307
  53.8 2.7 %collective-permute-start.14 = (f32[1,6,128,128]{3,2,1,0:T(8,128)S(1)}, f32[1,6,128,128]{3,2,1,0:T(8,128)S(1)}, u32[]{:S(2)}, u32[]{:S(2)}) collective-permute-start(f32[1,6,128,128]{3,2,1,0:T(8,128)S(1)} %collective-permute-done.9.refs_0_), channel_id=1, source_target_pairs={{0,32},{1,225},{2,34},{3,227},{4,36},{5,229},{6,38},{7,231},{8,40}... | collective-permute-start | bytes 1179656 | tf_op jit(solution)/shard_map/ppermute | solution.py:47
  56.5 0.0 collective-permute-start.15
  56.5 2.5 %pairs_0.1 = (f32[25,128,128]{2,1,0:T(8,128)S(1)}, f32[8,128]{1,0:T(8,128)S(1)}) custom-call(s32[384]{0:T(512)S(1)} %concatenate.7.meta, bf16[84,128,256]{2,1,0:T(8,128)(2,1)S(1)} %get-tuple-element.24.panel, f32[25,128,128]{2,1,0:T(8,128)S(1)} %get-tuple-element.25.base, ...), custom_call_target="tpu_custom_call", output_to_operand_aliasing={{0}: (2, {})} | custom-call | flops 1207959552 | bytes 4194304 | tf_op jit(solution)/shard_map/pairs_0/pallas_call | solution.py:332
  59.0 1.3 %pairs_1.1 = (f32[25,128,128]{2,1,0:T(8,128)S(1)}, f32[8,128]{1,0:T(8,128)S(1)}) custom-call(s32[384]{0:T(512)S(1)} %concatenate.7.meta, bf16[84,128,256]{2,1,0:T(8,128)(2,1)S(1)} %get-tuple-element.24.panel, f32[25,128,128]{2,1,0:T(8,128)S(1)} %get-tuple-element.29.base, ...), custom_call_target="tpu_custom_call", output_to_operand_aliasing={{0}: (2, {})} | custom-call | flops 805306368 | bytes 4194304 | tf_op jit(solution)/shard_map/pairs_1/pallas_call | solution.py:332
  60.4 1.8 %collective-permute-done.12.refs_2_ = f32[1,6,128,128]{3,2,1,0:T(8,128)S(1)} collective-permute-done((f32[1,6,128,128]{3,2,1,0:T(8,128)S(1)}, f32[1,6,128,128]{3,2,1,0:T(8,128)S(1)}, u32[]{:S(2)}, u32[]{:S(2)}) %collective-permute-start.12) | collective-permute-done | bytes 393248 | tf_op jit(solution)/shard_map/ppermute | solution.py:47
  62.2 2.9 %pairs_2.1 = (f32[25,128,128]{2,1,0:T(8,128)S(1)}, f32[8,128]{1,0:T(8,128)}, f32[24,128,128]{2,1,0:T(8,128)}) custom-call(s32[384]{0:T(512)S(1)} %concatenate.7.meta, bf16[84,128,256]{2,1,0:T(8,128)(2,1)S(1)} %get-tuple-element.24.panel, f32[25,128,128]{2,1,0:T(8,128)S(1)} %get-tuple-element.32.base, ...), custom_call_target="tpu_custom_call", output_to_operand_aliasing={{0}: (2, {})} | custom-call | flops 805306368 | bytes 4194304 | tf_op jit(solution)/shard_map/pairs_2/pallas_call | solution.py:332
  65.1 4.1 %collective-permute-done.14.refs_0_ = f32[1,6,128,128]{3,2,1,0:T(8,128)S(1)} collective-permute-done((f32[1,6,128,128]{3,2,1,0:T(8,128)S(1)}, f32[1,6,128,128]{3,2,1,0:T(8,128)S(1)}, u32[]{:S(2)}, u32[]{:S(2)}) %collective-permute-start.14) | collective-permute-done | bytes 393248 | tf_op jit(solution)/shard_map/ppermute | solution.py:47
  69.2 0.0 collective-permute-done.15.refs_1_
  69.2 2.2 %pairs_3.1 = f32[24,128,128]{2,1,0:T(8,128)} custom-call(s32[384]{0:T(512)S(1)} %concatenate.7.meta, bf16[84,128,256]{2,1,0:T(8,128)(2,1)S(1)} %get-tuple-element.24.panel, f32[25,128,128]{2,1,0:T(8,128)S(1)} %get-tuple-element.36.base, f32[1,6,128,128]{3,2,1,0:T(8,128)S(1)} %collective-permute-done.14.refs_0_, ...), custom_call_target="tpu_custom_call", output_to_operand_aliasing={{}: (5, {})} | custom-call | flops 402653184 | bytes 4194304 | tf_op jit(solution)/shard_map/pairs_3/pallas_call | solution.py:332
  (27 shorter events, 0.2 us)
Async XLA Ops:
  0.0 8.5 %copy-start = (s32[256,12]{0,1:T(8,128)S(1)}, s32[256,12]{0,1:T(8,128)}, u32[]{:S(2)}) copy-start(s32[256,12]{0,1:T(8,128)} %param.11) | copy-start | bytes 36868
  0.0 13.6 %collective-permute-start = (f32[1,12,128,128]{3,2,1,0:T(8,128)}, f32[1,12,128,128]{3,2,1,0:T(8,128)S(1)}, u32[]{:S(2)}, u32[]{:S(2)}) collective-permute-start(f32[1,12,128,128]{3,2,1,0:T(8,128)} %refs_0_.1), channel_id=1, source_target_pairs={{0,1},{1,0},{2,3},{3,2},{4,5},{5,4},{6,7},{7,6},{8,9},{9,8},{10,11... | collective-permute-start | bytes 2359304 | tf_op jit(solution)/shard_map/ppermute | solution.py:32
  3.2 15.9 %collective-permute-start.4 = (f32[1,12,128,128]{3,2,1,0:T(8,128)}, f32[1,12,128,128]{3,2,1,0:T(8,128)S(1)}, u32[]{:S(2)}, u32[]{:S(2)}) collective-permute-start(f32[1,12,128,128]{3,2,1,0:T(8,128)} %refs_0_.1), channel_id=1, source_target_pairs={{0,32},{1,225},{2,34},{3,227},{4,36},{5,229},{6,38},{7,231},{8,40}... | collective-permute-start | bytes 2359304 | tf_op jit(solution)/shard_map/ppermute | solution.py:47
  12.1 38.6 %copy-start.1 = (f32[1,12,128,128]{3,2,1,0:T(8,128)S(1)}, f32[1,12,128,128]{3,2,1,0:T(8,128)}, u32[]{:S(2)}) copy-start(f32[1,12,128,128]{3,2,1,0:T(8,128)} %refs_0_.1) | copy-start | bytes 2359300
  13.5 16.1 %collective-permute-start.8 = (f32[1,12,128,128]{3,2,1,0:T(8,128)}, f32[1,12,128,128]{3,2,1,0:T(8,128)S(1)}, u32[]{:S(2)}, u32[]{:S(2)}) collective-permute-start(f32[1,12,128,128]{3,2,1,0:T(8,128)} %refs_0_.1), channel_id=1, source_target_pairs={{0,224},{1,33},{2,226},{3,35},{4,228},{5,37},{6,230},{7,39},{8,232... | collective-permute-start | bytes 2359304 | tf_op jit(solution)/shard_map/ppermute | solution.py:47
  13.6 16.1 %collective-permute-start.2 = (f32[1,12,128,128]{3,2,1,0:T(8,128)S(1)}, f32[1,12,128,128]{3,2,1,0:T(8,128)S(1)}, u32[]{:S(2)}, u32[]{:S(2)}) collective-permute-start(f32[1,12,128,128]{3,2,1,0:T(8,128)S(1)} %collective-permute-done.refs_1_), channel_id=1, source_target_pairs={{0,2},{1,31},{2,4},{3,1},{4,6},{5,3},{6,8},{7,5},{8,10},{9,7},{10,... | collective-permute-start | bytes 2359304 | tf_op jit(solution)/shard_map/ppermute | solution.py:37
  18.6 17.5 %collective-permute-start.1 = (f32[1,12,128,128]{3,2,1,0:T(8,128)}, f32[1,12,128,128]{3,2,1,0:T(8,128)S(1)}, u32[]{:S(2)}, u32[]{:S(2)}) collective-permute-start(f32[1,12,128,128]{3,2,1,0:T(8,128)} %refs_0_.1), channel_id=1, source_target_pairs={{0,2},{1,31},{2,4},{3,1},{4,6},{5,3},{6,8},{7,5},{8,10},{9,7},{10,... | collective-permute-start | bytes 2359304 | tf_op jit(solution)/shard_map/ppermute | solution.py:37
  19.1 16.9 %collective-permute-start.5 = (f32[1,12,128,128]{3,2,1,0:T(8,128)S(1)}, f32[1,12,128,128]{3,2,1,0:T(8,128)S(1)}, u32[]{:S(2)}, u32[]{:S(2)}) collective-permute-start(f32[1,12,128,128]{3,2,1,0:T(8,128)S(1)} %collective-permute-done.4.refs_0_), channel_id=1, source_target_pairs={{0,32},{1,225},{2,34},{3,227},{4,36},{5,229},{6,38},{7,231},{8,40}... | collective-permute-start | bytes 2359304 | tf_op jit(solution)/shard_map/ppermute | solution.py:47
  29.7 14.7 %collective-permute-start.10 = (f32[1,12,128,128]{3,2,1,0:T(8,128)S(1)}, f32[1,12,128,128]{3,2,1,0:T(8,128)S(1)}, u32[]{:S(2)}, u32[]{:S(2)}) collective-permute-start(f32[1,12,128,128]{3,2,1,0:T(8,128)S(1)} %collective-permute-done.8.refs_1_), channel_id=1, source_target_pairs={{0,224},{1,33},{2,226},{3,35},{4,228},{5,37},{6,230},{7,39},{8,232... | collective-permute-start | bytes 2359304 | tf_op jit(solution)/shard_map/ppermute | solution.py:47
  36.1 8.6 %collective-permute-start.6 = (f32[1,12,128,128]{3,2,1,0:T(8,128)S(1)}, f32[1,12,128,128]{3,2,1,0:T(8,128)S(1)}, u32[]{:S(2)}, u32[]{:S(2)}) collective-permute-start(f32[1,12,128,128]{3,2,1,0:T(8,128)S(1)} %collective-permute-done.1.refs_2_), channel_id=1, source_target_pairs={{0,1},{1,0},{2,3},{3,2},{4,5},{5,4},{6,7},{7,6},{8,9},{9,8},{10,11... | collective-permute-start | bytes 2359304 | tf_op jit(solution)/shard_map/ppermute | solution.py:32
  37.7 6.9 %collective-permute-start.7 = (f32[1,12,128,128]{3,2,1,0:T(8,128)S(1)}, f32[1,12,128,128]{3,2,1,0:T(8,128)S(1)}, u32[]{:S(2)}, u32[]{:S(2)}) collective-permute-start(f32[1,12,128,128]{3,2,1,0:T(8,128)S(1)} %collective-permute-done.2.refs_3_), channel_id=1, source_target_pairs={{0,1},{1,0},{2,3},{3,2},{4,5},{5,4},{6,7},{7,6},{8,9},{9,8},{10,11... | collective-permute-start | bytes 2359304 | tf_op jit(solution)/shard_map/ppermute | solution.py:32
  37.7 12.9 %collective-permute-start.3 = (f32[1,12,128,128]{3,2,1,0:T(8,128)S(1)}, f32[1,12,128,128]{3,2,1,0:T(8,128)S(1)}, u32[]{:S(2)}, u32[]{:S(2)}) collective-permute-start(f32[1,12,128,128]{3,2,1,0:T(8,128)S(1)} %collective-permute-done.2.refs_3_), channel_id=1, source_target_pairs={{0,2},{1,31},{2,4},{3,1},{4,6},{5,3},{6,8},{7,5},{8,10},{9,7},{10,... | collective-permute-start | bytes 2359304 | tf_op jit(solution)/shard_map/ppermute | solution.py:37
  41.8 12.1 %collective-permute-start.9 = (f32[1,6,128,128]{3,2,1,0:T(8,128)S(1)}, f32[1,6,128,128]{3,2,1,0:T(8,128)S(1)}, u32[]{:S(2)}, u32[]{:S(2)}) collective-permute-start(f32[1,6,128,128]{3,2,1,0:T(8,128)S(1)} %get-tuple-element.48), channel_id=1, source_target_pairs={{0,32},{1,225},{2,34},{3,227},{4,36},{5,229},{6,38},{7,231},{8,40}... | collective-permute-start | bytes 1179656 | tf_op jit(solution)/shard_map/ppermute | solution.py:47
  44.5 12.0 %collective-permute-start.13 = (f32[1,6,128,128]{3,2,1,0:T(8,128)S(1)}, f32[1,6,128,128]{3,2,1,0:T(8,128)S(1)}, u32[]{:S(2)}, u32[]{:S(2)}) collective-permute-start(f32[1,6,128,128]{3,2,1,0:T(8,128)S(1)} %get-tuple-element.45), channel_id=1, source_target_pairs={{0,224},{1,33},{2,226},{3,35},{4,228},{5,37},{6,230},{7,39},{8,232... | collective-permute-start | bytes 1179656 | tf_op jit(solution)/shard_map/ppermute | solution.py:47
  44.6 17.6 %collective-permute-start.12 = (f32[1,6,128,128]{3,2,1,0:T(8,128)S(1)}, f32[1,6,128,128]{3,2,1,0:T(8,128)S(1)}, u32[]{:S(2)}, u32[]{:S(2)}) collective-permute-start(f32[1,6,128,128]{3,2,1,0:T(8,128)S(1)} %get-tuple-element.34), channel_id=1, source_target_pairs={{0,224},{1,33},{2,226},{3,35},{4,228},{5,37},{6,230},{7,39},{8,232... | collective-permute-start | bytes 1179656 | tf_op jit(solution)/shard_map/ppermute | solution.py:47
  44.7 17.5 %collective-permute-start.11 = (f32[1,6,128,128]{3,2,1,0:T(8,128)S(1)}, f32[1,6,128,128]{3,2,1,0:T(8,128)S(1)}, u32[]{:S(2)}, u32[]{:S(2)}) collective-permute-start(f32[1,6,128,128]{3,2,1,0:T(8,128)S(1)} %get-tuple-element.33), channel_id=1, source_target_pairs={{0,32},{1,225},{2,34},{3,227},{4,36},{5,229},{6,38},{7,231},{8,40}... | collective-permute-start | bytes 1179656 | tf_op jit(solution)/shard_map/ppermute | solution.py:47
  53.8 15.4 %collective-permute-start.14 = (f32[1,6,128,128]{3,2,1,0:T(8,128)S(1)}, f32[1,6,128,128]{3,2,1,0:T(8,128)S(1)}, u32[]{:S(2)}, u32[]{:S(2)}) collective-permute-start(f32[1,6,128,128]{3,2,1,0:T(8,128)S(1)} %collective-permute-done.9.refs_0_), channel_id=1, source_target_pairs={{0,32},{1,225},{2,34},{3,227},{4,36},{5,229},{6,38},{7,231},{8,40}... | collective-permute-start | bytes 1179656 | tf_op jit(solution)/shard_map/ppermute | solution.py:47
  56.5 12.8 %collective-permute-start.15 = (f32[1,6,128,128]{3,2,1,0:T(8,128)S(1)}, f32[1,6,128,128]{3,2,1,0:T(8,128)S(1)}, u32[]{:S(2)}, u32[]{:S(2)}) collective-permute-start(f32[1,6,128,128]{3,2,1,0:T(8,128)S(1)} %collective-permute-done.13.refs_3_), channel_id=1, source_target_pairs={{0,224},{1,33},{2,226},{3,35},{4,228},{5,37},{6,230},{7,39},{8,232... | collective-permute-start | bytes 1179656 | tf_op jit(solution)/shard_map/ppermute | solution.py:47

commit v6 on v5

--- a/solution.py
+++ b/solution.py
@@ -162,11 +162,14 @@
         def own(i, _):
             item = meta[TLIST + i]
             tile, at = item >> 8, (item & 255) - 1
-            for row, ref in enumerate(left):
-
-                @pl.when((at >= row * NNZ) & (at < (row + 1) * NNZ))
-                def _(row=row, ref=ref):
-                    base[tile] = 2.0 * ref[0, at - row * NNZ]
+
+            @pl.when(at >= 0)
+            def _():
+                for row, ref in enumerate(left):
+
+                    @pl.when((at >= row * NNZ) & (at < (row + 1) * NNZ))
+                    def _(row=row, ref=ref):
+                        base[tile] = 2.0 * ref[0, at - row * NNZ]
 
             return 0
 

time: 71.8 us -> 71.8 us (level)
  Pallas kernels: 12.2 us -> 11.1 us
  waiting for transfers between devices: 23.6 us -> 24.6 us
    pallas_call x1, Pallas kernels: 3.17 us -> 1.94 us  [run_prepare(): pl.pallas_call(functools.partial(prepare, len(left)), out_shape=[pltpu.VM...]
    ppermute x10, waiting for transfers between devices: 13.9 us -> 15 us  [ring(): return lax.ppermute(block, ('row', 'col'), route)]
  transfers between devices with their start and end apart: 16 -> 16, of which waited for: 5 -> 5; matrix products, arithmetic and copies ran while one was open for 8% -> 8% of each run, Pallas kernels for 14% -> 12%
where the time goes in v6:
time: 71.8 us; the launch traced here: 71.6 us
  starting transfers between devices  29 us (40%)
  waiting for transfers between devices  24.6 us (34%)
  Pallas kernels  11.1 us (15%)
  other arithmetic  4.19 us (6%)
  local copies, waits for them, and re-layouts  1.03 us (1%)
  between operations  1.03 us (1%)
    ppermute x10, waiting for transfers between devices, ring(): return lax.ppermute(block, ('row', 'col'), route)  15 us
    ppermute x10, starting transfers between devices, ring(): return lax.ppermute(block, ('row', 'col'), route)  14.6 us
    ppermute x3, waiting for transfers between devices, next_chip(): lax.ppermute(block, 'col', [(i, (i + (-2 if i % 2 else 2)) % n) for i in...  9.67 us
    ppermute x3, starting transfers between devices, next_chip(): lax.ppermute(block, 'col', [(i, (i + (-2 if i % 2 else 2)) % n) for i in...  9.53 us
    pallas_call x4, Pallas kernels, run_group(): pl.pallas_call(functools.partial(last_kernel if last else kernel, group,...  9.14 us
    ppermute x3, starting transfers between devices, swap_cores(): return lax.ppermute(block, 'col', [(i, i ^ 1) for i in range(n)])  4.89 us
    pallas_call x1, Pallas kernels, run_prepare(): pl.pallas_call(functools.partial(prepare, len(left)), out_shape=[pltpu.VM...  1.94 us
  transfers between devices with their start and end apart: 16, of which 5 were waited for; matrix products, arithmetic and copies ran while one was open for 8% of the time, Pallas kernels for 12%

profile of v6, /device:TPU:1, one launch (start us, length us, event | category | flops | bytes accessed | tf_op | source)
XLA Modules:
  0.0 71.6 jit_solution(7846833293550804787)
XLA Ops:
  0.0 3.2 %collective-permute-start = (f32[1,12,128,128]{3,2,1,0:T(8,128)}, f32[1,12,128,128]{3,2,1,0:T(8,128)S(1)}, u32[]{:S(2)}, u32[]{:S(2)}) collective-permute-start(f32[1,12,128,128]{3,2,1,0:T(8,128)} %refs_0_.1), channel_id=1, source_target_pairs={{0,1},{1,0},{2,3},{3,2},{4,5},{5,4},{6,7},{7,6},{8,9},{9,8},{10,11... | collective-permute-start | bytes 2359304 | tf_op jit(solution)/shard_map/ppermute | solution.py:32
  3.2 3.8 %collective-permute-start.4 = (f32[1,12,128,128]{3,2,1,0:T(8,128)}, f32[1,12,128,128]{3,2,1,0:T(8,128)S(1)}, u32[]{:S(2)}, u32[]{:S(2)}) collective-permute-start(f32[1,12,128,128]{3,2,1,0:T(8,128)} %refs_0_.1), channel_id=1, source_target_pairs={{0,32},{1,225},{2,34},{3,227},{4,36},{5,229},{6,38},{7,231},{8,40}... | collective-permute-start | bytes 2359304 | tf_op jit(solution)/shard_map/ppermute | solution.py:47
  7.1 0.7 fusion.21
  7.8 0.7 fusion.19
  8.4 0.1 pad_add_fusion
  8.5 0.2 fusion.1
  8.7 0.9 %select_reduce_fusion.1 = s32[15]{0:T(128)S(1)} fusion(s32[256]{0:T(256)} %param.12, s32[15]{0:T(128)S(1)} %pad_add_fusion), kind=kLoop, calls=%fused_computation.6 | loop fusion | flops 11505 | bytes 1144 | tf_op jit(solution)/shard_map/reduce_sum | solution.py:71
  9.6 0.1 slice.35
  9.6 0.8 %slice_bitcast_fusion.1 = (s32[24]{0:T(128)S(1)}, s32[24]{0:T(128)S(1)}) fusion(s32[24,2]{0,1:T(2,128)} %bitcast.10), kind=kLoop, calls=%fused_computation.70 | loop fusion | bytes 384 | tf_op jit(solution)/shard_map/eq | solution.py:74
  10.4 0.2 fusion.4
  10.6 0.2 fusion.6
  10.9 0.1 fusion.8
  11.0 0.7 %fusion.9 = (s32[24]{0:T(128)S(1)}, s32[24]{0:T(128)S(1)}) fusion(s32[8]{0:T(128)} %constant.100.clone, s32[24]{0:T(128)S(1)} %get-tuple-element.50, s32[8]{0:T(128)S(1)} %slice.35), kind=kLoop, calls=%fused_computation.30 | loop fusion | flops 912 | bytes 352 | tf_op jit(solution)/shard_map/reduce_sum | solution.py:83
  11.8 0.2 convert_reduce_fusion.1
  11.9 0.1 select_reduce_fusion.7
  12.1 0.0 copy-start.1
  12.1 0.1 select_reduce_fusion.6
  12.2 0.1 convert_reduce_fusion.3
  12.4 0.1 convert_reduce_fusion
  12.5 0.2 select_reduce_fusion
  12.7 0.1 select_reduce_fusion.2
  13.5 0.1 concatenate.7.meta
  13.5 0.0 collective-permute-start.8
  13.6 5.0 %collective-permute-start.2 = (f32[1,12,128,128]{3,2,1,0:T(8,128)S(1)}, f32[1,12,128,128]{3,2,1,0:T(8,128)S(1)}, u32[]{:S(2)}, u32[]{:S(2)}) collective-permute-start(f32[1,12,128,128]{3,2,1,0:T(8,128)S(1)} %collective-permute-done.refs_1_), channel_id=1, source_target_pairs={{0,2},{1,31},{2,4},{3,1},{4,6},{5,3},{6,8},{7,5},{8,10},{9,7},{10,... | collective-permute-start | bytes 2359304 | tf_op jit(solution)/shard_map/ppermute | solution.py:37
  18.6 0.5 collective-permute-start.1
  19.1 2.6 %collective-permute-start.5 = (f32[1,12,128,128]{3,2,1,0:T(8,128)S(1)}, f32[1,12,128,128]{3,2,1,0:T(8,128)S(1)}, u32[]{:S(2)}, u32[]{:S(2)}) collective-permute-start(f32[1,12,128,128]{3,2,1,0:T(8,128)S(1)} %collective-permute-done.4.refs_0_), channel_id=1, source_target_pairs={{0,32},{1,225},{2,34},{3,227},{4,36},{5,229},{6,38},{7,231},{8,40}... | collective-permute-start | bytes 2359304 | tf_op jit(solution)/shard_map/ppermute | solution.py:47
  21.7 8.0 %collective-permute-done.8.refs_1_ = f32[1,12,128,128]{3,2,1,0:T(8,128)S(1)} collective-permute-done((f32[1,12,128,128]{3,2,1,0:T(8,128)}, f32[1,12,128,128]{3,2,1,0:T(8,128)S(1)}, u32[]{:S(2)}, u32[]{:S(2)}) %collective-permute-start.8) | collective-permute-done | bytes 786464 | tf_op jit(solution)/shard_map/ppermute | solution.py:47
  29.7 6.4 %collective-permute-done.1.refs_2_ = f32[1,12,128,128]{3,2,1,0:T(8,128)S(1)} collective-permute-done((f32[1,12,128,128]{3,2,1,0:T(8,128)}, f32[1,12,128,128]{3,2,1,0:T(8,128)S(1)}, u32[]{:S(2)}, u32[]{:S(2)}) %collective-permute-start.1) | collective-permute-done | bytes 786464 | tf_op jit(solution)/shard_map/ppermute | solution.py:37
  36.1 1.6 %collective-permute-start.6 = (f32[1,12,128,128]{3,2,1,0:T(8,128)S(1)}, f32[1,12,128,128]{3,2,1,0:T(8,128)S(1)}, u32[]{:S(2)}, u32[]{:S(2)}) collective-permute-start(f32[1,12,128,128]{3,2,1,0:T(8,128)S(1)} %collective-permute-done.1.refs_2_), channel_id=1, source_target_pairs={{0,1},{1,0},{2,3},{3,2},{4,5},{5,4},{6,7},{7,6},{8,9},{9,8},{10,11... | collective-permute-start | bytes 2359304 | tf_op jit(solution)/shard_map/ppermute | solution.py:32
  37.7 0.0 collective-permute-start.7
  37.7 4.0 %collective-permute-start.3 = (f32[1,12,128,128]{3,2,1,0:T(8,128)S(1)}, f32[1,12,128,128]{3,2,1,0:T(8,128)S(1)}, u32[]{:S(2)}, u32[]{:S(2)}) collective-permute-start(f32[1,12,128,128]{3,2,1,0:T(8,128)S(1)} %collective-permute-done.2.refs_3_), channel_id=1, source_target_pairs={{0,2},{1,31},{2,4},{3,1},{4,6},{5,3},{6,8},{7,5},{8,10},{9,7},{10,... | collective-permute-start | bytes 2359304 | tf_op jit(solution)/shard_map/ppermute | solution.py:37
  41.7 0.1 fusion.25
  41.8 2.7 %collective-permute-start.9 = (f32[1,6,128,128]{3,2,1,0:T(8,128)S(1)}, f32[1,6,128,128]{3,2,1,0:T(8,128)S(1)}, u32[]{:S(2)}, u32[]{:S(2)}) collective-permute-start(f32[1,6,128,128]{3,2,1,0:T(8,128)S(1)} %get-tuple-element.48), channel_id=1, source_target_pairs={{0,32},{1,225},{2,34},{3,227},{4,36},{5,229},{6,38},{7,231},{8,40}... | collective-permute-start | bytes 1179656 | tf_op jit(solution)/shard_map/ppermute | solution.py:47
  44.4 0.1 fusion.24
  44.5 0.1 collective-permute-start.13
  44.6 0.1 collective-permute-start.12
  44.7 2.7 %collective-permute-start.11 = (f32[1,6,128,128]{3,2,1,0:T(8,128)S(1)}, f32[1,6,128,128]{3,2,1,0:T(8,128)S(1)}, u32[]{:S(2)}, u32[]{:S(2)}) collective-permute-start(f32[1,6,128,128]{3,2,1,0:T(8,128)S(1)} %get-tuple-element.33), channel_id=1, source_target_pairs={{0,32},{1,225},{2,34},{3,227},{4,36},{5,229},{6,38},{7,231},{8,40}... | collective-permute-start | bytes 1179656 | tf_op jit(solution)/shard_map/ppermute | solution.py:47
  47.3 3.3 %collective-permute-done.3.refs_4_ = f32[1,12,128,128]{3,2,1,0:T(8,128)S(1)} collective-permute-done((f32[1,12,128,128]{3,2,1,0:T(8,128)S(1)}, f32[1,12,128,128]{3,2,1,0:T(8,128)S(1)}, u32[]{:S(2)}, u32[]{:S(2)}) %collective-permute-start.3) | collective-permute-done | bytes 786464 | tf_op jit(solution)/shard_map/ppermute | solution.py:37
  50.6 1.9 %left_panel.1 = (bf16[84,128,256]{2,1,0:T(8,128)(2,1)S(1)}, f32[25,128,128]{2,1,0:T(8,128)S(1)}, f32[8,128]{1,0:T(8,128)S(1)}) custom-call(s32[384]{0:T(512)S(1)} %concatenate.7.meta, f32[1,12,128,128]{3,2,1,0:T(8,128)S(1)} %copy-done.1, f32[1,12,128,128]{3,2,1,0:T(8,128)S(1)} %collective-permute-done.refs_1_, ...), custom_call_target="tpu_custom_call" | custom-call | flops 5242880 | bytes 12582912 | tf_op jit(solution)/shard_map/left_panel/pallas_call | solution.py:310
  52.6 2.7 %collective-permute-start.14 = (f32[1,6,128,128]{3,2,1,0:T(8,128)S(1)}, f32[1,6,128,128]{3,2,1,0:T(8,128)S(1)}, u32[]{:S(2)}, u32[]{:S(2)}) collective-permute-start(f32[1,6,128,128]{3,2,1,0:T(8,128)S(1)} %collective-permute-done.9.refs_0_), channel_id=1, source_target_pairs={{0,32},{1,225},{2,34},{3,227},{4,36},{5,229},{6,38},{7,231},{8,40}... | collective-permute-start | bytes 1179656 | tf_op jit(solution)/shard_map/ppermute | solution.py:47
  55.3 0.0 collective-permute-start.15
  55.3 2.4 %pairs_0.1 = (f32[25,128,128]{2,1,0:T(8,128)S(1)}, f32[8,128]{1,0:T(8,128)S(1)}) custom-call(s32[384]{0:T(512)S(1)} %concatenate.7.meta, bf16[84,128,256]{2,1,0:T(8,128)(2,1)S(1)} %get-tuple-element.24.panel, f32[25,128,128]{2,1,0:T(8,128)S(1)} %get-tuple-element.25.base, ...), custom_call_target="tpu_custom_call", output_to_operand_aliasing={{0}: (2, {})} | custom-call | flops 1207959552 | bytes 4194304 | tf_op jit(solution)/shard_map/pairs_0/pallas_call | solution.py:335
  57.6 2.2 %pairs_1.1 = (f32[25,128,128]{2,1,0:T(8,128)S(1)}, f32[8,128]{1,0:T(8,128)S(1)}) custom-call(s32[384]{0:T(512)S(1)} %concatenate.7.meta, bf16[84,128,256]{2,1,0:T(8,128)(2,1)S(1)} %get-tuple-element.24.panel, f32[25,128,128]{2,1,0:T(8,128)S(1)} %get-tuple-element.29.base, ...), custom_call_target="tpu_custom_call", output_to_operand_aliasing={{0}: (2, {})} | custom-call | flops 805306368 | bytes 4194304 | tf_op jit(solution)/shard_map/pairs_1/pallas_call | solution.py:335
  59.8 1.8 %collective-permute-done.12.refs_2_ = f32[1,6,128,128]{3,2,1,0:T(8,128)S(1)} collective-permute-done((f32[1,6,128,128]{3,2,1,0:T(8,128)S(1)}, f32[1,6,128,128]{3,2,1,0:T(8,128)S(1)}, u32[]{:S(2)}, u32[]{:S(2)}) %collective-permute-start.12) | collective-permute-done | bytes 393248 | tf_op jit(solution)/shard_map/ppermute | solution.py:47
  61.7 2.4 %pairs_2.1 = (f32[25,128,128]{2,1,0:T(8,128)S(1)}, f32[8,128]{1,0:T(8,128)}, f32[24,128,128]{2,1,0:T(8,128)}) custom-call(s32[384]{0:T(512)S(1)} %concatenate.7.meta, bf16[84,128,256]{2,1,0:T(8,128)(2,1)S(1)} %get-tuple-element.24.panel, f32[25,128,128]{2,1,0:T(8,128)S(1)} %get-tuple-element.32.base, ...), custom_call_target="tpu_custom_call", output_to_operand_aliasing={{0}: (2, {})} | custom-call | flops 805306368 | bytes 4194304 | tf_op jit(solution)/shard_map/pairs_2/pallas_call | solution.py:335
  64.1 5.1 %collective-permute-done.14.refs_0_ = f32[1,6,128,128]{3,2,1,0:T(8,128)S(1)} collective-permute-done((f32[1,6,128,128]{3,2,1,0:T(8,128)S(1)}, f32[1,6,128,128]{3,2,1,0:T(8,128)S(1)}, u32[]{:S(2)}, u32[]{:S(2)}) %collective-permute-start.14) | collective-permute-done | bytes 393248 | tf_op jit(solution)/shard_map/ppermute | solution.py:47
  69.2 0.0 collective-permute-done.15.refs_1_
  69.2 2.2 %pairs_3.1 = f32[24,128,128]{2,1,0:T(8,128)} custom-call(s32[384]{0:T(512)S(1)} %concatenate.7.meta, bf16[84,128,256]{2,1,0:T(8,128)(2,1)S(1)} %get-tuple-element.24.panel, f32[25,128,128]{2,1,0:T(8,128)S(1)} %get-tuple-element.36.base, f32[1,6,128,128]{3,2,1,0:T(8,128)S(1)} %collective-permute-done.14.refs_0_, ...), custom_call_target="tpu_custom_call", output_to_operand_aliasing={{}: (5, {})} | custom-call | flops 402653184 | bytes 4194304 | tf_op jit(solution)/shard_map/pairs_3/pallas_call | solution.py:335
  (27 shorter events, 0.2 us)
Async XLA Ops:
  0.0 8.5 %copy-start = (s32[256,12]{0,1:T(8,128)S(1)}, s32[256,12]{0,1:T(8,128)}, u32[]{:S(2)}) copy-start(s32[256,12]{0,1:T(8,128)} %param.11) | copy-start | bytes 36868
  0.0 13.6 %collective-permute-start = (f32[1,12,128,128]{3,2,1,0:T(8,128)}, f32[1,12,128,128]{3,2,1,0:T(8,128)S(1)}, u32[]{:S(2)}, u32[]{:S(2)}) collective-permute-start(f32[1,12,128,128]{3,2,1,0:T(8,128)} %refs_0_.1), channel_id=1, source_target_pairs={{0,1},{1,0},{2,3},{3,2},{4,5},{5,4},{6,7},{7,6},{8,9},{9,8},{10,11... | collective-permute-start | bytes 2359304 | tf_op jit(solution)/shard_map/ppermute | solution.py:32
  3.2 15.9 %collective-permute-start.4 = (f32[1,12,128,128]{3,2,1,0:T(8,128)}, f32[1,12,128,128]{3,2,1,0:T(8,128)S(1)}, u32[]{:S(2)}, u32[]{:S(2)}) collective-permute-start(f32[1,12,128,128]{3,2,1,0:T(8,128)} %refs_0_.1), channel_id=1, source_target_pairs={{0,32},{1,225},{2,34},{3,227},{4,36},{5,229},{6,38},{7,231},{8,40}... | collective-permute-start | bytes 2359304 | tf_op jit(solution)/shard_map/ppermute | solution.py:47
  12.1 38.6 %copy-start.1 = (f32[1,12,128,128]{3,2,1,0:T(8,128)S(1)}, f32[1,12,128,128]{3,2,1,0:T(8,128)}, u32[]{:S(2)}) copy-start(f32[1,12,128,128]{3,2,1,0:T(8,128)} %refs_0_.1) | copy-start | bytes 2359300
  13.5 16.1 %collective-permute-start.8 = (f32[1,12,128,128]{3,2,1,0:T(8,128)}, f32[1,12,128,128]{3,2,1,0:T(8,128)S(1)}, u32[]{:S(2)}, u32[]{:S(2)}) collective-permute-start(f32[1,12,128,128]{3,2,1,0:T(8,128)} %refs_0_.1), channel_id=1, source_target_pairs={{0,224},{1,33},{2,226},{3,35},{4,228},{5,37},{6,230},{7,39},{8,232... | collective-permute-start | bytes 2359304 | tf_op jit(solution)/shard_map/ppermute | solution.py:47
  13.6 16.1 %collective-permute-start.2 = (f32[1,12,128,128]{3,2,1,0:T(8,128)S(1)}, f32[1,12,128,128]{3,2,1,0:T(8,128)S(1)}, u32[]{:S(2)}, u32[]{:S(2)}) collective-permute-start(f32[1,12,128,128]{3,2,1,0:T(8,128)S(1)} %collective-permute-done.refs_1_), channel_id=1, source_target_pairs={{0,2},{1,31},{2,4},{3,1},{4,6},{5,3},{6,8},{7,5},{8,10},{9,7},{10,... | collective-permute-start | bytes 2359304 | tf_op jit(solution)/shard_map/ppermute | solution.py:37
  18.6 17.5 %collective-permute-start.1 = (f32[1,12,128,128]{3,2,1,0:T(8,128)}, f32[1,12,128,128]{3,2,1,0:T(8,128)S(1)}, u32[]{:S(2)}, u32[]{:S(2)}) collective-permute-start(f32[1,12,128,128]{3,2,1,0:T(8,128)} %refs_0_.1), channel_id=1, source_target_pairs={{0,2},{1,31},{2,4},{3,1},{4,6},{5,3},{6,8},{7,5},{8,10},{9,7},{10,... | collective-permute-start | bytes 2359304 | tf_op jit(solution)/shard_map/ppermute | solution.py:37
  19.1 16.9 %collective-permute-start.5 = (f32[1,12,128,128]{3,2,1,0:T(8,128)S(1)}, f32[1,12,128,128]{3,2,1,0:T(8,128)S(1)}, u32[]{:S(2)}, u32[]{:S(2)}) collective-permute-start(f32[1,12,128,128]{3,2,1,0:T(8,128)S(1)} %collective-permute-done.4.refs_0_), channel_id=1, source_target_pairs={{0,32},{1,225},{2,34},{3,227},{4,36},{5,229},{6,38},{7,231},{8,40}... | collective-permute-start | bytes 2359304 | tf_op jit(solution)/shard_map/ppermute | solution.py:47
  29.7 14.7 %collective-permute-start.10 = (f32[1,12,128,128]{3,2,1,0:T(8,128)S(1)}, f32[1,12,128,128]{3,2,1,0:T(8,128)S(1)}, u32[]{:S(2)}, u32[]{:S(2)}) collective-permute-start(f32[1,12,128,128]{3,2,1,0:T(8,128)S(1)} %collective-permute-done.8.refs_1_), channel_id=1, source_target_pairs={{0,224},{1,33},{2,226},{3,35},{4,228},{5,37},{6,230},{7,39},{8,232... | collective-permute-start | bytes 2359304 | tf_op jit(solution)/shard_map/ppermute | solution.py:47
  36.1 8.6 %collective-permute-start.6 = (f32[1,12,128,128]{3,2,1,0:T(8,128)S(1)}, f32[1,12,128,128]{3,2,1,0:T(8,128)S(1)}, u32[]{:S(2)}, u32[]{:S(2)}) collective-permute-start(f32[1,12,128,128]{3,2,1,0:T(8,128)S(1)} %collective-permute-done.1.refs_2_), channel_id=1, source_target_pairs={{0,1},{1,0},{2,3},{3,2},{4,5},{5,4},{6,7},{7,6},{8,9},{9,8},{10,11... | collective-permute-start | bytes 2359304 | tf_op jit(solution)/shard_map/ppermute | solution.py:32
  37.7 6.9 %collective-permute-start.7 = (f32[1,12,128,128]{3,2,1,0:T(8,128)S(1)}, f32[1,12,128,128]{3,2,1,0:T(8,128)S(1)}, u32[]{:S(2)}, u32[]{:S(2)}) collective-permute-start(f32[1,12,128,128]{3,2,1,0:T(8,128)S(1)} %collective-permute-done.2.refs_3_), channel_id=1, source_target_pairs={{0,1},{1,0},{2,3},{3,2},{4,5},{5,4},{6,7},{7,6},{8,9},{9,8},{10,11... | collective-permute-start | bytes 2359304 | tf_op jit(solution)/shard_map/ppermute | solution.py:32
  37.7 12.9 %collective-permute-start.3 = (f32[1,12,128,128]{3,2,1,0:T(8,128)S(1)}, f32[1,12,128,128]{3,2,1,0:T(8,128)S(1)}, u32[]{:S(2)}, u32[]{:S(2)}) collective-permute-start(f32[1,12,128,128]{3,2,1,0:T(8,128)S(1)} %collective-permute-done.2.refs_3_), channel_id=1, source_target_pairs={{0,2},{1,31},{2,4},{3,1},{4,6},{5,3},{6,8},{7,5},{8,10},{9,7},{10,... | collective-permute-start | bytes 2359304 | tf_op jit(solution)/shard_map/ppermute | solution.py:37
  41.8 10.8 %collective-permute-start.9 = (f32[1,6,128,128]{3,2,1,0:T(8,128)S(1)}, f32[1,6,128,128]{3,2,1,0:T(8,128)S(1)}, u32[]{:S(2)}, u32[]{:S(2)}) collective-permute-start(f32[1,6,128,128]{3,2,1,0:T(8,128)S(1)} %get-tuple-element.48), channel_id=1, source_target_pairs={{0,32},{1,225},{2,34},{3,227},{4,36},{5,229},{6,38},{7,231},{8,40}... | collective-permute-start | bytes 1179656 | tf_op jit(solution)/shard_map/ppermute | solution.py:47
  44.5 10.8 %collective-permute-start.13 = (f32[1,6,128,128]{3,2,1,0:T(8,128)S(1)}, f32[1,6,128,128]{3,2,1,0:T(8,128)S(1)}, u32[]{:S(2)}, u32[]{:S(2)}) collective-permute-start(f32[1,6,128,128]{3,2,1,0:T(8,128)S(1)} %get-tuple-element.45), channel_id=1, source_target_pairs={{0,224},{1,33},{2,226},{3,35},{4,228},{5,37},{6,230},{7,39},{8,232... | collective-permute-start | bytes 1179656 | tf_op jit(solution)/shard_map/ppermute | solution.py:47
  44.6 17.1 %collective-permute-start.12 = (f32[1,6,128,128]{3,2,1,0:T(8,128)S(1)}, f32[1,6,128,128]{3,2,1,0:T(8,128)S(1)}, u32[]{:S(2)}, u32[]{:S(2)}) collective-permute-start(f32[1,6,128,128]{3,2,1,0:T(8,128)S(1)} %get-tuple-element.34), channel_id=1, source_target_pairs={{0,224},{1,33},{2,226},{3,35},{4,228},{5,37},{6,230},{7,39},{8,232... | collective-permute-start | bytes 1179656 | tf_op jit(solution)/shard_map/ppermute | solution.py:47
  44.7 17.0 %collective-permute-start.11 = (f32[1,6,128,128]{3,2,1,0:T(8,128)S(1)}, f32[1,6,128,128]{3,2,1,0:T(8,128)S(1)}, u32[]{:S(2)}, u32[]{:S(2)}) collective-permute-start(f32[1,6,128,128]{3,2,1,0:T(8,128)S(1)} %get-tuple-element.33), channel_id=1, source_target_pairs={{0,32},{1,225},{2,34},{3,227},{4,36},{5,229},{6,38},{7,231},{8,40}... | collective-permute-start | bytes 1179656 | tf_op jit(solution)/shard_map/ppermute | solution.py:47
  52.6 16.6 %collective-permute-start.14 = (f32[1,6,128,128]{3,2,1,0:T(8,128)S(1)}, f32[1,6,128,128]{3,2,1,0:T(8,128)S(1)}, u32[]{:S(2)}, u32[]{:S(2)}) collective-permute-start(f32[1,6,128,128]{3,2,1,0:T(8,128)S(1)} %collective-permute-done.9.refs_0_), channel_id=1, source_target_pairs={{0,32},{1,225},{2,34},{3,227},{4,36},{5,229},{6,38},{7,231},{8,40}... | collective-permute-start | bytes 1179656 | tf_op jit(solution)/shard_map/ppermute | solution.py:47
  55.3 14.0 %collective-permute-start.15 = (f32[1,6,128,128]{3,2,1,0:T(8,128)S(1)}, f32[1,6,128,128]{3,2,1,0:T(8,128)S(1)}, u32[]{:S(2)}, u32[]{:S(2)}) collective-permute-start(f32[1,6,128,128]{3,2,1,0:T(8,128)S(1)} %collective-permute-done.13.refs_3_), channel_id=1, source_target_pairs={{0,224},{1,33},{2,226},{3,35},{4,228},{5,37},{6,230},{7,39},{8,232... | collective-permute-start | bytes 1179656 | tf_op jit(solution)/shard_map/ppermute | solution.py:47
